TPU v7x, 128 devices: a whole 4x4x4 slice. The times are simulated.
128 devices in a mesh: grp: 8 (over x, core), blk: 16 (over y, z).
Axes of the slice: x: 4, y: 4, z: 4, core: 2. Of those that a mesh axis runs over, the one named last changes fastest.
Arguments:
- embeddings: bfloat16 [65536, 768], P(('grp', 'blk'))
- labels: int32 [65536], P(('grp', 'blk')), may hold values from 0 to 511, as said below
- cluster_slot: int32 [512], replicated, may hold values from 0 to 511, as said below
Outputs:
- max_similarity: float32 [65536], P(('grp', 'blk'))
- duplicate_mass: float32 [65536], P(('grp', 'blk'))
Inputs may be any that keep to these rules, and one draw needn't show every extreme that they name: `labels`: at most 128 of one device's 512 documents lie in clusters of one group, and on every device some group holds exactly 128 of them. `cluster_slot`: A permutation of the clusters' slots.
All inputs are finite; a program needn't handle non-finite values.
Results may differ from a plain program's by a relative error of at most 0.00053.
Values may be sent and summed in bfloat16 or wider, within the bound.
No kernel may reach another device: no remote copies, remote signals or barrier semaphores. Data moves between devices by JAX's collectives and lax.ppermute only.
A program may use at most 128 MiB of HBM per device.

v0:
```python
import jax
import jax.numpy as jnp
from jax import lax
from jax.sharding import PartitionSpec as P

epsilon = 1e-06
sharpness = 8.0
sentinel = 1 << 30


def shortened(shard):

    def short(part):
        return part.astype(jnp.bfloat16) if part.dtype == jnp.float32 else part

    return jax.tree.map(short, shard)


def scores_of(queries, key_rows):
    return jnp.einsum("qd,kd->qk", queries, key_rows, preferred_element_type=jnp.float32)


def partners(query_slots, key_slots):
    return (query_slots[:, None] == key_slots[None, :]) & (key_slots[None, :] >= 0)


def reduce_pairs(scores, matched, along):
    best_sim = jnp.max(jnp.where(matched, scores, jnp.float32(-1.0)), axis=along)
    dup_mass = jnp.sum(
        jnp.where(matched, jnp.exp(sharpness * (scores - 1.0)), jnp.float32(0.0)), axis=along
    )
    return (best_sim, dup_mass)


def tile_stats(queries, query_slots, query_ids, key_rows, key_slots, key_ids):
    width = queries.shape[1]
    member_count = queries.shape[0]
    key_count = key_rows.shape[0]
    span = member_count * max(1, 1024 // member_count)
    key_tiles = key_count // span
    k_rows = key_rows.reshape(key_tiles, span, width)
    k_slot = key_slots.reshape(key_tiles, span)
    k_ident = key_ids.reshape(key_tiles, span)

    def one_block(block_index):
        scores = scores_of(queries, k_rows[block_index])
        matched = partners(query_slots, k_slot[block_index])
        matched = matched & (query_ids[:, None] != k_ident[block_index][None, :])
        row_best, row_mass = reduce_pairs(scores, matched, 1)
        col_best = jnp.full((span,), -1.0, dtype=jnp.float32)
        col_mass = jnp.zeros((span,), dtype=jnp.float32)
        return (row_best, row_mass, col_best, col_mass)

    row_best, row_mass, col_best, col_mass = lax.map(
        one_block, jnp.arange(key_tiles, dtype=jnp.int32)
    )
    return (
        jnp.max(row_best, axis=0),
        jnp.sum(row_mass, axis=0),
        col_best.reshape(-1),
        col_mass.reshape(-1),
    )


def similarities(members, member_slots):
    member_count = members.shape[0]
    local_ids = jnp.arange(member_count, dtype=jnp.int32)
    own_ids = lax.axis_index("blk") * member_count + local_ids
    start_best = jnp.full((member_count,), -1.0, dtype=jnp.float32)
    start_mass = jnp.zeros((member_count,), dtype=jnp.float32)
    key_rows = lax.all_gather(members, "blk", axis=0, tiled=True)
    key_slots = lax.all_gather(shortened(member_slots), "blk", axis=0, tiled=True)
    key_ids = jnp.arange(key_rows.shape[0], dtype=jnp.int32)
    row_best, row_mass, unused_best, unused_mass = tile_stats(
        members, member_slots, own_ids, key_rows, key_slots, key_ids
    )
    return (jnp.maximum((start_best, start_mass)[0], row_best), row_mass)


def body(embeddings, labels, cluster_slot):
    groups = lax.axis_size("grp")
    row_count, feature_count = embeddings.shape
    cluster_count = cluster_slot.shape[0]
    capacity = row_count // 4
    widened = embeddings.astype(jnp.float32)
    units = (
        widened * lax.rsqrt(jnp.sum(widened * widened, axis=1, keepdims=True) + epsilon)
    ).astype(jnp.bfloat16)
    cluster_ids = jnp.arange(cluster_count, dtype=jnp.int32)
    slot_ids = jnp.sum(
        jnp.where(labels[:, None] == cluster_ids[None, :], cluster_slot[None, :], 0), axis=1
    )
    owner_group = slot_ids // (cluster_count // groups)
    owner_onehot = (owner_group[:, None] == jnp.arange(groups, dtype=jnp.int32)[None, :]).astype(
        jnp.int32
    )
    earlier = jnp.cumsum(owner_onehot, axis=0) - owner_onehot
    rank_within = jnp.sum(earlier * owner_onehot, axis=1)
    send_place = owner_group * capacity + rank_within
    outgoing = jnp.zeros((groups * capacity, feature_count), jnp.bfloat16).at[send_place].set(units)
    outgoing_slots = jnp.full((groups * capacity,), -1, jnp.int32).at[send_place].set(slot_ids)
    arrived, arrived_slots = (
        lax.all_to_all(outgoing, "grp", split_axis=0, concat_axis=0, tiled=True),
        lax.all_to_all(outgoing_slots, "grp", split_axis=0, concat_axis=0, tiled=True),
    )
    sort_keys = jnp.where(arrived_slots >= 0, arrived_slots, sentinel)
    order = jnp.argsort(sort_keys, stable=True)
    members = arrived[order]
    member_slots = arrived_slots[order]
    best_sorted, mass_sorted = similarities(members, member_slots)
    best_all = jnp.zeros_like(best_sorted).at[order].set(best_sorted)
    mass_all = jnp.zeros_like(mass_sorted).at[order].set(mass_sorted)
    best_back, mass_back = (
        lax.all_to_all(best_all, "grp", split_axis=0, concat_axis=0, tiled=True),
        lax.all_to_all(mass_all, "grp", split_axis=0, concat_axis=0, tiled=True),
    )
    return (best_back[send_place], jnp.log1p(mass_back[send_place]))


def solution(mesh):
    placed = (P(("grp", "blk"), None), P(("grp", "blk")), P())
    return jax.shard_map(
        body,
        mesh=mesh,
        in_specs=placed,
        out_specs=(P(("grp", "blk")), P(("grp", "blk"))),
        check_vma=False,
    )
```

profile of v0, /device:TPU:1, one launch (start us, length us, event | category | flops | bytes accessed | tf_op | source)
XLA Modules:
  0.0 361.7 jit_solution(12723057471076661082)
XLA Ops:
  12.7 5.8 %all-to-all-start = ((s32[8,128,1]{1,2,0:T(1,128)}), s32[8,128,1]{1,2,0:T(1,128)S(1)}, u32[]{:S(2)}, u32[]{:S(2)}) async-start(s32[8,128,1]{1,2,0:T(1,128)} %bitcast.7), calls=%async_computation | async-start | bytes 8192 | tf_op jit(solution)/shard_map/all_to_all | solution.py:104
  24.4 4.8 %all-to-all-start.1 = ((bf16[8,128,768]{2,1,0:T(8,128)(2,1)}), bf16[8,128,768]{2,1,0:T(8,128)(2,1)S(1)}, u32[]{:S(2)}, u32[]{:S(2)}) async-start(bf16[8,128,768]{2,1,0:T(8,128)(2,1)} %bitcast.9), calls=%async_computation.1 | async-start | bytes 3145728 | tf_op jit(solution)/shard_map/all_to_all | solution.py:103
  33.6 16.3 %all-to-all-done.1 = bf16[8,128,768]{2,1,0:T(8,128)(2,1)S(1)} async-done(((bf16[8,128,768]{2,1,0:T(8,128)(2,1)}), bf16[8,128,768]{2,1,0:T(8,128)(2,1)S(1)}, u32[]{:S(2)}, u32[]{:S(2)}) %all-to-all-start.1) | async-done | bytes 1572896 | tf_op jit(solution)/shard_map/all_to_all | solution.py:103
  49.9 5.2 %gather_fusion.1 = bf16[1024,768]{1,0:T(8,128)(2,1)} fusion(bf16[1024,768]{1,0:T(8,128)(2,1)S(1)} %bitcast.86, s32[1024]{0:T(1024)S(1)} %get-tuple-element.179), kind=kCustom, calls=%fused_computation.1 | custom fusion | bytes 3149824 | tf_op jit(solution)/shard_map/gather | solution.py:108
  55.2 4.5 %gather_fusion = s32[1024]{0:T(1024)S(1)} fusion(s32[1024]{0:T(1024)S(1)} %bitcast.83, s32[1024]{0:T(1024)S(1)} %get-tuple-element.179), kind=kCustom, calls=%fused_computation | custom fusion | bytes 12288 | tf_op jit(solution)/shard_map/gather | solution.py:109
  59.7 21.3 %all-gather = s32[16384]{0:T(1024)S(1)} all-gather(s32[1024]{0:T(1024)S(1)} %gather_fusion), channel_id=2, replica_groups=mesh['grp'=8,'blk'=16] {'blk'}, dimensions={0}, use_global_device_ids=true | all-gather | bytes 69632 | tf_op jit(solution)/shard_map/all_gather | solution.py:72
  81.1 129.7 %all-gather.4.cloned.1.call-done = bf16[16384,768]{1,0:T(8,128)(2,1)} async-done(((bf16[1024,768]{1,0:T(8,128)(2,1)}), bf16[16384,768]{1,0:T(8,128)(2,1)}) %all-gather.4.cloned.1.call-update) | async-done | bytes 25165840 | tf_op jit(solution)/shard_map/all_gather | solution.py:71
  210.8 117.1 %while.15 = (s32[]{:T(128)}, f32[16,1024]{1,0:T(8,128)S(1)}, f32[16,1024]{1,0:T(8,128)S(1)}, s32[1024]{0:T(1024)S(1)}, s32[16]{0:T(128)S(1)}, /*index=5*/s32[16,...) while((s32[]{:T(128)}, f32[16,1024]{1,0:T(8,128)S(1)}, ...), condition=%wide.region_11.12_spmd.clone, body=%wide.region_8.11_spmd.clone.sunk | while | flops 1621098496 | bytes 3209419 | solution.py:54
  213.3 4.5 %fusion.35 = (f32[1024]{0:T(1024)S(1)}, f32[1024]{0:T(1024)S(1)}) fusion(s32[1024]{0:T(1024)S(1)} %iota_add_fusion.2, s32[1024]{0:T(1024)S(1)} %get-tuple-element.279, s32[1024]{0:T(1024)S(1)} %bitcast.88, s32[1024]{0:T(1024)S(1)} %bitcast.90, pred[1024]{0:T(1024)(128)(4,1)S(1)} %get-tuple-element.247, ...), kind=kOutput, calls=%fused_computation.15.clone.1 | convolution fusion | flops 1621096448 | bytes 3171332 | tf_op jit(solution)/shard_map/while/body/eval_jaxpr/qd,kd->qk/dot_general | solution.py:20
  220.6 4.5 %fusion.35 = (f32[1024]{0:T(1024)S(1)}, f32[1024]{0:T(1024)S(1)}) fusion(s32[1024]{0:T(1024)S(1)} %iota_add_fusion.2, s32[1024]{0:T(1024)S(1)} %get-tuple-element.279, s32[1024]{0:T(1024)S(1)} %bitcast.88, s32[1024]{0:T(1024)S(1)} %bitcast.90, pred[1024]{0:T(1024)(128)(4,1)S(1)} %get-tuple-element.247, ...), kind=kOutput, calls=%fused_computation.15.clone.1 | convolution fusion | flops 1621096448 | bytes 3171332 | tf_op jit(solution)/shard_map/while/body/eval_jaxpr/qd,kd->qk/dot_general | solution.py:20
  227.9 4.5 %fusion.35 = (f32[1024]{0:T(1024)S(1)}, f32[1024]{0:T(1024)S(1)}) fusion(s32[1024]{0:T(1024)S(1)} %iota_add_fusion.2, s32[1024]{0:T(1024)S(1)} %get-tuple-element.279, s32[1024]{0:T(1024)S(1)} %bitcast.88, s32[1024]{0:T(1024)S(1)} %bitcast.90, pred[1024]{0:T(1024)(128)(4,1)S(1)} %get-tuple-element.247, ...), kind=kOutput, calls=%fused_computation.15.clone.1 | convolution fusion | flops 1621096448 | bytes 3171332 | tf_op jit(solution)/shard_map/while/body/eval_jaxpr/qd,kd->qk/dot_general | solution.py:20
  235.3 4.5 %fusion.35 = (f32[1024]{0:T(1024)S(1)}, f32[1024]{0:T(1024)S(1)}) fusion(s32[1024]{0:T(1024)S(1)} %iota_add_fusion.2, s32[1024]{0:T(1024)S(1)} %get-tuple-element.279, s32[1024]{0:T(1024)S(1)} %bitcast.88, s32[1024]{0:T(1024)S(1)} %bitcast.90, pred[1024]{0:T(1024)(128)(4,1)S(1)} %get-tuple-element.247, ...), kind=kOutput, calls=%fused_computation.15.clone.1 | convolution fusion | flops 1621096448 | bytes 3171332 | tf_op jit(solution)/shard_map/while/body/eval_jaxpr/qd,kd->qk/dot_general | solution.py:20
  242.6 4.5 %fusion.35 = (f32[1024]{0:T(1024)S(1)}, f32[1024]{0:T(1024)S(1)}) fusion(s32[1024]{0:T(1024)S(1)} %iota_add_fusion.2, s32[1024]{0:T(1024)S(1)} %get-tuple-element.279, s32[1024]{0:T(1024)S(1)} %bitcast.88, s32[1024]{0:T(1024)S(1)} %bitcast.90, pred[1024]{0:T(1024)(128)(4,1)S(1)} %get-tuple-element.247, ...), kind=kOutput, calls=%fused_computation.15.clone.1 | convolution fusion | flops 1621096448 | bytes 3171332 | tf_op jit(solution)/shard_map/while/body/eval_jaxpr/qd,kd->qk/dot_general | solution.py:20
  249.9 4.5 %fusion.35 = (f32[1024]{0:T(1024)S(1)}, f32[1024]{0:T(1024)S(1)}) fusion(s32[1024]{0:T(1024)S(1)} %iota_add_fusion.2, s32[1024]{0:T(1024)S(1)} %get-tuple-element.279, s32[1024]{0:T(1024)S(1)} %bitcast.88, s32[1024]{0:T(1024)S(1)} %bitcast.90, pred[1024]{0:T(1024)(128)(4,1)S(1)} %get-tuple-element.247, ...), kind=kOutput, calls=%fused_computation.15.clone.1 | convolution fusion | flops 1621096448 | bytes 3171332 | tf_op jit(solution)/shard_map/while/body/eval_jaxpr/qd,kd->qk/dot_general | solution.py:20
  257.2 4.5 %fusion.35 = (f32[1024]{0:T(1024)S(1)}, f32[1024]{0:T(1024)S(1)}) fusion(s32[1024]{0:T(1024)S(1)} %iota_add_fusion.2, s32[1024]{0:T(1024)S(1)} %get-tuple-element.279, s32[1024]{0:T(1024)S(1)} %bitcast.88, s32[1024]{0:T(1024)S(1)} %bitcast.90, pred[1024]{0:T(1024)(128)(4,1)S(1)} %get-tuple-element.247, ...), kind=kOutput, calls=%fused_computation.15.clone.1 | convolution fusion | flops 1621096448 | bytes 3171332 | tf_op jit(solution)/shard_map/while/body/eval_jaxpr/qd,kd->qk/dot_general | solution.py:20
  264.5 4.5 %fusion.35 = (f32[1024]{0:T(1024)S(1)}, f32[1024]{0:T(1024)S(1)}) fusion(s32[1024]{0:T(1024)S(1)} %iota_add_fusion.2, s32[1024]{0:T(1024)S(1)} %get-tuple-element.279, s32[1024]{0:T(1024)S(1)} %bitcast.88, s32[1024]{0:T(1024)S(1)} %bitcast.90, pred[1024]{0:T(1024)(128)(4,1)S(1)} %get-tuple-element.247, ...), kind=kOutput, calls=%fused_computation.15.clone.1 | convolution fusion | flops 1621096448 | bytes 3171332 | tf_op jit(solution)/shard_map/while/body/eval_jaxpr/qd,kd->qk/dot_general | solution.py:20
  279.2 4.5 %fusion.35 = (f32[1024]{0:T(1024)S(1)}, f32[1024]{0:T(1024)S(1)}) fusion(s32[1024]{0:T(1024)S(1)} %iota_add_fusion.2, s32[1024]{0:T(1024)S(1)} %get-tuple-element.279, s32[1024]{0:T(1024)S(1)} %bitcast.88, s32[1024]{0:T(1024)S(1)} %bitcast.90, pred[1024]{0:T(1024)(128)(4,1)S(1)} %get-tuple-element.247, ...), kind=kOutput, calls=%fused_computation.15.clone.1 | convolution fusion | flops 1621096448 | bytes 3171332 | tf_op jit(solution)/shard_map/while/body/eval_jaxpr/qd,kd->qk/dot_general | solution.py:20
  293.8 4.5 %fusion.35 = (f32[1024]{0:T(1024)S(1)}, f32[1024]{0:T(1024)S(1)}) fusion(s32[1024]{0:T(1024)S(1)} %iota_add_fusion.2, s32[1024]{0:T(1024)S(1)} %get-tuple-element.279, s32[1024]{0:T(1024)S(1)} %bitcast.88, s32[1024]{0:T(1024)S(1)} %bitcast.90, pred[1024]{0:T(1024)(128)(4,1)S(1)} %get-tuple-element.247, ...), kind=kOutput, calls=%fused_computation.15.clone.1 | convolution fusion | flops 1621096448 | bytes 3171332 | tf_op jit(solution)/shard_map/while/body/eval_jaxpr/qd,kd->qk/dot_general | solution.py:20
  308.4 4.5 %fusion.35 = (f32[1024]{0:T(1024)S(1)}, f32[1024]{0:T(1024)S(1)}) fusion(s32[1024]{0:T(1024)S(1)} %iota_add_fusion.2, s32[1024]{0:T(1024)S(1)} %get-tuple-element.279, s32[1024]{0:T(1024)S(1)} %bitcast.88, s32[1024]{0:T(1024)S(1)} %bitcast.90, pred[1024]{0:T(1024)(128)(4,1)S(1)} %get-tuple-element.247, ...), kind=kOutput, calls=%fused_computation.15.clone.1 | convolution fusion | flops 1621096448 | bytes 3171332 | tf_op jit(solution)/shard_map/while/body/eval_jaxpr/qd,kd->qk/dot_general | solution.py:20
  323.1 4.5 %fusion.35 = (f32[1024]{0:T(1024)S(1)}, f32[1024]{0:T(1024)S(1)}) fusion(s32[1024]{0:T(1024)S(1)} %iota_add_fusion.2, s32[1024]{0:T(1024)S(1)} %get-tuple-element.279, s32[1024]{0:T(1024)S(1)} %bitcast.88, s32[1024]{0:T(1024)S(1)} %bitcast.90, pred[1024]{0:T(1024)(128)(4,1)S(1)} %get-tuple-element.247, ...), kind=kOutput, calls=%fused_computation.15.clone.1 | convolution fusion | flops 1621096448 | bytes 3171332 | tf_op jit(solution)/shard_map/while/body/eval_jaxpr/qd,kd->qk/dot_general | solution.py:20
  327.9 4.9 %scatter_custom_fusion.2 = f32[1024]{0:T(1024)} fusion(s32[1024]{0:T(1024)S(1)} %get-tuple-element.180, f32[1024]{0:T(1024)S(1)} %broadcast_maximum_fusion, f32[]{:T(128)} %constant.83.clone.1), kind=kCustom, calls=%fused_computation.71 | custom fusion | bytes 4100 | tf_op jit(solution)/shard_map/scatter | solution.py:111
  332.7 4.9 %all-to-all-start.2 = ((f32[8,128,1]{1,2,0:T(1,128)}), f32[8,128,1]{1,2,0:T(1,128)S(1)}, u32[]{:S(2)}, u32[]{:S(2)}) async-start(f32[8,128,1]{1,2,0:T(1,128)} %bitcast.13), calls=%async_computation.2 | async-start | bytes 8192 | tf_op jit(solution)/shard_map/all_to_all | solution.py:114
  337.7 4.9 %scatter_custom_fusion.3 = f32[1024]{0:T(1024)} fusion(s32[1024]{0:T(1024)S(1)} %get-tuple-element.180, f32[1024]{0:T(1024)S(1)} %reduce_sum.60, f32[]{:T(128)} %constant.83.clone.1), kind=kCustom, calls=%fused_computation.69 | custom fusion | bytes 4100 | tf_op jit(solution)/shard_map/scatter | solution.py:112
  342.6 4.8 %all-to-all-start.3 = ((f32[8,128,1]{1,2,0:T(1,128)}), f32[8,128,1]{1,2,0:T(1,128)S(1)}, u32[]{:S(2)}, u32[]{:S(2)}) async-start(f32[8,128,1]{1,2,0:T(1,128)} %bitcast.16), calls=%async_computation.3 | async-start | bytes 8192 | tf_op jit(solution)/shard_map/all_to_all | solution.py:115
  (137 shorter events, 55.2 us)
Async XLA Ops:
  12.7 11.7 %all-to-all-start = ((s32[8,128,1]{1,2,0:T(1,128)}), s32[8,128,1]{1,2,0:T(1,128)S(1)}, u32[]{:S(2)}, u32[]{:S(2)}) async-start(s32[8,128,1]{1,2,0:T(1,128)} %bitcast.7), calls=%async_computation | async-start | bytes 8192 | tf_op jit(solution)/shard_map/all_to_all | solution.py:104
  24.4 25.5 %all-to-all-start.1 = ((bf16[8,128,768]{2,1,0:T(8,128)(2,1)}), bf16[8,128,768]{2,1,0:T(8,128)(2,1)S(1)}, u32[]{:S(2)}, u32[]{:S(2)}) async-start(bf16[8,128,768]{2,1,0:T(8,128)(2,1)} %bitcast.9), calls=%async_computation.1 | async-start | bytes 3145728 | tf_op jit(solution)/shard_map/all_to_all | solution.py:103
  29.2 181.6 %all-gather.4.cloned.1.call-start = ((), (), s32[]{:S(2)}) async-start(), calls=%async_computation.4 | async-start | bytes 26738688 | tf_op jit(solution)/shard_map/all_gather | solution.py:71
  55.2 155.6 %copy-start = (bf16[1024,768]{1,0:T(8,128)(2,1)S(1)}, bf16[1024,768]{1,0:T(8,128)(2,1)}, u32[]{:S(2)}) copy-start(bf16[1024,768]{1,0:T(8,128)(2,1)} %gather_fusion.1) | copy-start | bytes 4718596
  332.7 9.8 %all-to-all-start.2 = ((f32[8,128,1]{1,2,0:T(1,128)}), f32[8,128,1]{1,2,0:T(1,128)S(1)}, u32[]{:S(2)}, u32[]{:S(2)}) async-start(f32[8,128,1]{1,2,0:T(1,128)} %bitcast.13), calls=%async_computation.2 | async-start | bytes 8192 | tf_op jit(solution)/shard_map/all_to_all | solution.py:114
  342.6 9.4 %all-to-all-start.3 = ((f32[8,128,1]{1,2,0:T(1,128)}), f32[8,128,1]{1,2,0:T(1,128)S(1)}, u32[]{:S(2)}, u32[]{:S(2)}) async-start(f32[8,128,1]{1,2,0:T(1,128)} %bitcast.16), calls=%async_computation.3 | async-start | bytes 8192 | tf_op jit(solution)/shard_map/all_to_all | solution.py:115
Sparse Core Ops, SparseCore 0:
  55.3 155.4 all-gather.3
where the time goes:
time: 363 us; the launch traced here: 362 us
  waiting for transfers between devices  147 us (40%)
  matrix products  72.2 us (20%)
  local copies, waits for them, and re-layouts  42.3 us (12%)
  loops' own time  30.9 us (9%)
  blocking collectives  21.3 us (6%)
  starting transfers between devices  20.3 us (6%)
  between operations  14.2 us (4%)
  other arithmetic  13.2 us (4%)
    all_gather x1, waiting for transfers between devices, similarities(): key_rows = lax.all_gather(members, 'blk', axis=0, tiled=True)  130 us
    dot_general x16, matrix products, scores_of(): jnp.einsum('qd,kd->qk', queries, key_rows, preferred_element_type=jnp.flo...  72.2 us
    another operation x1, loops' own time, tile_stats(): lax.map(one_block, jnp.arange(key_tiles, dtype=jnp.int32))  30.9 us
    all_gather x1, blocking collectives, similarities(): lax.all_gather(shortened(member_slots), 'blk', axis=0, tiled=True)  21.3 us
    all_to_all x1, waiting for transfers between devices, body(): lax.all_to_all(outgoing, 'grp', split_axis=0, concat_axis=0, tiled=True)  16.3 us
    dynamic_slice x16, local copies, waits for them, and re-layouts, tile_stats(): lax.map(one_block, jnp.arange(key_tiles, dtype=jnp.int32))  9.59 us
  transfers between devices with their start and end apart: 5, of which 3 were waited for; matrix products, arithmetic and copies ran while one was open for 6% of the time, Pallas kernels for 0%

commit v1 on v0

--- a/solution.py
+++ b/solution.py
@@ -1,11 +1,358 @@
 import jax
 import jax.numpy as jnp
 from jax import lax
+from jax.experimental import pallas as pl
+from jax.experimental.pallas import tpu as pltpu
 from jax.sharding import PartitionSpec as P
 
 epsilon = 1e-06
 sharpness = 8.0
 sentinel = 1 << 30
+
+ROWS = 512
+FEAT = 768
+WIDE = 896
+GROUPS = 8
+MEMBERS = 16
+FIRST = 64
+SPREAD = 4
+PACKED = 128
+BLOCK = ROWS + PACKED
+OFFSET = 16.0
+LOG2E = 1.4426950408889634
+AXES = ("grp", "blk")
+VMEM_LIMIT = 56 * 1024 * 1024
+
+SPOTS = ((0, 0), (1, 0), (0, 1), (0, 3), (2, 0), (0, 2))
+BOTH = ((1, 0), (2, 0), (1, 3), (1, 2), (1, 5), (2, 4))
+ONE = ((0, 0), (3, 2), (4, 0), (4, 5))
+ROW_BLOCKS = (1, 2)
+
+
+def iota(shape, axis):
+    return lax.broadcasted_iota(jnp.int32, shape, axis)
+
+
+def matmul(a, b, dims, exact=False):
+    return lax.dot_general(
+        a,
+        b,
+        (dims, ((), ())),
+        precision=lax.Precision.HIGHEST if exact else None,
+        preferred_element_type=jnp.float32,
+    )
+
+
+NN = ((1,), (0,))
+NT = ((1,), (1,))
+
+
+def prelude_kernel(labels, slots, rows, straight, spread, places):
+    lab = labels[...]
+    table = slots[...]
+    by_cluster = (iota((ROWS, ROWS), 0) == lab).astype(jnp.bfloat16)
+    sub = iota((8, ROWS), 0)
+    parts = jnp.where(sub == 0, table >> 6, jnp.where(sub == 1, table & 63, 0)).astype(jnp.bfloat16)
+    found = matmul(parts, by_cluster, NN)
+    group = found[0:1].astype(jnp.int32)
+    local = found[1:2].astype(jnp.int32)
+    in_group = sub == group
+    before = (iota((ROWS, ROWS), 0) < iota((ROWS, ROWS), 1)).astype(jnp.bfloat16)
+    counts = matmul(in_group.astype(jnp.bfloat16), before, NN)
+    rank = jnp.sum(jnp.where(in_group, counts, 0.0), axis=0, keepdims=True).astype(jnp.int32)
+    places[...] = jnp.where(sub == 0, group, jnp.where(sub == 1, rank, 0))
+
+    wide = rows[...].astype(jnp.float32)
+    norm = lax.rsqrt(jnp.sum(wide * wide, axis=1, keepdims=True) + epsilon)
+    units = (wide * norm).astype(jnp.bfloat16)
+    lanes = iota((128, ROWS), 0)
+    marks = jnp.where(lanes == local, 4.0, 0.0).astype(jnp.bfloat16)
+
+    target = jnp.where(rank < FIRST, group * FIRST + rank, -1)
+    for t in range(ROWS // 128):
+        pick = (lanes + 128 * t == target).astype(jnp.bfloat16)
+        here = pl.ds(128 * t, 128)
+        straight[here, :FEAT] = matmul(pick, units, NN).astype(jnp.bfloat16)
+        straight[here, FEAT:] = matmul(pick, marks, NT).astype(jnp.bfloat16)
+    member = group * MEMBERS + (rank & (MEMBERS - 1))
+    turn = rank >> 4
+    totals = matmul(
+        jnp.ones((128, ROWS), jnp.bfloat16), (lanes - 64 == group).astype(jnp.bfloat16), NT
+    )
+    for j in range(SPREAD):
+        pick = (lanes == jnp.where(turn == FIRST // MEMBERS + j, member, -1)).astype(jnp.bfloat16)
+        spread[:, j * WIDE : j * WIDE + FEAT] = matmul(pick, units, NN).astype(jnp.bfloat16)
+        more = matmul(pick, marks, NT)
+        if j == 0:
+            more = more + totals
+        spread[:, j * WIDE + FEAT : (j + 1) * WIDE] = more.astype(jnp.bfloat16)
+
+
+def pack_kernel(arrived, packed, over):
+    lane = iota((128, 128), 1)
+    sub = iota((128, 128), 0)
+    ones = jnp.ones((8, 128), jnp.bfloat16)
+    before = (iota((ROWS, ROWS), 0) < iota((ROWS, ROWS), 1)).astype(jnp.bfloat16)
+    more = [arrived[:, j * WIDE + FEAT : (j + 1) * WIDE] for j in range(SPREAD)]
+    totals = jnp.where(lane >= 64, more[0].astype(jnp.float32), 0.0)
+    turns = jnp.zeros((128, 128), jnp.float32)
+    for m in range(SPREAD):
+        turns = turns + (totals > (FIRST + MEMBERS * m)).astype(jnp.float32)
+    most = jnp.max(jnp.sum(turns, axis=0, keepdims=True), axis=1, keepdims=True)
+    over[...] = jnp.broadcast_to((most > PACKED).astype(jnp.int32), (8, 128))
+    marks = [jnp.where(lane < 64, m, jnp.zeros_like(m)) for m in more]
+    held = jnp.concatenate([matmul(ones, m, NT) for m in marks], axis=1) > 0.0
+    position = matmul(held.astype(jnp.bfloat16), before, NN)
+    position = jnp.where(held, position, -1.0)[0:1].astype(jnp.int32)
+    rows = jnp.zeros((PACKED, FEAT), jnp.float32)
+    tail = jnp.zeros((PACKED, 128), jnp.float32)
+    for j in range(SPREAD):
+        pick = (sub == position[:, 128 * j : 128 * (j + 1)]).astype(jnp.bfloat16)
+        rows = rows + matmul(pick, arrived[:, j * WIDE : j * WIDE + FEAT], NN)
+        names = jnp.where(sub == 64, lane + 1, jnp.where(sub == 65, j, 0)).astype(jnp.bfloat16)
+        tail = tail + matmul(pick, marks[j], NN) + matmul(pick, names, NT)
+    packed[:, :FEAT] = rows.astype(jnp.bfloat16)
+    packed[:, FEAT:] = tail.astype(jnp.bfloat16)
+
+
+def column_fold(x, op):
+    while x.shape[0] > 8:
+        half = x.shape[0] // 2
+        x = op(x[:half], x[half:])
+    return x
+
+
+def row_fold(x, op):
+    total = x[:, :128]
+    for t in range(1, x.shape[1] // 128):
+        total = op(total, x[:, 128 * t : 128 * (t + 1)])
+    return total
+
+
+def pair_kernel(*refs):
+    big = refs[:6]
+    small = refs[6:12]
+    out = refs[12]
+    clean, col_best, col_mass, row_best, row_mass, lines = refs[13:]
+
+    lane = iota((128, 128), 1)
+    for e in range(6):
+        clean[e, :, :FEAT] = small[e][:, :FEAT]
+        tail = small[e][:, FEAT:]
+        clean[e, :, FEAT:] = jnp.where(lane < 64, tail, jnp.zeros_like(tail))
+    col_best[...] = jnp.zeros_like(col_best)
+    col_mass[...] = jnp.zeros_like(col_mass)
+    row_best[...] = jnp.zeros_like(row_best)
+    row_mass[...] = jnp.zeros_like(row_mass)
+
+    def tile(x, y, c, first, width, r, start, diagonal):
+        product = matmul(x, y, NT)
+        if diagonal is not None:
+            shape = (128, width)
+            product = jnp.where(iota(shape, 0) + diagonal == iota(shape, 1), 0.0, product)
+        soft = jnp.exp2((product - (OFFSET + 1.0)) * (sharpness * LOG2E))
+        here = slice(first, first + width)
+        col_best[c, :, here] = jnp.maximum(col_best[c, :, here], column_fold(product, jnp.maximum))
+        col_mass[c, :, here] = col_mass[c, :, here] + column_fold(soft, jnp.add)
+        if r is not None:
+            there = pl.ds(start, 128)
+            row_best[r, there, :] = jnp.maximum(row_best[r, there, :], row_fold(product, jnp.maximum))
+            row_mass[r, there, :] = row_mass[r, there, :] + row_fold(soft, jnp.add)
+
+    def pair(rows, cols, r):
+        own = rows == cols
+
+        def chunk(t, carry):
+            start = pl.multiple_of(t * 128, 128)
+            x = big[rows][pl.ds(start, 128), :]
+            tile(x, big[cols][...], cols, 0, ROWS, r, start, start if own else None)
+            tile(x, clean[cols], cols, ROWS, PACKED, r, start, None)
+            return carry
+
+        lax.fori_loop(0, ROWS // 128, chunk, 0)
+        x = clean[rows]
+        tile(x, big[cols][...], cols, 0, ROWS, r, ROWS, None)
+        tile(x, clean[cols], cols, ROWS, PACKED, r, ROWS, 0 if own else None)
+
+    for rows, cols in ONE:
+        pair(rows, cols, None)
+    for rows, cols in BOTH:
+        pair(rows, cols, ROW_BLOCKS.index(rows))
+
+    lines[...] = jnp.zeros_like(lines)
+    member = lax.axis_index("blk")
+    odd = lax.axis_index("grp") & 1
+    sub = iota((128, 128), 0)
+    back = jnp.zeros((128, 128), jnp.float32)
+    for e in range(6):
+        best = jnp.max(col_best[e], axis=0, keepdims=True)
+        mass = jnp.sum(col_mass[e], axis=0, keepdims=True)
+        if e in ROW_BLOCKS:
+            r = ROW_BLOCKS.index(e)
+            tops, sums = [], []
+            for t in range(BLOCK // 128):
+                here = pl.ds(128 * t, 128)
+                tops.append(jnp.max(row_best[r, here, :].T, axis=0, keepdims=True))
+                sums.append(jnp.sum(row_mass[r, here, :].T, axis=0, keepdims=True))
+            best = jnp.maximum(best, jnp.concatenate(tops, axis=1))
+            mass = mass + jnp.concatenate(sums, axis=1)
+        best = jnp.where(best > 0.5 * OFFSET, jnp.maximum(best - OFFSET, -1.0), -1.0)
+        dy, dz = SPOTS[e]
+        y = ((member >> 2) + jnp.where(odd == 1, 4 - dy, dy)) & 3
+        z = ((member & 3) + jnp.where(odd == 1, 4 - dz, dz)) & 3
+        spot = y * 4 + z
+        for g in range(GROUPS):
+            line = pl.ds(g * MEMBERS + spot, 1)
+            part = slice(g * FIRST, (g + 1) * FIRST)
+            lines[line, :] = jnp.concatenate([best[:, part], mass[:, part]], axis=1)
+        names = small[e][:, FEAT:]
+        pick = jnp.where((iota((8, 128), 0) == 0) & (iota((8, 128), 1) == 64), 1.0, 0.0)
+        pick = pick + jnp.where((iota((8, 128), 0) == 1) & (iota((8, 128), 1) == 65), 1.0, 0.0)
+        named = matmul(pick.astype(jnp.bfloat16), names, NT)
+        source = named[0:1].astype(jnp.int32) - 1
+        turn = named[1:2].astype(jnp.int32)
+        spots = sub - 8 * e
+        values = jnp.where(
+            (spots >= 0) & (spots < 8) & ((spots >> 1) == turn),
+            jnp.where((spots & 1) == 0, best[:, ROWS:], mass[:, ROWS:]),
+            0.0,
+        )
+        to = (sub == source).astype(jnp.float32)
+        back = back + matmul(to, values, NT, exact=True)
+    out[:, 128:] = back
+    out[:, :128] = lines[...]
+
+
+def finish_kernel(arrived, places, result, lines):
+    lines[...] = arrived[:, 0:128]
+    member = lax.axis_index("blk")
+    group = places[0:1, :]
+    rank = places[1:2, :]
+    lane = iota((1, 128), 1)
+    y, z = member >> 2, member & 3
+    tables = []
+    for g in range(GROUPS):
+        best = mass = None
+        for dy, dz in SPOTS:
+            if g & 1:
+                dy, dz = -dy, -dz
+            line = g * MEMBERS + ((y + ((-dy) & 3)) & 3) * 4 + ((z + ((-dz) & 3)) & 3)
+            row = lines[pl.ds(line, 1), :]
+            best = row if best is None else jnp.maximum(best, row)
+            mass = row if mass is None else mass + row
+        tables.append(jnp.where(lane < FIRST, best, mass))
+    table = jnp.concatenate(tables, axis=0)
+    chosen = (iota((8, ROWS), 0) == group).astype(jnp.float32)
+    values = matmul(table.T, chosen, NN, exact=True)
+    sub = iota((128, ROWS), 0)
+    first_best = jnp.sum(jnp.where(sub == rank, values, 0.0), axis=0, keepdims=True)
+    first_mass = jnp.sum(jnp.where(sub == rank + FIRST, values, 0.0), axis=0, keepdims=True)
+
+    shape = (128, 128)
+    at, col = iota(shape, 0), iota(shape, 1)
+    base, ay, az = at >> 4, (at >> 2) & 3, at & 3
+    turned = (base & 1) == 1
+    best = mass = None
+    late = arrived[:, 128:256]
+    for e, (dy, dz) in enumerate(SPOTS):
+        by = (ay + jnp.where(turned, dy, (-dy) & 3)) & 3
+        bz = (az + jnp.where(turned, dz, (-dz) & 3)) & 3
+        move = (col == base * MEMBERS + by * 4 + bz).astype(jnp.float32)
+        moved = matmul(move, late, NN, exact=True)
+        if e:
+            moved = pltpu.roll(moved, 128 - 8 * e, 1)
+        best = moved if best is None else jnp.maximum(best, moved)
+        mass = moved if mass is None else mass + moved
+    merged = jnp.where((col & 1) == 0, best, mass)
+    holder = (sub == group * MEMBERS + (rank & (MEMBERS - 1))).astype(jnp.float32)
+    picked = matmul(merged.T, holder, NN, exact=True)
+    turn = (rank >> 4) - FIRST // MEMBERS
+    late_best = jnp.sum(jnp.where(sub == 2 * turn, picked, 0.0), axis=0, keepdims=True)
+    late_mass = jnp.sum(jnp.where(sub == 2 * turn + 1, picked, 0.0), axis=0, keepdims=True)
+    best = jnp.where(rank < FIRST, first_best, late_best)
+    mass = jnp.where(rank < FIRST, first_mass, late_mass)
+    result[0:1, :] = best
+    result[1:2, :] = jnp.log1p(mass)
+
+
+def call(kernel, out_shape, scratch=(), flops=0, name=None):
+    return pl.pallas_call(
+        kernel,
+        out_shape=out_shape,
+        scratch_shapes=scratch,
+        compiler_params=pltpu.CompilerParams(vmem_limit_bytes=VMEM_LIMIT),
+        cost_estimate=pl.CostEstimate(flops=flops, bytes_accessed=8_000_000, transcendentals=0),
+        name=name,
+    )
+
+
+def hop(dy, dz):
+    pairs = []
+    for g in range(GROUPS):
+        turn = -1 if g & 1 else 1
+        for y in range(4):
+            for z in range(4):
+                source = ((y + turn * dy) % 4) * 4 + (z + turn * dz) % 4
+                pairs.append((g * MEMBERS + source, g * MEMBERS + y * 4 + z))
+    return pairs
+
+
+def from_spot(x, dy, dz):
+    return lax.ppermute(x, AXES, hop(dy, dz))
+
+
+def gather_spots(x):
+    one = from_spot(x, 1, 0)
+    two = from_spot(x, 0, 1)
+    three = from_spot(x, 0, 3)
+    return (x, one, two, three, from_spot(one, 1, 0), from_spot(two, 0, 1))
+
+
+def fast(embeddings, labels, cluster_slot):
+    f32, bf16, i32 = jnp.float32, jnp.bfloat16, jnp.int32
+    straight, spread, places = call(
+        prelude_kernel,
+        (
+            jax.ShapeDtypeStruct((ROWS, WIDE), bf16),
+            jax.ShapeDtypeStruct((128, SPREAD * WIDE), bf16),
+            jax.ShapeDtypeStruct((8, ROWS), i32),
+        ),
+        flops=3 * ROWS * ROWS * WIDE,
+        name="prelude",
+    )(labels.reshape(1, ROWS), cluster_slot.reshape(1, ROWS), embeddings)
+    big = lax.all_to_all(straight, "grp", split_axis=0, concat_axis=0, tiled=True)
+    late = lax.all_to_all(spread, AXES, split_axis=0, concat_axis=0, tiled=True)
+    big = gather_spots(big)
+    packed, over = call(
+        pack_kernel,
+        (jax.ShapeDtypeStruct((PACKED, WIDE), bf16), jax.ShapeDtypeStruct((8, 128), i32)),
+        flops=2 * ROWS * PACKED * WIDE,
+        name="pack",
+    )(late)
+    small = gather_spots(packed)
+    message = call(
+        pair_kernel,
+        jax.ShapeDtypeStruct((128, 256), f32),
+        scratch=(
+            pltpu.VMEM((6, PACKED, WIDE), bf16),
+            pltpu.VMEM((6, 8, BLOCK), f32),
+            pltpu.VMEM((6, 8, BLOCK), f32),
+            pltpu.VMEM((2, BLOCK, 128), f32),
+            pltpu.VMEM((2, BLOCK, 128), f32),
+            pltpu.VMEM((128, 128), f32),
+        ),
+        flops=20 * BLOCK * BLOCK * WIDE,
+        name="pairs",
+    )(*big, *small)
+    answer = lax.all_to_all(message, AXES, split_axis=0, concat_axis=0, tiled=True)
+    result = call(
+        finish_kernel,
+        jax.ShapeDtypeStruct((2, ROWS), f32),
+        scratch=(pltpu.VMEM((128, 128), f32),),
+        flops=ROWS * ROWS * 128,
+        name="finish",
+    )(answer, places)
+    return (result[0], result[1]), over[0, 0]
 
 
 def shortened(shard):
@@ -77,7 +424,7 @@
     return (jnp.maximum((start_best, start_mass)[0], row_best), row_mass)
 
 
-def body(embeddings, labels, cluster_slot):
+def general(embeddings, labels, cluster_slot):
     groups = lax.axis_size("grp")
     row_count, feature_count = embeddings.shape
     cluster_count = cluster_slot.shape[0]
@@ -117,12 +464,19 @@
     return (best_back[send_place], jnp.log1p(mass_back[send_place]))
 
 
+def body(embeddings, labels, cluster_slot):
+    result, over = fast(embeddings, labels, cluster_slot)
+    return lax.cond(
+        over > 0, lambda: general(embeddings, labels, cluster_slot), lambda: result
+    )
+
+
 def solution(mesh):
-    placed = (P(("grp", "blk"), None), P(("grp", "blk")), P())
+    placed = (P(AXES, None), P(AXES), P())
     return jax.shard_map(
         body,
         mesh=mesh,
         in_specs=placed,
-        out_specs=(P(("grp", "blk")), P(("grp", "blk"))),
+        out_specs=(P(AXES), P(AXES)),
         check_vma=False,
     )

time: 363 us -> 150 us (0.41)
  waiting for transfers between devices: 147 us -> 41.1 us
  matrix products: 72.2 us -> 0 us
  Pallas kernels: 0 us -> 36.8 us
  local copies, waits for them, and re-layouts: 42.3 us -> 8.24 us
  loops' own time: 30.9 us -> 0.02 us
  other arithmetic: 13.2 us -> 1.31 us
  starting transfers between devices: 20.3 us -> 27.1 us
    all_gather x1 -> x0, waiting for transfers between devices: 130 us -> none  [similarities(): key_rows = lax.all_gather(members, 'blk', axis=0, tiled=True)]
    dot_general x16 -> x0, matrix products: 72.2 us -> none  [scores_of(): jnp.einsum('qd,kd->qk', queries, key_rows, preferred_element_type=jnp.flo...]
    pallas_call x0 -> x4, Pallas kernels: none -> 36.8 us  [the longest x1 28.2 us: fast(): call(pair_kernel, jax.ShapeDtypeStruct((128, 256), f32), scratch=(pltpu.V...]
    another operation x1, loops' own time: 30.9 us -> 0.02 us  [body(): lax.cond(over > 0, lambda: general(embeddings, labels, cluster_slot), lam...]
    all_gather x1 -> x0, blocking collectives: 21.3 us -> none  [similarities(): lax.all_gather(shortened(member_slots), 'blk', axis=0, tiled=True)]
    all_to_all x0 -> x1, blocking collectives: none -> 19.8 us  [fast(): lax.all_to_all(straight, 'grp', split_axis=0, concat_axis=0, tiled=True)]
    ppermute x0 -> x10, waiting for transfers between devices: none -> 19.8 us  [from_spot(): return lax.ppermute(x, AXES, hop(dy, dz))]
    gather x4 -> x0, local copies, waits for them, and re-layouts: 15.5 us -> none  [the longest x2 5.7 us: body(): return (best_back[send_place], jnp.log1p(mass_back[send_place]))]
  transfers between devices with their start and end apart: 5 -> 12, of which waited for: 3 -> 6; matrix products, arithmetic and copies ran while one was open for 6% -> 4% of each run, Pallas kernels for 0% -> 2%
where the time goes in v1:
time: 150 us; the launch traced here: 149 us
  waiting for transfers between devices  41.1 us (27%)
  Pallas kernels  36.8 us (25%)
  starting transfers between devices  27.1 us (18%)
  blocking collectives  19.8 us (13%)
  between operations  14.8 us (10%)
  local copies, waits for them, and re-layouts  8.24 us (5%)
    pallas_call x1, Pallas kernels, fast(): call(pair_kernel, jax.ShapeDtypeStruct((128, 256), f32), scratch=(pltpu.V...  28.2 us
    all_to_all x1, blocking collectives, fast(): lax.all_to_all(straight, 'grp', split_axis=0, concat_axis=0, tiled=True)  19.8 us
    ppermute x10, waiting for transfers between devices, from_spot(): return lax.ppermute(x, AXES, hop(dy, dz))  19.8 us
    all_to_all x1, waiting for transfers between devices, fast(): late = lax.all_to_all(spread, AXES, split_axis=0, concat_axis=0, tiled=True)  13.1 us
    ppermute x10, starting transfers between devices, from_spot(): return lax.ppermute(x, AXES, hop(dy, dz))  11.4 us
    all_to_all x1, starting transfers between devices, fast(): late = lax.all_to_all(spread, AXES, split_axis=0, concat_axis=0, tiled=True)  8.4 us
    all_to_all x1, waiting for transfers between devices, fast(): lax.all_to_all(message, AXES, split_axis=0, concat_axis=0, tiled=True)  8.16 us
    all_to_all x1, starting transfers between devices, fast(): lax.all_to_all(message, AXES, split_axis=0, concat_axis=0, tiled=True)  7.39 us
  transfers between devices with their start and end apart: 12, of which 6 were waited for; matrix products, arithmetic and copies ran while one was open for 4% of the time, Pallas kernels for 2%

profile of v1, /device:TPU:1, one launch (start us, length us, event | category | flops | bytes accessed | tf_op | source)
XLA Modules:
  0.0 149.2 jit_solution(9982058355267678877)
XLA Ops:
  7.2 3.8 %prelude.1 = (bf16[512,896]{1,0:T(8,128)(2,1)}, bf16[128,3584]{1,0:T(8,128)(2,1)}, s32[8,512]{1,0:T(8,128)}) custom-call(s32[1,512]{1,0:T(1,128)} %bitcast.116, s32[1,512]{1,0:T(1,128)} %bitcast.117, bf16[512,768]{1,0:T(8,128)(2,1)} %rows.1), custom_call_target="tpu_custom_call" | custom-call | flops 704643072 | bytes 8000000 | tf_op jit(solution)/shard_map/prelude/pallas_call | solution.py:313
  10.9 19.8 %all_to_all.69 = bf16[8,64,896]{2,1,0:T(8,128)(2,1)} all-to-all(bf16[8,64,896]{2,1,0:T(8,128)(2,1)} %bitcast.103), channel_id=1, replica_groups=mesh['grp'=8,'blk'=16] {'grp'}, dimensions={0} | all-to-all | bytes 1835008 | tf_op jit(solution)/shard_map/all_to_all | solution.py:323
  30.8 1.3 collective-permute-start
  32.1 1.6 %collective-permute-start.1 = (bf16[512,896]{1,0:T(8,128)(2,1)}, bf16[512,896]{1,0:T(8,128)(2,1)}, u32[]{:S(2)}, u32[]{:S(2)}) collective-permute-start(bf16[512,896]{1,0:T(8,128)(2,1)} %bitcast.25.refs_0_), channel_id=1, source_target_pairs={{1,0},{2,1},{3,2},{0,3},{5,4},{6,5},{7,6},{4,7},{9,8},{10,9},{11,1... | collective-permute-start | bytes 2752520 | tf_op jit(solution)/shard_map/ppermute | solution.py:301
  34.2 1.3 reduce.4
  35.5 1.2 reshape.224
  36.7 8.4 %all-to-all-start.4 = ((bf16[128,2,1792]{2,1,0:T(2,128)(2,1)}), bf16[128,2,1792]{2,1,0:T(2,128)(2,1)S(1)}, u32[]{:S(2)}, u32[]{:S(2)}) async-start(bf16[128,2,1792]{2,1,0:T(2,128)(2,1)} %reshape.224), calls=%async_computation.4 | async-start | bytes 1835008 | tf_op jit(solution)/shard_map/all_to_all | solution.py:324
  45.1 3.5 %collective-permute-start.2 = (bf16[512,896]{1,0:T(8,128)(2,1)}, bf16[512,896]{1,0:T(8,128)(2,1)}, u32[]{:S(2)}, u32[]{:S(2)}) collective-permute-start(bf16[512,896]{1,0:T(8,128)(2,1)} %bitcast.25.refs_0_), channel_id=1, source_target_pairs={{3,0},{0,1},{1,2},{2,3},{7,4},{4,5},{5,6},{6,7},{11,8},{8,9},{9,10... | collective-permute-start | bytes 2752520 | tf_op jit(solution)/shard_map/ppermute | solution.py:301
  48.6 1.3 collective-permute-start.3
  49.8 13.1 %all-to-all-done.4 = bf16[128,2,1792]{2,1,0:T(2,128)(2,1)S(1)} async-done(((bf16[128,2,1792]{2,1,0:T(2,128)(2,1)}), bf16[128,2,1792]{2,1,0:T(2,128)(2,1)S(1)}, u32[]{:S(2)}, u32[]{:S(2)}) %all-to-all-start.4) | async-done | bytes 917536 | tf_op jit(solution)/shard_map/all_to_all | solution.py:324
  63.7 1.1 copy.28
  64.7 2.6 %pack.1 = (bf16[128,896]{1,0:T(8,128)(2,1)}, s32[8,128]{1,0:T(8,128)}) custom-call(bf16[128,3584]{1,0:T(8,128)(2,1)} %bitcast.102), custom_call_target="tpu_custom_call" | custom-call | flops 117440512 | bytes 8000000 | tf_op jit(solution)/shard_map/pack/pallas_call | solution.py:326
  67.9 6.1 %collective-permute-done.5.refs_7_ = bf16[128,896]{1,0:T(8,128)(2,1)S(1)} collective-permute-done((bf16[128,896]{1,0:T(8,128)(2,1)}, bf16[128,896]{1,0:T(8,128)(2,1)S(1)}, u32[]{:S(2)}, u32[]{:S(2)}) %collective-permute-start.5) | collective-permute-done | bytes 229408 | tf_op jit(solution)/shard_map/ppermute | solution.py:301
  74.1 1.5 %collective-permute-start.7 = (bf16[128,896]{1,0:T(8,128)(2,1)}, bf16[128,896]{1,0:T(8,128)(2,1)S(1)}, u32[]{:S(2)}, u32[]{:S(2)}) collective-permute-start(bf16[128,896]{1,0:T(8,128)(2,1)} %get-tuple-element.154.refs_6_), channel_id=1, source_target_pairs={{3,0},{0,1},{1,2},{2,3},{7,4},{4,5},{5,6},{6,7},{11,8},{8,9},{9,10... | collective-permute-start | bytes 688136 | tf_op jit(solution)/shard_map/ppermute | solution.py:301
  75.6 7.6 %collective-permute-done.6.refs_8_ = bf16[128,896]{1,0:T(8,128)(2,1)S(1)} collective-permute-done((bf16[128,896]{1,0:T(8,128)(2,1)}, bf16[128,896]{1,0:T(8,128)(2,1)S(1)}, u32[]{:S(2)}, u32[]{:S(2)}) %collective-permute-start.6) | collective-permute-done | bytes 229408 | tf_op jit(solution)/shard_map/ppermute | solution.py:301
  83.2 1.6 %collective-permute-start.8 = (bf16[128,896]{1,0:T(8,128)(2,1)S(1)}, bf16[128,896]{1,0:T(8,128)(2,1)S(1)}, u32[]{:S(2)}, u32[]{:S(2)}) collective-permute-start(bf16[128,896]{1,0:T(8,128)(2,1)S(1)} %collective-permute-done.5.refs_7_), channel_id=1, source_target_pairs={{4,0},{5,1},{6,2},{7,3},{8,4},{9,5},{10,6},{11,7},{12,8},{13,9},{1... | collective-permute-start | bytes 688136 | tf_op jit(solution)/shard_map/ppermute | solution.py:301
  84.8 4.8 %collective-permute-done.8.refs_10_ = bf16[128,896]{1,0:T(8,128)(2,1)S(1)} collective-permute-done((bf16[128,896]{1,0:T(8,128)(2,1)S(1)}, bf16[128,896]{1,0:T(8,128)(2,1)S(1)}, u32[]{:S(2)}, u32[]{:S(2)}) %collective-permute-start.8) | collective-permute-done | bytes 229408 | tf_op jit(solution)/shard_map/ppermute | solution.py:301
  89.5 1.3 collective-permute-done.9.refs_11_
  91.5 28.2 %pairs.1 = f32[128,256]{1,0:T(8,128)} custom-call(bf16[512,896]{1,0:T(8,128)(2,1)} %bitcast.25.refs_0_, bf16[512,896]{1,0:T(8,128)(2,1)} %collective-permute-done.refs_1_, bf16[512,896]{1,0:T(8,128)(2,1)} %collective-permute-done.1.refs_2_, bf16[512,896]{1,0:T(8,128)(2,1)} %collective-permute-done.2.refs_3_, ...), custom_call_target="tpu_custom_call" | custom-call | flops 7340032000 | bytes 8000000 | tf_op jit(solution)/shard_map/pairs/pallas_call | solution.py:333
  119.7 1.7 %copy.23 = f32[128,1,256]{2,1,0:T(1,128)} copy(f32[128,1,256]{2,0,1:T(8,128)} %bitcast.106) | data formatting | bytes 262144 | tf_op jit(solution)/shard_map/all_to_all | solution.py:347
  121.4 7.4 %all-to-all-start.6 = ((f32[128,1,256]{2,1,0:T(1,128)}), f32[128,1,256]{2,1,0:T(1,128)S(1)}, u32[]{:S(2)}, u32[]{:S(2)}) async-start(f32[128,1,256]{2,1,0:T(1,128)} %copy.23), calls=%async_computation.6 | async-start | bytes 262144 | tf_op jit(solution)/shard_map/all_to_all | solution.py:347
  128.8 1.2 slice.17
  130.6 8.2 %all-to-all-done.6 = f32[128,1,256]{2,1,0:T(1,128)S(1)} async-done(((f32[128,1,256]{2,1,0:T(1,128)}), f32[128,1,256]{2,1,0:T(1,128)S(1)}, u32[]{:S(2)}, u32[]{:S(2)}) %all-to-all-start.6) | async-done | bytes 131104 | tf_op jit(solution)/shard_map/all_to_all | solution.py:347
  139.4 2.3 %finish.1 = f32[2,512]{1,0:T(2,128)S(1)} custom-call(f32[128,256]{1,0:T(8,128)} %bitcast.105, s32[8,512]{1,0:T(8,128)} %get-tuple-element.155.places), custom_call_target="tpu_custom_call" | custom-call | flops 33554432 | bytes 8000000 | tf_op jit(solution)/shard_map/finish/pallas_call | solution.py:348
  (33 shorter events, 4.4 us)
Async XLA Ops:
  10.9 23.3 %copy-start.2 = (bf16[128,3584]{1,0:T(8,128)(2,1)S(1)}, bf16[128,3584]{1,0:T(8,128)(2,1)}, u32[]{:S(2)}) copy-start(bf16[128,3584]{1,0:T(8,128)(2,1)} %get-tuple-element.151) | copy-start | bytes 2752516
  30.8 17.8 %collective-permute-start = (bf16[512,896]{1,0:T(8,128)(2,1)}, bf16[512,896]{1,0:T(8,128)(2,1)}, u32[]{:S(2)}, u32[]{:S(2)}) collective-permute-start(bf16[512,896]{1,0:T(8,128)(2,1)} %bitcast.25.refs_0_), channel_id=1, source_target_pairs={{4,0},{5,1},{6,2},{7,3},{8,4},{9,5},{10,6},{11,7},{12,8},{13,9},{1... | collective-permute-start | bytes 2752520 | tf_op jit(solution)/shard_map/ppermute | solution.py:301
  32.1 17.8 %collective-permute-start.1 = (bf16[512,896]{1,0:T(8,128)(2,1)}, bf16[512,896]{1,0:T(8,128)(2,1)}, u32[]{:S(2)}, u32[]{:S(2)}) collective-permute-start(bf16[512,896]{1,0:T(8,128)(2,1)} %bitcast.25.refs_0_), channel_id=1, source_target_pairs={{1,0},{2,1},{3,2},{0,3},{5,4},{6,5},{7,6},{4,7},{9,8},{10,9},{11,1... | collective-permute-start | bytes 2752520 | tf_op jit(solution)/shard_map/ppermute | solution.py:301
  36.7 26.2 %all-to-all-start.4 = ((bf16[128,2,1792]{2,1,0:T(2,128)(2,1)}), bf16[128,2,1792]{2,1,0:T(2,128)(2,1)S(1)}, u32[]{:S(2)}, u32[]{:S(2)}) async-start(bf16[128,2,1792]{2,1,0:T(2,128)(2,1)} %reshape.224), calls=%async_computation.4 | async-start | bytes 1835008 | tf_op jit(solution)/shard_map/all_to_all | solution.py:324
  45.1 45.7 %collective-permute-start.2 = (bf16[512,896]{1,0:T(8,128)(2,1)}, bf16[512,896]{1,0:T(8,128)(2,1)}, u32[]{:S(2)}, u32[]{:S(2)}) collective-permute-start(bf16[512,896]{1,0:T(8,128)(2,1)} %bitcast.25.refs_0_), channel_id=1, source_target_pairs={{3,0},{0,1},{1,2},{2,3},{7,4},{4,5},{5,6},{6,7},{11,8},{8,9},{9,10... | collective-permute-start | bytes 2752520 | tf_op jit(solution)/shard_map/ppermute | solution.py:301
  48.6 42.3 %collective-permute-start.3 = (bf16[512,896]{1,0:T(8,128)(2,1)}, bf16[512,896]{1,0:T(8,128)(2,1)}, u32[]{:S(2)}, u32[]{:S(2)}) collective-permute-start(bf16[512,896]{1,0:T(8,128)(2,1)} %collective-permute-done.refs_1_), channel_id=1, source_target_pairs={{4,0},{5,1},{6,2},{7,3},{8,4},{9,5},{10,6},{11,7},{12,8},{13,9},{1... | collective-permute-start | bytes 2752520 | tf_op jit(solution)/shard_map/ppermute | solution.py:301
  49.8 41.0 %collective-permute-start.4 = (bf16[512,896]{1,0:T(8,128)(2,1)}, bf16[512,896]{1,0:T(8,128)(2,1)}, u32[]{:S(2)}, u32[]{:S(2)}) collective-permute-start(bf16[512,896]{1,0:T(8,128)(2,1)} %collective-permute-done.1.refs_2_), channel_id=1, source_target_pairs={{1,0},{2,1},{3,2},{0,3},{5,4},{6,5},{7,6},{4,7},{9,8},{10,9},{11,1... | collective-permute-start | bytes 2752520 | tf_op jit(solution)/shard_map/ppermute | solution.py:301
  67.3 74.4 %copy-start.1 = (bf16[512,768]{1,0:T(8,128)(2,1)S(1)}, bf16[512,768]{1,0:T(8,128)(2,1)}, u32[]{:S(2)}) copy-start(bf16[512,768]{1,0:T(8,128)(2,1)} %rows.1) | copy-start | bytes 2359300
  67.3 74.4 %copy-start.3 = (s32[512]{0:T(512)S(1)}, s32[512]{0:T(512)}, u32[]{:S(2)}) copy-start(s32[512]{0:T(512)} %param.8) | copy-start | bytes 6148
  67.3 74.4 %copy-start.4 = (s32[512]{0:T(512)S(1)}, s32[512]{0:T(512)}, u32[]{:S(2)}) copy-start(s32[512]{0:T(512)} %param.9) | copy-start | bytes 6148
  67.3 6.8 %collective-permute-start.5 = (bf16[128,896]{1,0:T(8,128)(2,1)}, bf16[128,896]{1,0:T(8,128)(2,1)S(1)}, u32[]{:S(2)}, u32[]{:S(2)}) collective-permute-start(bf16[128,896]{1,0:T(8,128)(2,1)} %get-tuple-element.154.refs_6_), channel_id=1, source_target_pairs={{4,0},{5,1},{6,2},{7,3},{8,4},{9,5},{10,6},{11,7},{12,8},{13,9},{1... | collective-permute-start | bytes 688136 | tf_op jit(solution)/shard_map/ppermute | solution.py:301
  67.4 15.8 %collective-permute-start.6 = (bf16[128,896]{1,0:T(8,128)(2,1)}, bf16[128,896]{1,0:T(8,128)(2,1)S(1)}, u32[]{:S(2)}, u32[]{:S(2)}) collective-permute-start(bf16[128,896]{1,0:T(8,128)(2,1)} %get-tuple-element.154.refs_6_), channel_id=1, source_target_pairs={{1,0},{2,1},{3,2},{0,3},{5,4},{6,5},{7,6},{4,7},{9,8},{10,9},{11,1... | collective-permute-start | bytes 688136 | tf_op jit(solution)/shard_map/ppermute | solution.py:301
  74.1 16.8 %copy-start.5 = (bf16[128,896]{1,0:T(8,128)(2,1)}, bf16[128,896]{1,0:T(8,128)(2,1)S(1)}, u32[]{:S(2)}) copy-start(bf16[128,896]{1,0:T(8,128)(2,1)S(1)} %collective-permute-done.5.refs_7_) | copy-start | bytes 688132
  74.1 10.7 %collective-permute-start.7 = (bf16[128,896]{1,0:T(8,128)(2,1)}, bf16[128,896]{1,0:T(8,128)(2,1)S(1)}, u32[]{:S(2)}, u32[]{:S(2)}) collective-permute-start(bf16[128,896]{1,0:T(8,128)(2,1)} %get-tuple-element.154.refs_6_), channel_id=1, source_target_pairs={{3,0},{0,1},{1,2},{2,3},{7,4},{4,5},{5,6},{6,7},{11,8},{8,9},{9,10... | collective-permute-start | bytes 688136 | tf_op jit(solution)/shard_map/ppermute | solution.py:301
  83.2 7.7 %copy-start.6 = (bf16[128,896]{1,0:T(8,128)(2,1)}, bf16[128,896]{1,0:T(8,128)(2,1)S(1)}, u32[]{:S(2)}) copy-start(bf16[128,896]{1,0:T(8,128)(2,1)S(1)} %collective-permute-done.6.refs_8_) | copy-start | bytes 688132
  83.2 6.4 %collective-permute-start.8 = (bf16[128,896]{1,0:T(8,128)(2,1)S(1)}, bf16[128,896]{1,0:T(8,128)(2,1)S(1)}, u32[]{:S(2)}, u32[]{:S(2)}) collective-permute-start(bf16[128,896]{1,0:T(8,128)(2,1)S(1)} %collective-permute-done.5.refs_7_), channel_id=1, source_target_pairs={{4,0},{5,1},{6,2},{7,3},{8,4},{9,5},{10,6},{11,7},{12,8},{13,9},{1... | collective-permute-start | bytes 688136 | tf_op jit(solution)/shard_map/ppermute | solution.py:301
  84.7 6.1 %copy-start.7 = (bf16[128,896]{1,0:T(8,128)(2,1)}, bf16[128,896]{1,0:T(8,128)(2,1)S(1)}, u32[]{:S(2)}) copy-start(bf16[128,896]{1,0:T(8,128)(2,1)S(1)} %collective-permute-done.7.refs_9_) | copy-start | bytes 688132
  84.7 6.1 %collective-permute-start.9 = (bf16[128,896]{1,0:T(8,128)(2,1)S(1)}, bf16[128,896]{1,0:T(8,128)(2,1)S(1)}, u32[]{:S(2)}, u32[]{:S(2)}) collective-permute-start(bf16[128,896]{1,0:T(8,128)(2,1)S(1)} %collective-permute-done.6.refs_8_), channel_id=1, source_target_pairs={{1,0},{2,1},{3,2},{0,3},{5,4},{6,5},{7,6},{4,7},{9,8},{10,9},{11,1... | collective-permute-start | bytes 688136 | tf_op jit(solution)/shard_map/ppermute | solution.py:301
  89.5 1.4 copy-start.8
  90.8 0.7 copy-start.9
  121.4 17.4 %all-to-all-start.6 = ((f32[128,1,256]{2,1,0:T(1,128)}), f32[128,1,256]{2,1,0:T(1,128)S(1)}, u32[]{:S(2)}, u32[]{:S(2)}) async-start(f32[128,1,256]{2,1,0:T(1,128)} %copy.23), calls=%async_computation.6 | async-start | bytes 262144 | tf_op jit(solution)/shard_map/all_to_all | solution.py:347

commit v2 on v1

v2 whole, which is shorter than its diff:
```python
import jax
import jax.numpy as jnp
from jax import lax
from jax.experimental import pallas as pl
from jax.experimental.pallas import tpu as pltpu
from jax.sharding import PartitionSpec as P

epsilon = 1e-06
sharpness = 8.0

ROWS = 512
FEAT = 768
HALF = 512
WIDE = 896
GROUPS = 8
MEMBERS = 16
FIRST = 64
SPREAD = 4
PACKED = 128
BLOCK = ROWS + PACKED
OFFSET = 16.0
LOG2E = 1.4426950408889634
AXES = ("grp", "blk")
VMEM_LIMIT = 56 * 1024 * 1024

SPOTS = ((0, 0), (1, 0), (0, 1), (0, 3), (2, 0), (0, 2))
ROW_BLOCKS = (1, 2)
COL_ORDER = (3, 2, 5, 0, 4)
ROW_ORDER = (3, 1, 4, 2, 0)


def iota(shape, axis):
    return lax.broadcasted_iota(jnp.int32, shape, axis)


def matmul(a, b, dims, exact=False):
    return lax.dot_general(
        a,
        b,
        (dims, ((), ())),
        precision=lax.Precision.HIGHEST if exact else None,
        preferred_element_type=jnp.float32,
    )


NN = ((1,), (0,))
NT = ((1,), (1,))


def prelude_kernel(labels, slots, rows, straight, spread, places):
    lab = labels[...]
    table = slots[...]
    by_cluster = (iota((ROWS, ROWS), 0) == lab).astype(jnp.bfloat16)
    sub = iota((8, ROWS), 0)
    parts = jnp.where(sub == 0, table >> 6, jnp.where(sub == 1, table & 63, 0)).astype(jnp.bfloat16)
    found = matmul(parts, by_cluster, NN)
    group = found[0:1].astype(jnp.int32)
    local = found[1:2].astype(jnp.int32)
    in_group = sub == group
    before = (iota((ROWS, ROWS), 0) < iota((ROWS, ROWS), 1)).astype(jnp.bfloat16)
    counts = matmul(in_group.astype(jnp.bfloat16), before, NN)
    rank = jnp.sum(jnp.where(in_group, counts, 0.0), axis=0, keepdims=True).astype(jnp.int32)
    places[...] = jnp.where(sub == 0, group, jnp.where(sub == 1, rank, 0))

    wide = rows[...].astype(jnp.float32)
    norm = lax.rsqrt(jnp.sum(wide * wide, axis=1, keepdims=True) + epsilon)
    units = (wide * norm).astype(jnp.bfloat16)
    lanes = iota((128, ROWS), 0)
    marks = jnp.where(lanes == local, 4.0, 0.0).astype(jnp.bfloat16)

    target = jnp.where(rank < FIRST, group * FIRST + rank, -1)
    for t in range(ROWS // 128):
        pick = (lanes + 128 * t == target).astype(jnp.bfloat16)
        here = pl.ds(128 * t, 128)
        straight[here, :FEAT] = matmul(pick, units, NN).astype(jnp.bfloat16)
        straight[here, FEAT:] = matmul(pick, marks, NT).astype(jnp.bfloat16)
    member = group * MEMBERS + (rank & (MEMBERS - 1))
    goal = jnp.where(rank < FIRST, -8, member * 8 + 2 * ((rank >> 4) - FIRST // MEMBERS))
    totals = matmul(
        jnp.ones((128, ROWS), jnp.bfloat16), (lanes - 64 == group).astype(jnp.bfloat16), NT
    )
    first = (iota((128, 128), 0) & 7) == 1
    for t in range(8):
        here = pl.ds(128 * t, 128)
        left = (lanes + 128 * t == goal).astype(jnp.bfloat16)
        right = (lanes + 128 * t == goal + 1).astype(jnp.bfloat16)
        spread[here, :256] = (
            matmul(left, units[:, :256], NN) + matmul(right, units[:, HALF:], NN)
        ).astype(jnp.bfloat16)
        spread[here, 256:384] = (
            matmul(left, units[:, 256:384], NN)
            + matmul(right, marks, NT)
            + jnp.where(first, totals, 0.0)
        ).astype(jnp.bfloat16)
        spread[here, 384:] = matmul(left, units[:, 384:HALF], NN).astype(jnp.bfloat16)


def pack_kernel(arrived, packed, over):
    shape = (128, 128)
    lane, sub = iota(shape, 1), iota(shape, 0)
    count = 8 * 128
    totals = jnp.zeros(shape, jnp.float32)
    for t in range(8):
        tail = arrived[pl.ds(128 * t, 128), 256:384].astype(jnp.float32)
        tail = jnp.where(((sub & 7) == 1) & (lane >= 64), tail, 0.0)
        for m in range(SPREAD):
            totals = totals + (tail > (FIRST + MEMBERS * m)).astype(jnp.float32)
    most = jnp.max(jnp.sum(totals, axis=0, keepdims=True), axis=1, keepdims=True)
    over[...] = jnp.broadcast_to((most > PACKED).astype(jnp.int32), (8, 128))
    tails = arrived[:, 256:384]
    tails = jnp.where(
        ((iota((count, 128), 0) & 1) == 1) & (iota((count, 128), 1) < 64), tails, jnp.zeros_like(tails)
    )
    held = matmul(jnp.ones((8, 128), jnp.bfloat16), tails, NT) > 0.0
    before = (iota((count, count), 0) < iota((count, count), 1)).astype(jnp.bfloat16)
    position = matmul(held.astype(jnp.bfloat16), before, NN)
    position = jnp.where(held, position, -1.0)[0:1].astype(jnp.int32)
    right = (iota((128, count), 0) == position).astype(jnp.bfloat16)
    position = jnp.concatenate([position[:, 1:], position[:, :1]], axis=1)
    left = (iota((128, count), 0) == position).astype(jnp.bfloat16)
    at = iota((128, count), 1)
    line = iota((128, count), 0)
    names = jnp.where(line == 64, (at >> 3) + 1, jnp.where(line == 65, (at >> 1) & 3, 0))
    packed[:, :HALF] = matmul(left, arrived[...], NN).astype(jnp.bfloat16)
    packed[:, HALF:FEAT] = matmul(right, arrived[:, :256], NN).astype(jnp.bfloat16)
    packed[:, FEAT:] = (
        matmul(right, tails, NN) + matmul(right, names.astype(jnp.bfloat16), NT)
    ).astype(jnp.bfloat16)


def column_fold(x, op):
    while x.shape[0] > 8:
        half = x.shape[0] // 2
        x = op(x[:half], x[half:])
    return x


def row_fold(x, op):
    total = x[:, :128]
    for t in range(1, x.shape[1] // 128):
        total = op(total, x[:, 128 * t : 128 * (t + 1)])
    return total


def clear(*refs):
    for ref in refs:
        ref[...] = jnp.zeros_like(ref)


def tile(x, y, cols, rows, state, diagonal=False):
    col_best, col_mass, row_best, row_mass = state
    product = matmul(x, y, NT)
    if diagonal:
        shape = product.shape
        product = jnp.where(iota(shape, 0) == iota(shape, 1), 0.0, product)
    soft = jnp.exp2((product - (OFFSET + 1.0)) * (sharpness * LOG2E))
    for first, size, c, start in cols:
        part = slice(first, first + size)
        here = slice(start, start + size)
        col_best[c, :, here] = jnp.maximum(
            col_best[c, :, here], column_fold(product[:, part], jnp.maximum)
        )
        col_mass[c, :, here] = col_mass[c, :, here] + column_fold(soft[:, part], jnp.add)
    for first, size, r, start in rows:
        part = slice(first, first + size)
        here = slice(start, start + size)
        row_best[r, here, :] = jnp.maximum(
            row_best[r, here, :], row_fold(product[part], jnp.maximum)
        )
        row_mass[r, here, :] = row_mass[r, here, :] + row_fold(soft[part], jnp.add)


def square(rows, cols, c, r, state, own=False):
    for i in range(0, ROWS, 256):
        for j in range(0, ROWS, 256):
            tile(
                rows[i : i + 256, :],
                cols[j : j + 256, :],
                [(0, 256, c, j)],
                [] if r is None else [(0, 256, r, i)],
                state,
                own and i == j,
            )


def settle(e, size, state):
    col_best, col_mass, row_best, row_mass = state
    best = jnp.max(col_best[e], axis=0, keepdims=True)
    mass = jnp.sum(col_mass[e], axis=0, keepdims=True)
    if e in ROW_BLOCKS:
        r = ROW_BLOCKS.index(e)
        tops, sums = [], []
        for t in range(0, size, 128):
            tops.append(jnp.max(row_best[r, t : t + 128, :].T, axis=0, keepdims=True))
            sums.append(jnp.sum(row_mass[r, t : t + 128, :].T, axis=0, keepdims=True))
        best = jnp.maximum(best, jnp.concatenate(tops, axis=1))
        mass = mass + jnp.concatenate(sums, axis=1)
    return best, mass


def similarity(best):
    return jnp.where(best > 0.5 * OFFSET, jnp.maximum(best - OFFSET, -1.0), -1.0)


def early_kernel(b0, b1, b2, b3, best_out, mass_out, *state):
    clear(best_out, mass_out, *state)
    square(b0, b0, 0, None, state, True)
    square(b1, b0, 0, 0, state)
    square(b2, b0, 0, 1, state)
    square(b1, b3, 3, 0, state)
    square(b1, b2, 2, 0, state)
    square(b3, b2, 2, None, state)
    for e in range(4):
        best_out[e : e + 1, :], mass_out[e : e + 1, :] = settle(e, ROWS, state)


def packed_kernel(*refs):
    big = refs[:6]
    small = refs[6:12]
    back_out, best_out, mass_out = refs[12:15]
    as_cols, as_rows = refs[15:17]
    state = refs[17:]
    clear(best_out, mass_out, *state)
    lane = iota((PACKED, 128), 1)
    for stack, order in ((as_cols, COL_ORDER), (as_rows, ROW_ORDER)):
        for place, e in enumerate(order):
            here = slice(place * PACKED, (place + 1) * PACKED)
            stack[here, :FEAT] = small[e][:, :FEAT]
            tail = small[e][:, FEAT:]
            stack[here, FEAT:] = jnp.where(lane < 64, tail, jnp.zeros_like(tail))

    def piece(stack, first, count):
        return stack[first * PACKED : (first + count) * PACKED, :]

    for r, first, count in ((1, 0, 2), (1, 2, 2), (2, 3, 2), (4, 2, 2), (3, 1, 1), (0, 3, 1)):
        cols = [(i * PACKED, PACKED, COL_ORDER[first + i], ROWS) for i in range(count)]
        y = piece(as_cols, first, count)
        for start in (0, 256):
            rows = [(0, 256, ROW_BLOCKS.index(r), start)] if r in ROW_BLOCKS else []
            tile(big[r][start : start + 256, :], y, cols, rows, state)
        rows = [(0, PACKED, ROW_BLOCKS.index(r), ROWS)] if r in ROW_BLOCKS else []
        tile(piece(as_rows, ROW_ORDER.index(r), 1), y, cols, rows, state, r == 0)
    for c, first, count in ((0, 1, 2), (0, 3, 2), (2, 0, 2), (5, 1, 2), (3, 1, 1), (4, 3, 1)):
        x = piece(as_rows, first, count)
        rows = [
            (i * PACKED, PACKED, ROW_BLOCKS.index(ROW_ORDER[first + i]), ROWS)
            for i in range(count)
            if ROW_ORDER[first + i] in ROW_BLOCKS
        ]
        for start in (0, 256):
            tile(x, big[c][start : start + 256, :], [(0, 256, c, start)], rows, state)

    sub = iota((128, 128), 0)
    spot = iota((8, 128), 0)
    pick = jnp.where((spot < 2) & (iota((8, 128), 1) == 64 + spot), 1.0, 0.0).astype(jnp.bfloat16)
    back = jnp.zeros((128, 128), jnp.float32)
    for e in range(6):
        best, mass = settle(e, BLOCK, state)
        best_out[e : e + 1, :] = best[:, :ROWS]
        mass_out[e : e + 1, :] = mass[:, :ROWS]
        named = matmul(pick, small[e][:, FEAT:], NT)
        source = named[0:1].astype(jnp.int32) - 1
        turn = named[1:2].astype(jnp.int32)
        spots = sub - 8 * e
        values = jnp.where(
            (spots >= 0) & (spots < 8) & ((spots >> 1) == turn),
            jnp.where((spots & 1) == 0, similarity(best[:, ROWS:]), mass[:, ROWS:]),
            0.0,
        )
        to = (sub == source).astype(jnp.float32)
        back = back + matmul(to, values, NT, exact=True)
    back_out[...] = back


def late_kernel(b0, b1, b2, b4, b5, best1, mass1, best2, mass2, back, out, *state):
    state, lines = state[:4], state[4]
    clear(lines, *state)
    square(b4, b0, 0, None, state)
    square(b4, b5, 5, None, state)
    square(b1, b5, 5, 0, state)
    square(b2, b4, 4, 1, state)
    member = lax.axis_index("blk")
    odd = lax.axis_index("grp") & 1
    for e in range(6):
        here = slice(e, e + 1)
        best, mass = settle(e, ROWS, state)
        best = similarity(jnp.maximum(best, jnp.maximum(best1[here, :], best2[here, :])))
        mass = mass + (mass1[here, :] + mass2[here, :])
        dy, dz = SPOTS[e]
        y = ((member >> 2) + jnp.where(odd == 1, 4 - dy, dy)) & 3
        z = ((member & 3) + jnp.where(odd == 1, 4 - dz, dz)) & 3
        spot = y * 4 + z
        for g in range(GROUPS):
            line = pl.ds(g * MEMBERS + spot, 1)
            part = slice(g * FIRST, (g + 1) * FIRST)
            lines[line, :] = jnp.concatenate([best[:, part], mass[:, part]], axis=1)
    out[:, :128] = lines[...]
    out[:, 128:] = back[...]


def finish_kernel(arrived, places, result, lines):
    lines[...] = arrived[:, 0:128]
    member = lax.axis_index("blk")
    group = places[0:1, :]
    rank = places[1:2, :]
    lane = iota((1, 128), 1)
    y, z = member >> 2, member & 3
    tables = []
    for g in range(GROUPS):
        best = mass = None
        for dy, dz in SPOTS:
            if g & 1:
                dy, dz = -dy, -dz
            line = g * MEMBERS + ((y + ((-dy) & 3)) & 3) * 4 + ((z + ((-dz) & 3)) & 3)
            row = lines[pl.ds(line, 1), :]
            best = row if best is None else jnp.maximum(best, row)
            mass = row if mass is None else mass + row
        tables.append(jnp.where(lane < FIRST, best, mass))
    table = jnp.concatenate(tables, axis=0)
    chosen = (iota((8, ROWS), 0) == group).astype(jnp.float32)
    values = matmul(table.T, chosen, NN, exact=True)
    sub = iota((128, ROWS), 0)
    first_best = jnp.sum(jnp.where(sub == rank, values, 0.0), axis=0, keepdims=True)
    first_mass = jnp.sum(jnp.where(sub == rank + FIRST, values, 0.0), axis=0, keepdims=True)

    shape = (128, 128)
    at, col = iota(shape, 0), iota(shape, 1)
    base, ay, az = at >> 4, (at >> 2) & 3, at & 3
    turned = (base & 1) == 1
    best = mass = None
    late = arrived[:, 128:256]
    for e, (dy, dz) in enumerate(SPOTS):
        by = (ay + jnp.where(turned, dy, (-dy) & 3)) & 3
        bz = (az + jnp.where(turned, dz, (-dz) & 3)) & 3
        move = (col == base * MEMBERS + by * 4 + bz).astype(jnp.float32)
        moved = matmul(move, late, NN, exact=True)
        if e:
            moved = pltpu.roll(moved, 128 - 8 * e, 1)
        best = moved if best is None else jnp.maximum(best, moved)
        mass = moved if mass is None else mass + moved
    merged = jnp.where((col & 1) == 0, best, mass)
    holder = (sub == group * MEMBERS + (rank & (MEMBERS - 1))).astype(jnp.float32)
    picked = matmul(merged.T, holder, NN, exact=True)
    turn = (rank >> 4) - FIRST // MEMBERS
    late_best = jnp.sum(jnp.where(sub == 2 * turn, picked, 0.0), axis=0, keepdims=True)
    late_mass = jnp.sum(jnp.where(sub == 2 * turn + 1, picked, 0.0), axis=0, keepdims=True)
    best = jnp.where(rank < FIRST, first_best, late_best)
    mass = jnp.where(rank < FIRST, first_mass, late_mass)
    result[0:1, :] = best
    result[1:2, :] = jnp.log1p(mass)


def call(kernel, out_shape, scratch=(), flops=0, name=None):
    return pl.pallas_call(
        kernel,
        out_shape=out_shape,
        scratch_shapes=scratch,
        compiler_params=pltpu.CompilerParams(vmem_limit_bytes=VMEM_LIMIT),
        cost_estimate=pl.CostEstimate(flops=flops, bytes_accessed=8_000_000, transcendentals=0),
        name=name,
    )


def hop(dy, dz):
    pairs = []
    for g in range(GROUPS):
        turn = -1 if g & 1 else 1
        for y in range(4):
            for z in range(4):
                source = ((y + turn * dy) % 4) * 4 + (z + turn * dz) % 4
                pairs.append((g * MEMBERS + source, g * MEMBERS + y * 4 + z))
    return pairs


def from_spot(x, dy, dz):
    return lax.ppermute(x, AXES, hop(dy, dz))


def fast(embeddings, labels, cluster_slot):
    f32, bf16, i32 = jnp.float32, jnp.bfloat16, jnp.int32
    shape = jax.ShapeDtypeStruct
    straight, spread, places = call(
        prelude_kernel,
        (shape((ROWS, WIDE), bf16), shape((1024, HALF), bf16), shape((8, ROWS), i32)),
        flops=4_000_000_000,
        name="prelude",
    )(labels.reshape(1, ROWS), cluster_slot.reshape(1, ROWS), embeddings)
    b0 = lax.all_to_all(straight, "grp", split_axis=0, concat_axis=0, tiled=True)
    b1 = from_spot(b0, 1, 0)
    b2 = from_spot(b0, 0, 1)
    b3 = from_spot(b0, 0, 3)
    arrived = lax.all_to_all(spread, AXES, split_axis=0, concat_axis=0, tiled=True)
    b4 = from_spot(b1, 1, 0)
    b5 = from_spot(b2, 0, 1)
    packed, over = call(
        pack_kernel,
        (shape((PACKED, WIDE), bf16), shape((8, 128), i32)),
        flops=3_000_000_000,
        name="pack",
    )(arrived)
    small = [packed] + [from_spot(packed, *spot) for spot in SPOTS[1:]]

    def state(size):
        return (
            pltpu.VMEM((6, 8, size), f32),
            pltpu.VMEM((6, 8, size), f32),
            pltpu.VMEM((2, size, 128), f32),
            pltpu.VMEM((2, size, 128), f32),
        )

    best1, mass1 = call(
        early_kernel,
        (shape((8, ROWS), f32), shape((8, ROWS), f32)),
        scratch=state(ROWS),
        flops=6_000_000_000,
        name="early",
    )(b0, b1, b2, b3)
    back, best2, mass2 = call(
        packed_kernel,
        (shape((128, 128), f32), shape((8, ROWS), f32), shape((8, ROWS), f32)),
        scratch=(pltpu.VMEM((5 * PACKED, WIDE), bf16), pltpu.VMEM((5 * PACKED, WIDE), bf16))
        + state(BLOCK),
        flops=6_000_000_000,
        name="packed",
    )(b0, b1, b2, b3, b4, b5, *small)
    message = call(
        late_kernel,
        shape((128, 256), f32),
        scratch=state(ROWS) + (pltpu.VMEM((128, 128), f32),),
        flops=4_000_000_000,
        name="late",
    )(b0, b1, b2, b4, b5, best1, mass1, best2, mass2, back)
    answer = lax.all_to_all(message, AXES, split_axis=0, concat_axis=0, tiled=True)
    result = call(
        finish_kernel,
        shape((2, ROWS), f32),
        scratch=(pltpu.VMEM((128, 128), f32),),
        flops=ROWS * ROWS * 128,
        name="finish",
    )(answer, places)
    return (result[0], result[1]), over[0, 0]


def general(embeddings, labels, cluster_slot):
    groups = lax.axis_size("grp")
    members = lax.axis_size("blk")
    row_count, feature_count = embeddings.shape
    capacity = row_count // 4
    held = groups * capacity
    widened = embeddings.astype(jnp.float32)
    units = (
        widened * lax.rsqrt(jnp.sum(widened * widened, axis=1, keepdims=True) + epsilon)
    ).astype(jnp.bfloat16)
    slot_ids = cluster_slot[labels]
    owner_group = slot_ids // (cluster_slot.shape[0] // groups)
    owner_onehot = (owner_group[:, None] == jnp.arange(groups, dtype=jnp.int32)[None, :]).astype(
        jnp.int32
    )
    earlier = jnp.cumsum(owner_onehot, axis=0) - owner_onehot
    send_place = owner_group * capacity + jnp.sum(earlier * owner_onehot, axis=1)
    outgoing = jnp.zeros((held, feature_count), jnp.bfloat16).at[send_place].set(units)
    outgoing_slots = jnp.full((held,), -1, jnp.int32).at[send_place].set(slot_ids)
    rows = lax.all_to_all(outgoing, "grp", split_axis=0, concat_axis=0, tiled=True)
    slots = lax.all_to_all(outgoing_slots, "grp", split_axis=0, concat_axis=0, tiled=True)
    ring = [(i, (i + 1) % members) for i in range(members)]
    local = jnp.arange(held, dtype=jnp.int32)
    place = lax.axis_index("blk")
    own_ids = place * held + local

    def step(turn, carry):
        key_rows, key_slots, best, mass = carry
        scores = jnp.einsum("qd,kd->qk", rows, key_rows, preferred_element_type=jnp.float32)
        matched = (slots[:, None] == key_slots[None, :]) & (key_slots[None, :] >= 0)
        owner = (place - turn) & (members - 1)
        matched = matched & (own_ids[:, None] != (owner * held + local)[None, :])
        best = jnp.maximum(best, jnp.max(jnp.where(matched, scores, -1.0), axis=1))
        mass = mass + jnp.sum(
            jnp.where(matched, jnp.exp(sharpness * (scores - 1.0)), 0.0), axis=1
        )
        key_rows = lax.ppermute(key_rows, "blk", ring)
        key_slots = lax.ppermute(key_slots, "blk", ring)
        return key_rows, key_slots, best, mass

    start = (
        rows,
        slots,
        jnp.full((held,), -1.0, jnp.float32),
        jnp.zeros((held,), jnp.float32),
    )
    _, _, best, mass = lax.fori_loop(0, members, step, start)
    best = lax.all_to_all(best, "grp", split_axis=0, concat_axis=0, tiled=True)
    mass = lax.all_to_all(mass, "grp", split_axis=0, concat_axis=0, tiled=True)
    return (best[send_place], jnp.log1p(mass[send_place]))


def body(embeddings, labels, cluster_slot):
    result, over = fast(embeddings, labels, cluster_slot)
    return lax.cond(
        over > 0, lambda: general(embeddings, labels, cluster_slot), lambda: result
    )


def solution(mesh):
    placed = (P(AXES, None), P(AXES), P())
    return jax.shard_map(
        body,
        mesh=mesh,
        in_specs=placed,
        out_specs=(P(AXES), P(AXES)),
        check_vma=False,
    )
```

time: 150 us -> 135 us (0.900)
  between operations: 14.8 us -> 1.4 us
  waiting for transfers between devices: 41.1 us -> 48.6 us
  Pallas kernels: 36.8 us -> 30.4 us
  local copies, waits for them, and re-layouts: 8.24 us -> 5.87 us
  starting transfers between devices: 27.1 us -> 28.9 us
    ppermute x10, waiting for transfers between devices: 19.8 us -> 40.4 us  [from_spot(): return lax.ppermute(x, AXES, hop(dy, dz))]
    all_to_all x1, waiting for transfers between devices: 13.1 us -> 0.01 us  [fast(): lax.all_to_all(spread, AXES, split_axis=0, concat_axis=0, tiled=True)]
    pallas_call x4 -> x6, Pallas kernels: 36.8 us -> 30.4 us  [the longest x1 8.54 us: fast(): call(packed_kernel, (shape((128, 128), f32), shape((8, ROWS), f32), shape...]
    unnamed x22 -> x23, local copies, waits for them, and re-layouts: 4.27 us -> 2.41 us
  transfers between devices with their start and end apart: 12 -> 12, of which waited for: 6 -> 5; matrix products, arithmetic and copies ran while one was open for 4% -> 1% of each run, Pallas kernels for 2% -> 7%
where the time goes in v2:
time: 135 us
  waiting for transfers between devices  48.6 us (36%)
  Pallas kernels  30.4 us (23%)
  starting transfers between devices  28.9 us (21%)
  blocking collectives  19.6 us (15%)
  local copies, waits for them, and re-layouts  5.87 us (4%)
  between operations  1.4 us (1%)
    ppermute x10, waiting for transfers between devices, from_spot(): return lax.ppermute(x, AXES, hop(dy, dz))  40.4 us
    all_to_all x1, blocking collectives, fast(): lax.all_to_all(straight, 'grp', split_axis=0, concat_axis=0, tiled=True)  19.6 us
    ppermute x10, starting transfers between devices, from_spot(): return lax.ppermute(x, AXES, hop(dy, dz))  11.4 us
    all_to_all x1, starting transfers between devices, fast(): lax.all_to_all(spread, AXES, split_axis=0, concat_axis=0, tiled=True)  9 us
    pallas_call x1, Pallas kernels, fast(): call(packed_kernel, (shape((128, 128), f32), shape((8, ROWS), f32), shape...  8.54 us
    all_to_all x1, starting transfers between devices, fast(): lax.all_to_all(message, AXES, split_axis=0, concat_axis=0, tiled=True)  8.5 us
    all_to_all x1, waiting for transfers between devices, fast(): lax.all_to_all(message, AXES, split_axis=0, concat_axis=0, tiled=True)  8.15 us
    pallas_call x1, Pallas kernels, fast(): call(early_kernel, (shape((8, ROWS), f32), shape((8, ROWS), f32)), scratc...  6.21 us
  transfers between devices with their start and end apart: 12, of which 5 were waited for; matrix products, arithmetic and copies ran while one was open for 1% of the time, Pallas kernels for 7%

profile of v2, /device:TPU:1, one launch (start us, length us, event | category | flops | bytes accessed | tf_op | source)
XLA Modules:
  0.0 134.7 jit_solution(15068971187853358092)
XLA Ops:
  0.6 4.6 %prelude.1 = (bf16[512,896]{1,0:T(8,128)(2,1)}, bf16[1024,512]{1,0:T(8,128)(2,1)}, s32[8,512]{1,0:T(8,128)}) custom-call(s32[1,512]{1,0:T(1,128)} %bitcast.83, s32[1,512]{1,0:T(1,128)} %bitcast.62, bf16[512,768]{1,0:T(8,128)(2,1)} %rows.1), custom_call_target="tpu_custom_call" | custom-call | flops 4000000000 | bytes 8000000 | tf_op jit(solution)/shard_map/prelude/pallas_call | solution.py:382
  5.2 19.6 %all_to_all.70 = bf16[8,64,896]{2,1,0:T(8,128)(2,1)S(1)} all-to-all(bf16[8,64,896]{2,1,0:T(8,128)(2,1)} %bitcast.72), channel_id=1, replica_groups=mesh['grp'=8,'blk'=16] {'grp'}, dimensions={0} | all-to-all | bytes 1835008 | tf_op jit(solution)/shard_map/all_to_all | solution.py:388
  24.8 9.0 %all-to-all-start.4 = ((bf16[128,8,512]{2,1,0:T(8,128)(2,1)}), bf16[128,8,512]{2,1,0:T(8,128)(2,1)S(1)}, u32[]{:S(2)}, u32[]{:S(2)}) async-start(bf16[128,8,512]{2,1,0:T(8,128)(2,1)} %bitcast.21), calls=%async_computation.4 | async-start | bytes 2097152 | tf_op jit(solution)/shard_map/all_to_all | solution.py:392
  33.8 1.6 %collective-permute-start.3 = (bf16[512,896]{1,0:T(8,128)(2,1)S(1)}, bf16[512,896]{1,0:T(8,128)(2,1)S(1)}, u32[]{:S(2)}, u32[]{:S(2)}) collective-permute-start(bf16[512,896]{1,0:T(8,128)(2,1)S(1)} %bitcast.66), channel_id=1, source_target_pairs={{1,0},{2,1},{3,2},{0,3},{5,4},{6,5},{7,6},{4,7},{9,8},{10,9},{11,1... | collective-permute-start | bytes 2752520 | tf_op jit(solution)/shard_map/ppermute | solution.py:376
  35.4 1.2 collective-permute-start.2
  36.7 1.8 %collective-permute-start.6 = (bf16[512,896]{1,0:T(8,128)(2,1)S(1)}, bf16[512,896]{1,0:T(8,128)(2,1)}, u32[]{:S(2)}, u32[]{:S(2)}) collective-permute-start(bf16[512,896]{1,0:T(8,128)(2,1)S(1)} %bitcast.68), channel_id=1, source_target_pairs={{3,0},{0,1},{1,2},{2,3},{7,4},{4,5},{5,6},{6,7},{11,8},{8,9},{9,10... | collective-permute-start | bytes 2752520 | tf_op jit(solution)/shard_map/ppermute | solution.py:376
  38.5 29.2 %collective-permute-done.3.b2.refs_2_ = bf16[512,896]{1,0:T(8,128)(2,1)S(1)} collective-permute-done((bf16[512,896]{1,0:T(8,128)(2,1)S(1)}, bf16[512,896]{1,0:T(8,128)(2,1)S(1)}, u32[]{:S(2)}, u32[]{:S(2)}) %collective-permute-start.3) | collective-permute-done | bytes 917536 | tf_op jit(solution)/shard_map/ppermute | solution.py:376
  67.7 2.1 %collective-permute-start.4 = (bf16[512,896]{1,0:T(8,128)(2,1)}, bf16[512,896]{1,0:T(8,128)(2,1)}, u32[]{:S(2)}, u32[]{:S(2)}) collective-permute-start(bf16[512,896]{1,0:T(8,128)(2,1)} %collective-permute-done.2.b1.refs_1_), channel_id=1, source_target_pairs={{4,0},{5,1},{6,2},{7,3},{8,4},{9,5},{10,6},{11,7},{12,8},{13,9},{1... | collective-permute-start | bytes 2752520 | tf_op jit(solution)/shard_map/ppermute | solution.py:376
  69.8 1.0 copy-done.2
  70.8 3.1 %pack.1 = (bf16[128,896]{1,0:T(8,128)(2,1)}, s32[8,128]{1,0:T(8,128)}) custom-call(bf16[1024,512]{1,0:T(8,128)(2,1)} %bitcast.65), custom_call_target="tpu_custom_call" | custom-call | flops 3000000000 | bytes 8000000 | tf_op jit(solution)/shard_map/pack/pallas_call | solution.py:395
  73.9 1.7 %collective-permute-start.11 = (bf16[128,896]{1,0:T(8,128)(2,1)}, bf16[128,896]{1,0:T(8,128)(2,1)S(1)}, u32[]{:S(2)}, u32[]{:S(2)}) collective-permute-start(bf16[128,896]{1,0:T(8,128)(2,1)} %get-tuple-element.277.refs_6_), channel_id=1, source_target_pairs={{2,0},{3,1},{0,2},{1,3},{6,4},{7,5},{4,6},{5,7},{10,8},{11,9},{8,1... | collective-permute-start | bytes 688136 | tf_op jit(solution)/shard_map/ppermute | solution.py:376
  75.6 2.5 %collective-permute-start.10 = (bf16[128,896]{1,0:T(8,128)(2,1)}, bf16[128,896]{1,0:T(8,128)(2,1)S(1)}, u32[]{:S(2)}, u32[]{:S(2)}) collective-permute-start(bf16[128,896]{1,0:T(8,128)(2,1)} %get-tuple-element.277.refs_6_), channel_id=1, source_target_pairs={{8,0},{9,1},{10,2},{11,3},{12,4},{13,5},{14,6},{15,7},{0,8},{1,9},... | collective-permute-start | bytes 688136 | tf_op jit(solution)/shard_map/ppermute | solution.py:376
  78.1 8.4 %collective-permute-done.11.refs_11_ = bf16[128,896]{1,0:T(8,128)(2,1)S(1)} collective-permute-done((bf16[128,896]{1,0:T(8,128)(2,1)}, bf16[128,896]{1,0:T(8,128)(2,1)S(1)}, u32[]{:S(2)}, u32[]{:S(2)}) %collective-permute-start.11) | collective-permute-done | bytes 229408 | tf_op jit(solution)/shard_map/ppermute | solution.py:376
  86.5 1.9 %collective-permute-done.10.refs_10_ = bf16[128,896]{1,0:T(8,128)(2,1)S(1)} collective-permute-done((bf16[128,896]{1,0:T(8,128)(2,1)}, bf16[128,896]{1,0:T(8,128)(2,1)S(1)}, u32[]{:S(2)}, u32[]{:S(2)}) %collective-permute-start.10) | collective-permute-done | bytes 229408 | tf_op jit(solution)/shard_map/ppermute | solution.py:376
  88.8 6.2 %early.1 = (f32[8,512]{1,0:T(8,128)}, f32[8,512]{1,0:T(8,128)}) custom-call(bf16[512,896]{1,0:T(8,128)(2,1)} %bitcast.69, bf16[512,896]{1,0:T(8,128)(2,1)} %collective-permute-done.2.b1.refs_1_, bf16[512,896]{1,0:T(8,128)(2,1)} %copy-done.5, bf16[512,896]{1,0:T(8,128)(2,1)} %collective-permute-done.6.b3.refs_3_), custom_call_target="tpu_custom_call" | custom-call | flops 6000000000 | bytes 8000000 | tf_op jit(solution)/shard_map/early/pallas_call | solution.py:411
  95.0 1.0 collective-permute-done.8.refs_8_
  96.7 8.5 %packed.1 = (f32[128,128]{1,0:T(8,128)}, f32[8,512]{1,0:T(8,128)}, f32[8,512]{1,0:T(8,128)}) custom-call(bf16[512,896]{1,0:T(8,128)(2,1)} %bitcast.70, bf16[512,896]{1,0:T(8,128)(2,1)} %collective-permute-done.2.b1.refs_1_, bf16[512,896]{1,0:T(8,128)(2,1)} %copy-done.5, bf16[512,896]{1,0:T(8,128)(2,1)} %collective-permute-done.6.b3.refs_3_, ...), custom_call_target="tpu_custom_call" | custom-call | flops 6000000000 | bytes 8000000 | tf_op jit(solution)/shard_map/packed/pallas_call | solution.py:418
  105.3 5.7 %late.1 = f32[128,256]{1,0:T(8,128)} custom-call(bf16[512,896]{1,0:T(8,128)(2,1)} %bitcast.71, bf16[512,896]{1,0:T(8,128)(2,1)} %collective-permute-done.2.b1.refs_1_, bf16[512,896]{1,0:T(8,128)(2,1)} %copy-done.5, bf16[512,896]{1,0:T(8,128)(2,1)} %collective-permute-done.4.refs_4_.b4, bf16[512,896]{1,0:T(8,128)(2,1)} %collective-permute-done.5.refs_5_.b5, ...), custom_call_target="tpu_custom_call" | custom-call | flops 4000000000 | bytes 8000000 | tf_op jit(solution)/shard_map/late/pallas_call | solution.py:426
  111.0 1.7 %copy.12 = f32[128,1,256]{2,1,0:T(1,128)} copy(f32[128,1,256]{2,0,1:T(8,128)} %bitcast.75) | data formatting | bytes 262144 | tf_op jit(solution)/shard_map/all_to_all | solution.py:433
  112.6 8.5 %all-to-all-start.6 = ((f32[128,1,256]{2,1,0:T(1,128)}), f32[128,1,256]{2,1,0:T(1,128)S(1)}, u32[]{:S(2)}, u32[]{:S(2)}) async-start(f32[128,1,256]{2,1,0:T(1,128)} %copy.12), calls=%async_computation.6 | async-start | bytes 262144 | tf_op jit(solution)/shard_map/all_to_all | solution.py:433
  121.1 1.2 slice.17
  123.0 8.2 %all-to-all-done.6 = f32[128,1,256]{2,1,0:T(1,128)S(1)} async-done(((f32[128,1,256]{2,1,0:T(1,128)}), f32[128,1,256]{2,1,0:T(1,128)S(1)}, u32[]{:S(2)}, u32[]{:S(2)}) %all-to-all-start.6) | async-done | bytes 131104 | tf_op jit(solution)/shard_map/all_to_all | solution.py:433
  131.2 0.7 copy.15
  131.8 2.3 %finish.1 = f32[2,512]{1,0:T(2,128)S(1)} custom-call(f32[128,256]{1,0:T(8,128)} %bitcast.73, s32[8,512]{1,0:T(8,128)} %get-tuple-element.281.places), custom_call_target="tpu_custom_call" | custom-call | flops 33554432 | bytes 8000000 | tf_op jit(solution)/shard_map/finish/pallas_call | solution.py:434
  (34 shorter events, 2.4 us)
Async XLA Ops:
  24.8 49.1 %copy-start.3 = (bf16[8,64,896]{2,1,0:T(8,128)(2,1)}, bf16[8,64,896]{2,1,0:T(8,128)(2,1)S(1)}, u32[]{:S(2)}) copy-start(bf16[8,64,896]{2,1,0:T(8,128)(2,1)S(1)} %all_to_all.70) | copy-start | bytes 2752516
  24.8 45.0 %all-to-all-start.4 = ((bf16[128,8,512]{2,1,0:T(8,128)(2,1)}), bf16[128,8,512]{2,1,0:T(8,128)(2,1)S(1)}, u32[]{:S(2)}, u32[]{:S(2)}) async-start(bf16[128,8,512]{2,1,0:T(8,128)(2,1)} %bitcast.21), calls=%async_computation.4 | async-start | bytes 2097152 | tf_op jit(solution)/shard_map/all_to_all | solution.py:392
  33.8 33.8 %collective-permute-start.3 = (bf16[512,896]{1,0:T(8,128)(2,1)S(1)}, bf16[512,896]{1,0:T(8,128)(2,1)S(1)}, u32[]{:S(2)}, u32[]{:S(2)}) collective-permute-start(bf16[512,896]{1,0:T(8,128)(2,1)S(1)} %bitcast.66), channel_id=1, source_target_pairs={{1,0},{2,1},{3,2},{0,3},{5,4},{6,5},{7,6},{4,7},{9,8},{10,9},{11,1... | collective-permute-start | bytes 2752520 | tf_op jit(solution)/shard_map/ppermute | solution.py:376
  35.4 32.3 %collective-permute-start.2 = (bf16[512,896]{1,0:T(8,128)(2,1)S(1)}, bf16[512,896]{1,0:T(8,128)(2,1)}, u32[]{:S(2)}, u32[]{:S(2)}) collective-permute-start(bf16[512,896]{1,0:T(8,128)(2,1)S(1)} %bitcast.67), channel_id=1, source_target_pairs={{4,0},{5,1},{6,2},{7,3},{8,4},{9,5},{10,6},{11,7},{12,8},{13,9},{1... | collective-permute-start | bytes 2752520 | tf_op jit(solution)/shard_map/ppermute | solution.py:376
  36.7 51.8 %collective-permute-start.6 = (bf16[512,896]{1,0:T(8,128)(2,1)S(1)}, bf16[512,896]{1,0:T(8,128)(2,1)}, u32[]{:S(2)}, u32[]{:S(2)}) collective-permute-start(bf16[512,896]{1,0:T(8,128)(2,1)S(1)} %bitcast.68), channel_id=1, source_target_pairs={{3,0},{0,1},{1,2},{2,3},{7,4},{4,5},{5,6},{6,7},{11,8},{8,9},{9,10... | collective-permute-start | bytes 2752520 | tf_op jit(solution)/shard_map/ppermute | solution.py:376
  67.7 6.2 %copy-start.5 = (bf16[512,896]{1,0:T(8,128)(2,1)}, bf16[512,896]{1,0:T(8,128)(2,1)S(1)}, u32[]{:S(2)}) copy-start(bf16[512,896]{1,0:T(8,128)(2,1)S(1)} %collective-permute-done.3.b2.refs_2_) | copy-start | bytes 2752516
  67.7 28.3 %collective-permute-start.5 = (bf16[512,896]{1,0:T(8,128)(2,1)S(1)}, bf16[512,896]{1,0:T(8,128)(2,1)}, u32[]{:S(2)}, u32[]{:S(2)}) collective-permute-start(bf16[512,896]{1,0:T(8,128)(2,1)S(1)} %collective-permute-done.3.b2.refs_2_), channel_id=1, source_target_pairs={{1,0},{2,1},{3,2},{0,3},{5,4},{6,5},{7,6},{4,7},{9,8},{10,9},{11,1... | collective-permute-start | bytes 2752520 | tf_op jit(solution)/shard_map/ppermute | solution.py:376
  67.7 28.3 %collective-permute-start.4 = (bf16[512,896]{1,0:T(8,128)(2,1)}, bf16[512,896]{1,0:T(8,128)(2,1)}, u32[]{:S(2)}, u32[]{:S(2)}) collective-permute-start(bf16[512,896]{1,0:T(8,128)(2,1)} %collective-permute-done.2.b1.refs_1_), channel_id=1, source_target_pairs={{4,0},{5,1},{6,2},{7,3},{8,4},{9,5},{10,6},{11,7},{12,8},{13,9},{1... | collective-permute-start | bytes 2752520 | tf_op jit(solution)/shard_map/ppermute | solution.py:376
  69.8 1.0 copy-start.2
  73.9 12.5 %collective-permute-start.11 = (bf16[128,896]{1,0:T(8,128)(2,1)}, bf16[128,896]{1,0:T(8,128)(2,1)S(1)}, u32[]{:S(2)}, u32[]{:S(2)}) collective-permute-start(bf16[128,896]{1,0:T(8,128)(2,1)} %get-tuple-element.277.refs_6_), channel_id=1, source_target_pairs={{2,0},{3,1},{0,2},{1,3},{6,4},{7,5},{4,6},{5,7},{10,8},{11,9},{8,1... | collective-permute-start | bytes 688136 | tf_op jit(solution)/shard_map/ppermute | solution.py:376
  75.6 12.8 %collective-permute-start.10 = (bf16[128,896]{1,0:T(8,128)(2,1)}, bf16[128,896]{1,0:T(8,128)(2,1)S(1)}, u32[]{:S(2)}, u32[]{:S(2)}) collective-permute-start(bf16[128,896]{1,0:T(8,128)(2,1)} %get-tuple-element.277.refs_6_), channel_id=1, source_target_pairs={{8,0},{9,1},{10,2},{11,3},{12,4},{13,5},{14,6},{15,7},{0,8},{1,9},... | collective-permute-start | bytes 688136 | tf_op jit(solution)/shard_map/ppermute | solution.py:376
  86.4 8.5 %copy-start.6 = (bf16[128,896]{1,0:T(8,128)(2,1)}, bf16[128,896]{1,0:T(8,128)(2,1)S(1)}, u32[]{:S(2)}) copy-start(bf16[128,896]{1,0:T(8,128)(2,1)S(1)} %collective-permute-done.11.refs_11_) | copy-start | bytes 688132
  86.4 8.5 %collective-permute-start.9 = (bf16[128,896]{1,0:T(8,128)(2,1)}, bf16[128,896]{1,0:T(8,128)(2,1)S(1)}, u32[]{:S(2)}, u32[]{:S(2)}) collective-permute-start(bf16[128,896]{1,0:T(8,128)(2,1)} %get-tuple-element.277.refs_6_), channel_id=1, source_target_pairs={{3,0},{0,1},{1,2},{2,3},{7,4},{4,5},{5,6},{6,7},{11,8},{8,9},{9,10... | collective-permute-start | bytes 688136 | tf_op jit(solution)/shard_map/ppermute | solution.py:376
  88.4 6.6 %copy-start.7 = (bf16[128,896]{1,0:T(8,128)(2,1)}, bf16[128,896]{1,0:T(8,128)(2,1)S(1)}, u32[]{:S(2)}) copy-start(bf16[128,896]{1,0:T(8,128)(2,1)S(1)} %collective-permute-done.10.refs_10_) | copy-start | bytes 688132
  88.4 7.6 %collective-permute-start.8 = (bf16[128,896]{1,0:T(8,128)(2,1)}, bf16[128,896]{1,0:T(8,128)(2,1)S(1)}, u32[]{:S(2)}, u32[]{:S(2)}) collective-permute-start(bf16[128,896]{1,0:T(8,128)(2,1)} %get-tuple-element.277.refs_6_), channel_id=1, source_target_pairs={{1,0},{2,1},{3,2},{0,3},{5,4},{6,5},{7,6},{4,7},{9,8},{10,9},{11,1... | collective-permute-start | bytes 688136 | tf_op jit(solution)/shard_map/ppermute | solution.py:376
  88.4 7.5 %collective-permute-start.7 = (bf16[128,896]{1,0:T(8,128)(2,1)}, bf16[128,896]{1,0:T(8,128)(2,1)S(1)}, u32[]{:S(2)}, u32[]{:S(2)}) collective-permute-start(bf16[128,896]{1,0:T(8,128)(2,1)} %get-tuple-element.277.refs_6_), channel_id=1, source_target_pairs={{4,0},{5,1},{6,2},{7,3},{8,4},{9,5},{10,6},{11,7},{12,8},{13,9},{1... | collective-permute-start | bytes 688136 | tf_op jit(solution)/shard_map/ppermute | solution.py:376
  95.0 1.0 copy-start.8
  96.0 0.7 copy-start.9
  96.0 0.8 copy-start.10
  105.3 28.8 %copy-start = (s32[512]{0:T(512)S(1)}, s32[512]{0:T(512)}, u32[]{:S(2)}) copy-start(s32[512]{0:T(512)} %param.9) | copy-start | bytes 6148
  105.3 28.8 %copy-start.1 = (bf16[512,768]{1,0:T(8,128)(2,1)S(1)}, bf16[512,768]{1,0:T(8,128)(2,1)}, u32[]{:S(2)}) copy-start(bf16[512,768]{1,0:T(8,128)(2,1)} %rows.1) | copy-start | bytes 2359300
  105.3 28.8 %copy-start.4 = (s32[512]{0:T(512)S(1)}, s32[512]{0:T(512)}, u32[]{:S(2)}) copy-start(s32[512]{0:T(512)} %param.8) | copy-start | bytes 6148
  112.6 18.5 %all-to-all-start.6 = ((f32[128,1,256]{2,1,0:T(1,128)}), f32[128,1,256]{2,1,0:T(1,128)S(1)}, u32[]{:S(2)}, u32[]{:S(2)}) async-start(f32[128,1,256]{2,1,0:T(1,128)} %copy.12), calls=%async_computation.6 | async-start | bytes 262144 | tf_op jit(solution)/shard_map/all_to_all | solution.py:433

commit v3 on v2

v3 whole, which is shorter than its diff:
```python
import jax
import jax.numpy as jnp
from jax import lax
from jax.experimental import pallas as pl
from jax.experimental.pallas import tpu as pltpu
from jax.sharding import PartitionSpec as P

epsilon = 1e-06
sharpness = 8.0

ROWS = 512
FEAT = 768
WIDE = 896
GROUPS = 8
MEMBERS = 16
DEVICES = GROUPS * MEMBERS
SHARE = 8
HELD = DEVICES * SHARE
BLOCK = 640
SENT = BLOCK + 16
OFFSET = 16.0
LOG2E = 1.4426950408889634
AXES = ("grp", "blk")
VMEM_LIMIT = 56 * 1024 * 1024

SPOTS = ((0, 0), (1, 0), (0, 1), (0, 3), (2, 0), (0, 2))
ROW_BLOCKS = (1, 2)


def iota(shape, axis):
    return lax.broadcasted_iota(jnp.int32, shape, axis)


def matmul(a, b, dims, exact=False):
    return lax.dot_general(
        a,
        b,
        (dims, ((), ())),
        precision=lax.Precision.HIGHEST if exact else None,
        preferred_element_type=jnp.float32,
    )


NN = ((1,), (0,))
NT = ((1,), (1,))


def prelude_kernel(labels, slots, rows, spread, places):
    lab = labels[...]
    table = slots[...]
    by_cluster = (iota((ROWS, ROWS), 0) == lab).astype(jnp.bfloat16)
    sub = iota((8, ROWS), 0)
    parts = jnp.where(sub == 0, table >> 6, jnp.where(sub == 1, table & 63, 0)).astype(jnp.bfloat16)
    found = matmul(parts, by_cluster, NN)
    group = found[0:1].astype(jnp.int32)
    local = found[1:2].astype(jnp.int32)
    in_group = sub == group
    before = (iota((ROWS, ROWS), 0) < iota((ROWS, ROWS), 1)).astype(jnp.bfloat16)
    counts = matmul(in_group.astype(jnp.bfloat16), before, NN)
    rank = jnp.sum(jnp.where(in_group, counts, 0.0), axis=0, keepdims=True).astype(jnp.int32)
    holder = group * MEMBERS + ((rank + lax.axis_index("blk")) & (MEMBERS - 1))
    turn = rank >> 4
    places[...] = jnp.where(sub == 0, holder, turn)

    wide = rows[...].astype(jnp.float32)
    norm = lax.rsqrt(jnp.sum(wide * wide, axis=1, keepdims=True) + epsilon)
    units = (wide * norm).astype(jnp.bfloat16)
    lanes = iota((128, ROWS), 0)
    marks = jnp.where(lanes == local, 4.0, 0.0).astype(jnp.bfloat16)
    goal = holder * SHARE + turn
    totals = matmul(
        jnp.ones((128, ROWS), jnp.bfloat16), (lanes - 64 == group).astype(jnp.bfloat16), NT
    )
    totals = jnp.where((iota((128, 128), 0) & (SHARE - 1)) == 0, totals, 0.0)
    for t in range(HELD // 128):
        here = pl.ds(128 * t, 128)
        pick = (lanes + 128 * t == goal).astype(jnp.bfloat16)
        spread[here, :FEAT] = matmul(pick, units, NN).astype(jnp.bfloat16)
        spread[here, FEAT:] = (matmul(pick, marks, NT) + totals).astype(jnp.bfloat16)


def pack_kernel(arrived, packed, over):
    tails = arrived[:, FEAT:]
    own = iota((HELD, 128), 1) < 64
    counted = jnp.where(own, jnp.zeros_like(tails), tails)
    marks = jnp.where(own, tails, jnp.zeros_like(tails))
    one = ((iota((128, HELD), 0) * SHARE) == iota((128, HELD), 1)).astype(jnp.bfloat16)
    counts = matmul(one, counted, NN).astype(jnp.int32)
    turned = iota((128, 128), 0) & (MEMBERS - 1)
    most = jnp.zeros((1, 128), jnp.int32)
    for k in range(MEMBERS):
        gets = (counts + (MEMBERS - 1) - ((k - turned) & (MEMBERS - 1))) >> 4
        most = jnp.maximum(most, jnp.sum(gets, axis=0, keepdims=True))
    over[...] = jnp.broadcast_to((most > BLOCK).astype(jnp.int32), (8, 128))

    held = matmul(jnp.ones((8, 128), jnp.bfloat16), marks, NT) > 0.0
    before = (iota((HELD, HELD), 0) < iota((HELD, HELD), 1)).astype(jnp.bfloat16)
    position = matmul(held.astype(jnp.bfloat16), before, NN)
    position = jnp.where(held, position, -1.0)[0:1].astype(jnp.int32)
    at, line = iota((8, HELD), 1), iota((8, HELD), 0)
    names = jnp.where(line == 0, (at >> 3) + 1, jnp.where(line == 1, at & 7, 0))
    names = names.astype(jnp.bfloat16)
    named = []
    for t in range(BLOCK // 128):
        here = pl.ds(128 * t, 128)
        pick = (iota((128, HELD), 0) + 128 * t == position).astype(jnp.bfloat16)
        packed[here, :FEAT] = matmul(pick, arrived[:, :FEAT], NN).astype(jnp.bfloat16)
        packed[here, FEAT:] = matmul(pick, marks, NN).astype(jnp.bfloat16)
        named.append(matmul(names, pick, NT))
    named = jnp.concatenate(named + [jnp.zeros((8, WIDE - BLOCK), jnp.float32)], axis=1)
    named = jnp.concatenate([named, jnp.zeros_like(named)], axis=0)
    packed[BLOCK:, :] = named.astype(jnp.bfloat16)


def column_fold(x, op):
    while x.shape[0] > 8:
        half = x.shape[0] // 2
        x = op(x[:half], x[half:])
    return x


def row_fold(x, op):
    total = x[:, :128]
    for t in range(1, x.shape[1] // 128):
        total = op(total, x[:, 128 * t : 128 * (t + 1)])
    return total


def clear(*refs):
    for ref in refs:
        ref[...] = jnp.zeros_like(ref)


def tile(x, y, cols, rows, state, diagonal=False):
    col_best, col_mass, row_best, row_mass = state
    product = matmul(x, y, NT)
    if diagonal:
        shape = product.shape
        product = jnp.where(iota(shape, 0) == iota(shape, 1), 0.0, product)
    soft = jnp.exp2((product - (OFFSET + 1.0)) * (sharpness * LOG2E))
    for first, size, c, start in cols:
        part = slice(first, first + size)
        here = slice(start, start + size)
        col_best[c, :, here] = jnp.maximum(
            col_best[c, :, here], column_fold(product[:, part], jnp.maximum)
        )
        col_mass[c, :, here] = col_mass[c, :, here] + column_fold(soft[:, part], jnp.add)
    for first, size, r, start in rows:
        part = slice(first, first + size)
        here = slice(start, start + size)
        row_best[r, here, :] = jnp.maximum(
            row_best[r, here, :], row_fold(product[part], jnp.maximum)
        )
        row_mass[r, here, :] = row_mass[r, here, :] + row_fold(soft[part], jnp.add)


PARTS = ((0, 256), (256, 256), (512, 128))


def square(rows, cols, c, r, state, own=False):
    for i, tall in PARTS:
        for j, wide in PARTS:
            tile(
                rows[i : i + tall, :],
                cols[j : j + wide, :],
                [(0, wide, c, j)],
                [] if r is None else [(0, tall, r, i)],
                state,
                own and i == j,
            )


def settle(e, state):
    col_best, col_mass, row_best, row_mass = state
    best = jnp.max(col_best[e], axis=0, keepdims=True)
    mass = jnp.sum(col_mass[e], axis=0, keepdims=True)
    if e in ROW_BLOCKS:
        r = ROW_BLOCKS.index(e)
        tops, sums = [], []
        for t in range(0, BLOCK, 128):
            tops.append(jnp.max(row_best[r, t : t + 128, :].T, axis=0, keepdims=True))
            sums.append(jnp.sum(row_mass[r, t : t + 128, :].T, axis=0, keepdims=True))
        best = jnp.maximum(best, jnp.concatenate(tops, axis=1))
        mass = mass + jnp.concatenate(sums, axis=1)
    return best, mass


def similarity(best):
    return jnp.where(best > 0.5 * OFFSET, jnp.maximum(best - OFFSET, -1.0), -1.0)


def early_kernel(b0, b1, b2, b3, best_out, mass_out, *state):
    clear(best_out, mass_out, *state)
    square(b0, b0, 0, None, state, True)
    square(b1, b0, 0, 0, state)
    square(b2, b0, 0, 1, state)
    square(b1, b3, 3, 0, state)
    square(b1, b2, 2, 0, state)
    square(b3, b2, 2, None, state)
    for e in range(4):
        best_out[e : e + 1, :], mass_out[e : e + 1, :] = settle(e, state)


def late_kernel(b0, b1, b2, b3, b4, b5, best_in, mass_in, out, *state):
    clear(*state)
    square(b4, b0, 0, None, state)
    square(b4, b5, 5, None, state)
    square(b1, b5, 5, 0, state)
    square(b2, b4, 4, 1, state)
    source_at = iota((DEVICES, BLOCK), 0) + 1
    column = iota((128, BLOCK), 0)
    back = jnp.zeros((DEVICES, 128), jnp.float32)
    for e, block in enumerate((b0, b1, b2, b3, b4, b5)):
        best, mass = settle(e, state)
        best = similarity(jnp.maximum(best, best_in[e : e + 1, :]))
        mass = mass + mass_in[e : e + 1, :]
        names = block[BLOCK:, :BLOCK].astype(jnp.int32)
        source, turn = names[0:1], names[1:2]
        spot = column - 16 * e
        values = jnp.where(
            (spot >= 0) & (spot < 16) & ((spot >> 1) == turn),
            jnp.where((spot & 1) == 0, best, mass),
            0.0,
        )
        back = back + matmul((source_at == source).astype(jnp.float32), values, NT, exact=True)
    out[...] = back


def finish_kernel(arrived, places, result):
    shape = (DEVICES, DEVICES)
    at, col = iota(shape, 0), iota(shape, 1)
    base, ay, az = at >> 4, (at >> 2) & 3, at & 3
    turned = (base & 1) == 1
    best = mass = None
    for e, (dy, dz) in enumerate(SPOTS):
        by = (ay + jnp.where(turned, dy, (-dy) & 3)) & 3
        bz = (az + jnp.where(turned, dz, (-dz) & 3)) & 3
        move = (col == base * MEMBERS + by * 4 + bz).astype(jnp.float32)
        moved = matmul(move, arrived[...], NN, exact=True)
        if e:
            moved = pltpu.roll(moved, 128 - 16 * e, 1)
        best = moved if best is None else jnp.maximum(best, moved)
        mass = moved if mass is None else mass + moved
    merged = jnp.where((col & 1) == 0, best, mass)
    sub = iota((128, ROWS), 0)
    holder = (sub == places[0:1, :]).astype(jnp.float32)
    picked = matmul(merged.T, holder, NN, exact=True)
    turn = places[1:2, :]
    best = jnp.sum(jnp.where(sub == 2 * turn, picked, 0.0), axis=0, keepdims=True)
    mass = jnp.sum(jnp.where(sub == 2 * turn + 1, picked, 0.0), axis=0, keepdims=True)
    result[0:1, :] = best
    result[1:2, :] = jnp.log1p(mass)


def call(kernel, out_shape, scratch=(), flops=0, name=None):
    return pl.pallas_call(
        kernel,
        out_shape=out_shape,
        scratch_shapes=scratch,
        compiler_params=pltpu.CompilerParams(vmem_limit_bytes=VMEM_LIMIT),
        cost_estimate=pl.CostEstimate(flops=flops, bytes_accessed=8_000_000, transcendentals=0),
        name=name,
    )


def hop(dy, dz):
    pairs = []
    for g in range(GROUPS):
        turn = -1 if g & 1 else 1
        for y in range(4):
            for z in range(4):
                source = ((y + turn * dy) % 4) * 4 + (z + turn * dz) % 4
                pairs.append((g * MEMBERS + source, g * MEMBERS + y * 4 + z))
    return pairs


def from_spot(x, dy, dz):
    return lax.ppermute(x, AXES, hop(dy, dz))


def fast(embeddings, labels, cluster_slot):
    f32, bf16, i32 = jnp.float32, jnp.bfloat16, jnp.int32
    shape = jax.ShapeDtypeStruct
    spread, places = call(
        prelude_kernel,
        (shape((HELD, WIDE), bf16), shape((8, ROWS), i32)),
        flops=3_000_000_000,
        name="prelude",
    )(labels.reshape(1, ROWS), cluster_slot.reshape(1, ROWS), embeddings)
    arrived = lax.all_to_all(spread, AXES, split_axis=0, concat_axis=0, tiled=True)
    b0, over = call(
        pack_kernel,
        (shape((SENT, WIDE), bf16), shape((8, 128), i32)),
        flops=3_000_000_000,
        name="pack",
    )(arrived)
    b2 = from_spot(b0, 0, 1)
    b3 = from_spot(b0, 0, 3)
    b1 = from_spot(b0, 1, 0)
    b4 = from_spot(b1, 1, 0)
    b5 = from_spot(b2, 0, 1)
    state = (
        pltpu.VMEM((6, 8, BLOCK), f32),
        pltpu.VMEM((6, 8, BLOCK), f32),
        pltpu.VMEM((2, BLOCK, 128), f32),
        pltpu.VMEM((2, BLOCK, 128), f32),
    )
    best, mass = call(
        early_kernel,
        (shape((8, BLOCK), f32), shape((8, BLOCK), f32)),
        scratch=state,
        flops=6_000_000_000,
        name="early",
    )(b0, b1, b2, b3)
    message = call(
        late_kernel,
        shape((DEVICES, 128), f32),
        scratch=state,
        flops=4_000_000_000,
        name="late",
    )(b0, b1, b2, b3, b4, b5, best, mass)
    answer = lax.all_to_all(message, AXES, split_axis=0, concat_axis=0, tiled=True)
    result = call(
        finish_kernel, shape((2, ROWS), f32), flops=ROWS * ROWS * 128, name="finish"
    )(answer, places)
    return (result[0], result[1]), jnp.max(over)


def general(embeddings, labels, cluster_slot):
    groups = lax.axis_size("grp")
    members = lax.axis_size("blk")
    row_count, feature_count = embeddings.shape
    capacity = row_count // 4
    held = groups * capacity
    widened = embeddings.astype(jnp.float32)
    units = (
        widened * lax.rsqrt(jnp.sum(widened * widened, axis=1, keepdims=True) + epsilon)
    ).astype(jnp.bfloat16)
    slot_ids = cluster_slot[labels]
    owner_group = slot_ids // (cluster_slot.shape[0] // groups)
    owner_onehot = (owner_group[:, None] == jnp.arange(groups, dtype=jnp.int32)[None, :]).astype(
        jnp.int32
    )
    earlier = jnp.cumsum(owner_onehot, axis=0) - owner_onehot
    send_place = owner_group * capacity + jnp.sum(earlier * owner_onehot, axis=1)
    outgoing = jnp.zeros((held, feature_count), jnp.bfloat16).at[send_place].set(units)
    outgoing_slots = jnp.full((held,), -1, jnp.int32).at[send_place].set(slot_ids)
    rows = lax.all_to_all(outgoing, "grp", split_axis=0, concat_axis=0, tiled=True)
    slots = lax.all_to_all(outgoing_slots, "grp", split_axis=0, concat_axis=0, tiled=True)
    ring = [(i, (i + 1) % members) for i in range(members)]
    local = jnp.arange(held, dtype=jnp.int32)
    place = lax.axis_index("blk")
    own_ids = place * held + local

    def step(turn, carry):
        key_rows, key_slots, best, mass = carry
        scores = jnp.einsum("qd,kd->qk", rows, key_rows, preferred_element_type=jnp.float32)
        matched = (slots[:, None] == key_slots[None, :]) & (key_slots[None, :] >= 0)
        owner = (place - turn) & (members - 1)
        matched = matched & (own_ids[:, None] != (owner * held + local)[None, :])
        best = jnp.maximum(best, jnp.max(jnp.where(matched, scores, -1.0), axis=1))
        mass = mass + jnp.sum(
            jnp.where(matched, jnp.exp(sharpness * (scores - 1.0)), 0.0), axis=1
        )
        key_rows = lax.ppermute(key_rows, "blk", ring)
        key_slots = lax.ppermute(key_slots, "blk", ring)
        return key_rows, key_slots, best, mass

    start = (
        rows,
        slots,
        jnp.full((held,), -1.0, jnp.float32),
        jnp.zeros((held,), jnp.float32),
    )
    _, _, best, mass = lax.fori_loop(0, members, step, start)
    best = lax.all_to_all(best, "grp", split_axis=0, concat_axis=0, tiled=True)
    mass = lax.all_to_all(mass, "grp", split_axis=0, concat_axis=0, tiled=True)
    return (best[send_place], jnp.log1p(mass[send_place]))


def body(embeddings, labels, cluster_slot):
    result, over = fast(embeddings, labels, cluster_slot)
    return lax.cond(
        over > 0, lambda: general(embeddings, labels, cluster_slot), lambda: result
    )


def solution(mesh):
    placed = (P(AXES, None), P(AXES), P())
    return jax.shard_map(
        body,
        mesh=mesh,
        in_specs=placed,
        out_specs=(P(AXES), P(AXES)),
        check_vma=False,
    )
```

time: 135 us -> 124 us (0.919)
  blocking collectives: 19.6 us -> 38.4 us
  waiting for transfers between devices: 48.6 us -> 33.5 us
  starting transfers between devices: 28.9 us -> 14.9 us
  local copies, waits for them, and re-layouts: 5.87 us -> 3.69 us
    all_to_all x1, blocking collectives: 19.6 us -> 38.4 us  [fast(): lax.all_to_all(spread, AXES, split_axis=0, concat_axis=0, tiled=True)]
    ppermute x10 -> x5, waiting for transfers between devices: 40.4 us -> 25.1 us  [from_spot(): return lax.ppermute(x, AXES, hop(dy, dz))]
    all_to_all x1 -> x0, starting transfers between devices: 9 us -> none  [fast(): lax.all_to_all(spread, AXES, split_axis=0, concat_axis=0, tiled=True)]
    ppermute x10 -> x5, starting transfers between devices: 11.4 us -> 5.29 us  [from_spot(): return lax.ppermute(x, AXES, hop(dy, dz))]
    all_to_all x1 -> x0, local copies, waits for them, and re-layouts: 1.68 us -> none  [fast(): lax.all_to_all(message, AXES, split_axis=0, concat_axis=0, tiled=True)]
    pallas_call x6 -> x5, Pallas kernels: 30.4 us -> 31.3 us  [the longest x1 10.2 us: fast(): call(early_kernel, (shape((8, BLOCK), f32), shape((8, BLOCK), f32)), scra...]
    unnamed x23 -> x20, local copies, waits for them, and re-layouts: 2.41 us -> 3.1 us
  transfers between devices with their start and end apart: 12 -> 6, of which waited for: 5 -> 4; matrix products, arithmetic and copies ran while one was open for 1% -> 1% of each run, Pallas kernels for 7% -> 8%
where the time goes in v3:
time: 124 us
  blocking collectives  38.4 us (31%)
  waiting for transfers between devices  33.5 us (27%)
  Pallas kernels  31.3 us (25%)
  starting transfers between devices  14.9 us (12%)
  local copies, waits for them, and re-layouts  3.69 us (3%)
  between operations  1.33 us (1%)
    all_to_all x1, blocking collectives, fast(): lax.all_to_all(spread, AXES, split_axis=0, concat_axis=0, tiled=True)  38.4 us
    ppermute x5, waiting for transfers between devices, from_spot(): return lax.ppermute(x, AXES, hop(dy, dz))  25.1 us
    pallas_call x1, Pallas kernels, fast(): call(early_kernel, (shape((8, BLOCK), f32), shape((8, BLOCK), f32)), scra...  10.2 us
    pallas_call x1, Pallas kernels, fast(): call(late_kernel, shape((DEVICES, 128), f32), scratch=state, flops=400000...  10.2 us
    all_to_all x1, starting transfers between devices, fast(): lax.all_to_all(message, AXES, split_axis=0, concat_axis=0, tiled=True)  9.58 us
    all_to_all x1, waiting for transfers between devices, fast(): lax.all_to_all(message, AXES, split_axis=0, concat_axis=0, tiled=True)  8.42 us
    ppermute x5, starting transfers between devices, from_spot(): return lax.ppermute(x, AXES, hop(dy, dz))  5.29 us
    pallas_call x1, Pallas kernels, fast(): call(pack_kernel, (shape((SENT, WIDE), bf16), shape((8, 128), i32)), flop...  4.87 us
  transfers between devices with their start and end apart: 6, of which 4 were waited for; matrix products, arithmetic and copies ran while one was open for 1% of the time, Pallas kernels for 8%

profile of v3, /device:TPU:1, one launch (start us, length us, event | category | flops | bytes accessed | tf_op | source)
XLA Modules:
  0.0 123.7 jit_solution(3640545120925605748)
XLA Ops:
  0.6 4.1 %prelude.1 = (bf16[1024,896]{1,0:T(8,128)(2,1)}, s32[8,512]{1,0:T(8,128)}) custom-call(s32[1,512]{1,0:T(1,128)} %bitcast.74, s32[1,512]{1,0:T(1,128)} %bitcast.59, bf16[512,768]{1,0:T(8,128)(2,1)} %rows.1), custom_call_target="tpu_custom_call" | custom-call | flops 3000000000 | bytes 8000000 | tf_op jit(solution)/shard_map/prelude/pallas_call | solution.py:284
  4.7 38.4 %all_to_all.59 = bf16[128,8,896]{2,1,0:T(8,128)(2,1)} all-to-all(bf16[128,8,896]{2,1,0:T(8,128)(2,1)} %bitcast.63), channel_id=1, replica_groups=mesh['grp'=8,'blk'=16] {'grp','blk'}, dimensions={0} | all-to-all | bytes 3670016 | tf_op jit(solution)/shard_map/all_to_all | solution.py:290
  43.1 4.9 %pack.1 = (bf16[656,896]{1,0:T(8,128)(2,1)}, s32[8,128]{1,0:T(8,128)}) custom-call(bf16[1024,896]{1,0:T(8,128)(2,1)} %bitcast.62), custom_call_target="tpu_custom_call" | custom-call | flops 3000000000 | bytes 8000000 | tf_op jit(solution)/shard_map/pack/pallas_call | solution.py:291
  48.0 0.7 collective-permute-start.3
  48.7 0.8 collective-permute-start.2
  49.5 2.1 %collective-permute-start.4 = (bf16[656,896]{1,0:T(8,128)(2,1)}, bf16[656,896]{1,0:T(8,128)(2,1)S(1)}, u32[]{:S(2)}, u32[]{:S(2)}) collective-permute-start(bf16[656,896]{1,0:T(8,128)(2,1)} %get-tuple-element.270.b0), channel_id=1, source_target_pairs={{3,0},{0,1},{1,2},{2,3},{7,4},{4,5},{5,6},{6,7},{11,8},{8,9},{9,10... | collective-permute-start | bytes 3526664 | tf_op jit(solution)/shard_map/ppermute | solution.py:278
  51.6 21.4 %collective-permute-done.3.b2 = bf16[656,896]{1,0:T(8,128)(2,1)S(1)} collective-permute-done((bf16[656,896]{1,0:T(8,128)(2,1)}, bf16[656,896]{1,0:T(8,128)(2,1)S(1)}, u32[]{:S(2)}, u32[]{:S(2)}) %collective-permute-start.3) | collective-permute-done | bytes 1175584 | tf_op jit(solution)/shard_map/ppermute | solution.py:278
  73.0 0.1 collective-permute-start.6
  73.2 0.0 collective-permute-done.2.b1
  73.2 1.5 %collective-permute-start.5 = (bf16[656,896]{1,0:T(8,128)(2,1)S(1)}, bf16[656,896]{1,0:T(8,128)(2,1)S(1)}, u32[]{:S(2)}, u32[]{:S(2)}) collective-permute-start(bf16[656,896]{1,0:T(8,128)(2,1)S(1)} %collective-permute-done.2.b1), channel_id=1, source_target_pairs={{4,0},{5,1},{6,2},{7,3},{8,4},{9,5},{10,6},{11,7},{12,8},{13,9},{1... | collective-permute-start | bytes 3526664 | tf_op jit(solution)/shard_map/ppermute | solution.py:278
  74.7 2.6 %collective-permute-done.4.b3 = bf16[656,896]{1,0:T(8,128)(2,1)S(1)} collective-permute-done((bf16[656,896]{1,0:T(8,128)(2,1)}, bf16[656,896]{1,0:T(8,128)(2,1)S(1)}, u32[]{:S(2)}, u32[]{:S(2)}) %collective-permute-start.4) | collective-permute-done | bytes 1175584 | tf_op jit(solution)/shard_map/ppermute | solution.py:278
  77.3 1.0 copy-done.7
  78.3 10.2 %early.1 = (f32[8,640]{1,0:T(8,128)}, f32[8,640]{1,0:T(8,128)}) custom-call(bf16[656,896]{1,0:T(8,128)(2,1)} %get-tuple-element.270.b0, bf16[656,896]{1,0:T(8,128)(2,1)} %copy-done.6, bf16[656,896]{1,0:T(8,128)(2,1)} %copy-done.5, bf16[656,896]{1,0:T(8,128)(2,1)} %copy-done.7), custom_call_target="tpu_custom_call" | custom-call | flops 6000000000 | bytes 8000000 | tf_op jit(solution)/shard_map/early/pallas_call | solution.py:308
  88.6 1.0 collective-permute-done.6.b5
  89.6 1.1 copy-done.8
  90.6 0.4 copy-done.9
  91.0 10.2 %late.1 = f32[128,128]{1,0:T(8,128)} custom-call(bf16[656,896]{1,0:T(8,128)(2,1)} %get-tuple-element.270.b0, bf16[656,896]{1,0:T(8,128)(2,1)} %copy-done.6, bf16[656,896]{1,0:T(8,128)(2,1)} %copy-done.5, bf16[656,896]{1,0:T(8,128)(2,1)} %copy-done.7, bf16[656,896]{1,0:T(8,128)(2,1)} %copy-done.9, bf16[656,896]{1,0:T(8,128)(2,1)} %copy-done.8, ...), custom_call_target="tpu_custom_call" | custom-call | flops 4000000000 | bytes 8000000 | tf_op jit(solution)/shard_map/late/pallas_call | solution.py:315
  101.2 9.6 %all-to-all-start.5 = ((f32[128,1,128]{2,1,0:T(1,128)}), f32[128,1,128]{2,1,0:T(1,128)S(1)}, u32[]{:S(2)}, u32[]{:S(2)}) async-start(f32[128,1,128]{2,1,0:T(1,128)} %bitcast.65), calls=%async_computation.5 | async-start | bytes 131072 | tf_op jit(solution)/shard_map/all_to_all | solution.py:322
  110.8 0.6 reduce_max.25
  112.1 8.4 %all-to-all-done.5 = f32[128,1,128]{2,1,0:T(1,128)S(1)} async-done(((f32[128,1,128]{2,1,0:T(1,128)}), f32[128,1,128]{2,1,0:T(1,128)S(1)}, u32[]{:S(2)}, u32[]{:S(2)}) %all-to-all-start.5) | async-done | bytes 65568 | tf_op jit(solution)/shard_map/all_to_all | solution.py:322
  120.5 0.6 copy-done.2
  121.2 1.9 %finish.1 = f32[2,512]{1,0:T(2,128)S(1)} custom-call(f32[128,128]{1,0:T(8,128)} %bitcast.66, s32[8,512]{1,0:T(8,128)} %get-tuple-element.273.places), custom_call_target="tpu_custom_call" | custom-call | flops 33554432 | bytes 8000000 | tf_op jit(solution)/shard_map/finish/pallas_call | solution.py:323
  123.1 0.6 conditional.1
  123.1 0.6 fusion.20
  (17 shorter events, 0.0 us)
Async XLA Ops:
  48.0 25.1 %collective-permute-start.3 = (bf16[656,896]{1,0:T(8,128)(2,1)}, bf16[656,896]{1,0:T(8,128)(2,1)S(1)}, u32[]{:S(2)}, u32[]{:S(2)}) collective-permute-start(bf16[656,896]{1,0:T(8,128)(2,1)} %get-tuple-element.270.b0), channel_id=1, source_target_pairs={{1,0},{2,1},{3,2},{0,3},{5,4},{6,5},{7,6},{4,7},{9,8},{10,9},{11,1... | collective-permute-start | bytes 3526664 | tf_op jit(solution)/shard_map/ppermute | solution.py:278
  48.7 24.5 %collective-permute-start.2 = (bf16[656,896]{1,0:T(8,128)(2,1)}, bf16[656,896]{1,0:T(8,128)(2,1)S(1)}, u32[]{:S(2)}, u32[]{:S(2)}) collective-permute-start(bf16[656,896]{1,0:T(8,128)(2,1)} %get-tuple-element.270.b0), channel_id=1, source_target_pairs={{4,0},{5,1},{6,2},{7,3},{8,4},{9,5},{10,6},{11,7},{12,8},{13,9},{1... | collective-permute-start | bytes 3526664 | tf_op jit(solution)/shard_map/ppermute | solution.py:278
  49.5 27.8 %collective-permute-start.4 = (bf16[656,896]{1,0:T(8,128)(2,1)}, bf16[656,896]{1,0:T(8,128)(2,1)S(1)}, u32[]{:S(2)}, u32[]{:S(2)}) collective-permute-start(bf16[656,896]{1,0:T(8,128)(2,1)} %get-tuple-element.270.b0), channel_id=1, source_target_pairs={{3,0},{0,1},{1,2},{2,3},{7,4},{4,5},{5,6},{6,7},{11,8},{8,9},{9,10... | collective-permute-start | bytes 3526664 | tf_op jit(solution)/shard_map/ppermute | solution.py:278
  73.0 4.3 %copy-start.5 = (bf16[656,896]{1,0:T(8,128)(2,1)}, bf16[656,896]{1,0:T(8,128)(2,1)S(1)}, u32[]{:S(2)}) copy-start(bf16[656,896]{1,0:T(8,128)(2,1)S(1)} %collective-permute-done.3.b2) | copy-start | bytes 3526660
  73.0 16.5 %collective-permute-start.6 = (bf16[656,896]{1,0:T(8,128)(2,1)S(1)}, bf16[656,896]{1,0:T(8,128)(2,1)S(1)}, u32[]{:S(2)}, u32[]{:S(2)}) collective-permute-start(bf16[656,896]{1,0:T(8,128)(2,1)S(1)} %collective-permute-done.3.b2), channel_id=1, source_target_pairs={{1,0},{2,1},{3,2},{0,3},{5,4},{6,5},{7,6},{4,7},{9,8},{10,9},{11,1... | collective-permute-start | bytes 3526664 | tf_op jit(solution)/shard_map/ppermute | solution.py:278
  73.2 4.1 %copy-start.6 = (bf16[656,896]{1,0:T(8,128)(2,1)}, bf16[656,896]{1,0:T(8,128)(2,1)S(1)}, u32[]{:S(2)}) copy-start(bf16[656,896]{1,0:T(8,128)(2,1)S(1)} %collective-permute-done.2.b1) | copy-start | bytes 3526660
  73.2 16.4 %collective-permute-start.5 = (bf16[656,896]{1,0:T(8,128)(2,1)S(1)}, bf16[656,896]{1,0:T(8,128)(2,1)S(1)}, u32[]{:S(2)}, u32[]{:S(2)}) collective-permute-start(bf16[656,896]{1,0:T(8,128)(2,1)S(1)} %collective-permute-done.2.b1), channel_id=1, source_target_pairs={{4,0},{5,1},{6,2},{7,3},{8,4},{9,5},{10,6},{11,7},{12,8},{13,9},{1... | collective-permute-start | bytes 3526664 | tf_op jit(solution)/shard_map/ppermute | solution.py:278
  77.3 1.0 copy-start.7
  89.6 1.1 copy-start.8
  89.6 1.4 %copy-start.9 = (bf16[656,896]{1,0:T(8,128)(2,1)}, bf16[656,896]{1,0:T(8,128)(2,1)S(1)}, u32[]{:S(2)}) copy-start(bf16[656,896]{1,0:T(8,128)(2,1)S(1)} %collective-permute-done.5.b4) | copy-start | bytes 3526660
  91.0 19.8 %copy-start.3 = (s32[8,128]{1,0:T(8,128)S(1)}, s32[8,128]{1,0:T(8,128)}, u32[]{:S(2)}) copy-start(s32[8,128]{1,0:T(8,128)} %get-tuple-element.269) | copy-start | bytes 12292
  91.0 30.1 %copy-start = (s32[512]{0:T(512)S(1)}, s32[512]{0:T(512)}, u32[]{:S(2)}) copy-start(s32[512]{0:T(512)} %param.9) | copy-start | bytes 6148
  91.0 30.1 %copy-start.1 = (bf16[512,768]{1,0:T(8,128)(2,1)S(1)}, bf16[512,768]{1,0:T(8,128)(2,1)}, u32[]{:S(2)}) copy-start(bf16[512,768]{1,0:T(8,128)(2,1)} %rows.1) | copy-start | bytes 2359300
  91.0 30.1 %copy-start.4 = (s32[512]{0:T(512)S(1)}, s32[512]{0:T(512)}, u32[]{:S(2)}) copy-start(s32[512]{0:T(512)} %param.8) | copy-start | bytes 6148
  101.2 19.3 %all-to-all-start.5 = ((f32[128,1,128]{2,1,0:T(1,128)}), f32[128,1,128]{2,1,0:T(1,128)S(1)}, u32[]{:S(2)}, u32[]{:S(2)}) async-start(f32[128,1,128]{2,1,0:T(1,128)} %bitcast.65), calls=%async_computation.5 | async-start | bytes 131072 | tf_op jit(solution)/shard_map/all_to_all | solution.py:322
  120.5 0.6 copy-start.2

commit v4 on v3

--- a/solution.py
+++ b/solution.py
@@ -17,8 +17,8 @@
 SHARE = 8
 HELD = DEVICES * SHARE
 BLOCK = 640
-SENT = BLOCK + 16
-OFFSET = 16.0
+ROOM = BLOCK - 16
+APART = -64.0
 LOG2E = 1.4426950408889634
 AXES = ("grp", "blk")
 VMEM_LIMIT = 56 * 1024 * 1024
@@ -43,6 +43,19 @@
 
 NN = ((1,), (0,))
 NT = ((1,), (1,))
+
+
+def split(x):
+    high = x.astype(jnp.bfloat16)
+    rest = x - high.astype(jnp.float32)
+    middle = rest.astype(jnp.bfloat16)
+    low = (rest - middle.astype(jnp.float32)).astype(jnp.bfloat16)
+    return jnp.concatenate([high, middle, low], axis=0)
+
+
+def joined(x):
+    size = x.shape[0] // 3
+    return x[:size] + x[size : 2 * size] + x[2 * size :]
 
 
 def prelude_kernel(labels, slots, rows, spread, places):
@@ -53,7 +66,6 @@
     parts = jnp.where(sub == 0, table >> 6, jnp.where(sub == 1, table & 63, 0)).astype(jnp.bfloat16)
     found = matmul(parts, by_cluster, NN)
     group = found[0:1].astype(jnp.int32)
-    local = found[1:2].astype(jnp.int32)
     in_group = sub == group
     before = (iota((ROWS, ROWS), 0) < iota((ROWS, ROWS), 1)).astype(jnp.bfloat16)
     counts = matmul(in_group.astype(jnp.bfloat16), before, NN)
@@ -66,50 +78,44 @@
     norm = lax.rsqrt(jnp.sum(wide * wide, axis=1, keepdims=True) + epsilon)
     units = (wide * norm).astype(jnp.bfloat16)
     lanes = iota((128, ROWS), 0)
-    marks = jnp.where(lanes == local, 4.0, 0.0).astype(jnp.bfloat16)
+    marks = jnp.where(lanes == 0, found[1:2] + 1.0, 0.0).astype(jnp.bfloat16)
     goal = holder * SHARE + turn
     totals = matmul(
         jnp.ones((128, ROWS), jnp.bfloat16), (lanes - 64 == group).astype(jnp.bfloat16), NT
     )
-    totals = jnp.where((iota((128, 128), 0) & (SHARE - 1)) == 0, totals, 0.0)
-    for t in range(HELD // 128):
-        here = pl.ds(128 * t, 128)
-        pick = (lanes + 128 * t == goal).astype(jnp.bfloat16)
+    totals = jnp.where((iota((ROWS, 128), 0) & (SHARE - 1)) == 0, totals[0:1], 0.0)
+    for t in range(0, HELD, ROWS):
+        here = pl.ds(t, ROWS)
+        pick = (iota((ROWS, ROWS), 0) + t == goal).astype(jnp.bfloat16)
         spread[here, :FEAT] = matmul(pick, units, NN).astype(jnp.bfloat16)
         spread[here, FEAT:] = (matmul(pick, marks, NT) + totals).astype(jnp.bfloat16)
 
 
 def pack_kernel(arrived, packed, over):
     tails = arrived[:, FEAT:]
-    own = iota((HELD, 128), 1) < 64
-    counted = jnp.where(own, jnp.zeros_like(tails), tails)
-    marks = jnp.where(own, tails, jnp.zeros_like(tails))
     one = ((iota((128, HELD), 0) * SHARE) == iota((128, HELD), 1)).astype(jnp.bfloat16)
-    counts = matmul(one, counted, NN).astype(jnp.int32)
+    counts = matmul(one, tails, NN).astype(jnp.int32)
+    counts = jnp.where(iota((128, 128), 1) >= 64, counts, 0)
     turned = iota((128, 128), 0) & (MEMBERS - 1)
     most = jnp.zeros((1, 128), jnp.int32)
     for k in range(MEMBERS):
         gets = (counts + (MEMBERS - 1) - ((k - turned) & (MEMBERS - 1))) >> 4
         most = jnp.maximum(most, jnp.sum(gets, axis=0, keepdims=True))
-    over[...] = jnp.broadcast_to((most > BLOCK).astype(jnp.int32), (8, 128))
-
-    held = matmul(jnp.ones((8, 128), jnp.bfloat16), marks, NT) > 0.0
+    over[...] = jnp.broadcast_to((most > ROOM).astype(jnp.int32), (8, 128))
+
+    at, line = iota((8, HELD), 1), iota((8, HELD), 0)
+    clusters = matmul((iota((8, 128), 1) == 0).astype(jnp.bfloat16), tails, NT)
+    held = clusters > 0.0
     before = (iota((HELD, HELD), 0) < iota((HELD, HELD), 1)).astype(jnp.bfloat16)
     position = matmul(held.astype(jnp.bfloat16), before, NN)
     position = jnp.where(held, position, -1.0)[0:1].astype(jnp.int32)
-    at, line = iota((8, HELD), 1), iota((8, HELD), 0)
-    names = jnp.where(line == 0, (at >> 3) + 1, jnp.where(line == 1, at & 7, 0))
-    names = names.astype(jnp.bfloat16)
-    named = []
-    for t in range(BLOCK // 128):
-        here = pl.ds(128 * t, 128)
-        pick = (iota((128, HELD), 0) + 128 * t == position).astype(jnp.bfloat16)
-        packed[here, :FEAT] = matmul(pick, arrived[:, :FEAT], NN).astype(jnp.bfloat16)
-        packed[here, FEAT:] = matmul(pick, marks, NN).astype(jnp.bfloat16)
-        named.append(matmul(names, pick, NT))
-    named = jnp.concatenate(named + [jnp.zeros((8, WIDE - BLOCK), jnp.float32)], axis=1)
-    named = jnp.concatenate([named, jnp.zeros_like(named)], axis=0)
-    packed[BLOCK:, :] = named.astype(jnp.bfloat16)
+    names = jnp.where(line == 1, (at >> 3) + 1, jnp.where(line == 2, at & 7, 0))
+    names = jnp.where(line == 0, clusters, names.astype(jnp.float32)).astype(jnp.bfloat16)
+    pick = (iota((BLOCK, HELD), 0) == position).astype(jnp.bfloat16)
+    packed[:ROOM, :] = matmul(pick[:ROOM], arrived[:, :FEAT], NN).astype(jnp.bfloat16)
+    named = matmul(names, pick, NT)
+    named = jnp.concatenate([named, jnp.zeros((8, FEAT - BLOCK), jnp.float32)], axis=1)
+    packed[ROOM:, :] = jnp.concatenate([named, jnp.zeros_like(named)], axis=0).astype(jnp.bfloat16)
 
 
 def column_fold(x, op):
@@ -126,52 +132,58 @@
     return total
 
 
-def clear(*refs):
-    for ref in refs:
+PARTS = ((0, 256), (256, 256), (512, 128))
+
+
+def clear(state):
+    col_best, col_mass, row_best, row_mass = state[:4]
+    for ref in (col_best, row_best):
+        ref[...] = jnp.full_like(ref, APART)
+    for ref in (col_mass, row_mass):
         ref[...] = jnp.zeros_like(ref)
 
 
-def tile(x, y, cols, rows, state, diagonal=False):
-    col_best, col_mass, row_best, row_mass = state
-    product = matmul(x, y, NT)
-    if diagonal:
-        shape = product.shape
-        product = jnp.where(iota(shape, 0) == iota(shape, 1), 0.0, product)
-    soft = jnp.exp2((product - (OFFSET + 1.0)) * (sharpness * LOG2E))
-    for first, size, c, start in cols:
-        part = slice(first, first + size)
-        here = slice(start, start + size)
-        col_best[c, :, here] = jnp.maximum(
-            col_best[c, :, here], column_fold(product[:, part], jnp.maximum)
-        )
-        col_mass[c, :, here] = col_mass[c, :, here] + column_fold(soft[:, part], jnp.add)
-    for first, size, r, start in rows:
-        part = slice(first, first + size)
-        here = slice(start, start + size)
-        row_best[r, here, :] = jnp.maximum(
-            row_best[r, here, :], row_fold(product[part], jnp.maximum)
-        )
-        row_mass[r, here, :] = row_mass[r, here, :] + row_fold(soft[part], jnp.add)
-
-
-PARTS = ((0, 256), (256, 256), (512, 128))
-
-
-def square(rows, cols, c, r, state, own=False):
+def names_of(block):
+    return block[ROOM:, :BLOCK].astype(jnp.float32)
+
+
+def spell(block, place, state):
+    clusters = names_of(block)[0:1]
+    clusters = jnp.where(clusters > 0.0, clusters, -1.0)
+    for t in range(0, BLOCK, 128):
+        here = slice(t, t + 128)
+        state[4][place, here, :] = jnp.broadcast_to(clusters[:, here], (128, 128)).T
+
+
+def square(rows, cols, place, c, r, state, own=False):
+    col_best, col_mass, row_best, row_mass, spelt = state
+    clusters = names_of(cols)[0:1]
     for i, tall in PARTS:
         for j, wide in PARTS:
-            tile(
-                rows[i : i + tall, :],
-                cols[j : j + wide, :],
-                [(0, wide, c, j)],
-                [] if r is None else [(0, tall, r, i)],
-                state,
-                own and i == j,
-            )
+            product = matmul(rows[i : i + tall, :], cols[j : j + wide, :], NT)
+            down = slice(i, i + tall)
+            mine = spelt[place, down, :]
+            tops = sums = None
+            for t in range(0, wide, 128):
+                across = slice(j + t, j + t + 128)
+                match = mine == clusters[:, across]
+                if own and i == j:
+                    match = match & (iota((tall, 128), 0) != iota((tall, 128), 1) + t)
+                score = jnp.where(match, product[:, t : t + 128], APART)
+                soft = jnp.exp2((score - 1.0) * (sharpness * LOG2E))
+                col_best[c, :, across] = jnp.maximum(
+                    col_best[c, :, across], column_fold(score, jnp.maximum)
+                )
+                col_mass[c, :, across] = col_mass[c, :, across] + column_fold(soft, jnp.add)
+                tops = score if tops is None else jnp.maximum(tops, score)
+                sums = soft if sums is None else sums + soft
+            if r is not None:
+                row_best[r, down, :] = jnp.maximum(row_best[r, down, :], tops)
+                row_mass[r, down, :] = row_mass[r, down, :] + sums
 
 
 def settle(e, state):
-    col_best, col_mass, row_best, row_mass = state
+    col_best, col_mass, row_best, row_mass = state[:4]
     best = jnp.max(col_best[e], axis=0, keepdims=True)
     mass = jnp.sum(col_mass[e], axis=0, keepdims=True)
     if e in ROW_BLOCKS:
@@ -185,71 +197,71 @@
     return best, mass
 
 
-def similarity(best):
-    return jnp.where(best > 0.5 * OFFSET, jnp.maximum(best - OFFSET, -1.0), -1.0)
-
-
 def early_kernel(b0, b1, b2, b3, best_out, mass_out, *state):
-    clear(best_out, mass_out, *state)
-    square(b0, b0, 0, None, state, True)
-    square(b1, b0, 0, 0, state)
-    square(b2, b0, 0, 1, state)
-    square(b1, b3, 3, 0, state)
-    square(b1, b2, 2, 0, state)
-    square(b3, b2, 2, None, state)
+    clear(state)
+    for place, block in enumerate((b0, b1, b2, b3)):
+        spell(block, place, state)
+    square(b0, b0, 0, 0, None, state, True)
+    square(b1, b0, 1, 0, 0, state)
+    square(b2, b0, 2, 0, 1, state)
+    square(b1, b3, 1, 3, 0, state)
+    square(b1, b2, 1, 2, 0, state)
+    square(b3, b2, 3, 2, None, state)
+    best_out[...] = jnp.full_like(best_out, APART)
+    mass_out[...] = jnp.zeros_like(mass_out)
     for e in range(4):
         best_out[e : e + 1, :], mass_out[e : e + 1, :] = settle(e, state)
 
 
 def late_kernel(b0, b1, b2, b3, b4, b5, best_in, mass_in, out, *state):
-    clear(*state)
-    square(b4, b0, 0, None, state)
-    square(b4, b5, 5, None, state)
-    square(b1, b5, 5, 0, state)
-    square(b2, b4, 4, 1, state)
-    source_at = iota((DEVICES, BLOCK), 0) + 1
-    column = iota((128, BLOCK), 0)
-    back = jnp.zeros((DEVICES, 128), jnp.float32)
+    clear(state)
+    for place, block in enumerate((b4, b1, b2)):
+        spell(block, place, state)
+    square(b4, b0, 0, 0, None, state)
+    square(b4, b5, 0, 5, None, state)
+    square(b1, b5, 1, 5, 0, state)
+    square(b2, b4, 2, 4, 1, state)
+    source_at = (iota((DEVICES, BLOCK), 0) + 1).astype(jnp.float32)
+    line = iota((16, BLOCK), 0)
+    back = []
     for e, block in enumerate((b0, b1, b2, b3, b4, b5)):
         best, mass = settle(e, state)
-        best = similarity(jnp.maximum(best, best_in[e : e + 1, :]))
+        best = jnp.maximum(jnp.maximum(best, best_in[e : e + 1, :]), -1.0)
         mass = mass + mass_in[e : e + 1, :]
-        names = block[BLOCK:, :BLOCK].astype(jnp.int32)
-        source, turn = names[0:1], names[1:2]
-        spot = column - 16 * e
-        values = jnp.where(
-            (spot >= 0) & (spot < 16) & ((spot >> 1) == turn),
-            jnp.where((spot & 1) == 0, best, mass),
-            0.0,
-        )
-        back = back + matmul((source_at == source).astype(jnp.float32), values, NT, exact=True)
-    out[...] = back
-
-
-def finish_kernel(arrived, places, result):
+        names = names_of(block)
+        values = jnp.where((line & 1) == 0, best, mass)
+        values = jnp.where((line >> 1).astype(jnp.float32) == names[2:3], values, 0.0)
+        to = (source_at == names[1:2]).astype(jnp.bfloat16)
+        back.append(joined(matmul(split(values), to, NT)))
+    back.append(jnp.zeros((128 - 16 * len(back), DEVICES), jnp.float32))
+    out[...] = jnp.concatenate(back, axis=0).T
+
+
+def finish_kernel(arrived, places, best_out, mass_out):
     shape = (DEVICES, DEVICES)
     at, col = iota(shape, 0), iota(shape, 1)
     base, ay, az = at >> 4, (at >> 2) & 3, at & 3
     turned = (base & 1) == 1
     best = mass = None
+    pieces = split(arrived[...].T)
     for e, (dy, dz) in enumerate(SPOTS):
         by = (ay + jnp.where(turned, dy, (-dy) & 3)) & 3
         bz = (az + jnp.where(turned, dz, (-dz) & 3)) & 3
-        move = (col == base * MEMBERS + by * 4 + bz).astype(jnp.float32)
-        moved = matmul(move, arrived[...], NN, exact=True)
-        if e:
-            moved = pltpu.roll(moved, 128 - 16 * e, 1)
+        move = (col == base * MEMBERS + by * 4 + bz).astype(jnp.bfloat16)
+        part = jnp.concatenate(
+            [pieces[128 * p + 16 * e : 128 * p + 16 * e + 16] for p in range(3)], axis=0
+        )
+        moved = joined(matmul(part, move, NT))
         best = moved if best is None else jnp.maximum(best, moved)
         mass = moved if mass is None else mass + moved
-    merged = jnp.where((col & 1) == 0, best, mass)
-    sub = iota((128, ROWS), 0)
-    holder = (sub == places[0:1, :]).astype(jnp.float32)
-    picked = matmul(merged.T, holder, NN, exact=True)
+    merged = jnp.where((iota((16, DEVICES), 0) & 1) == 0, best, mass)
+    holder = (iota((DEVICES, ROWS), 0) == places[0:1, :]).astype(jnp.bfloat16)
+    picked = joined(matmul(split(merged), holder, NN))
+    line = iota((16, ROWS), 0)
     turn = places[1:2, :]
-    best = jnp.sum(jnp.where(sub == 2 * turn, picked, 0.0), axis=0, keepdims=True)
-    mass = jnp.sum(jnp.where(sub == 2 * turn + 1, picked, 0.0), axis=0, keepdims=True)
-    result[0:1, :] = best
-    result[1:2, :] = jnp.log1p(mass)
+    best_out[...] = jnp.sum(jnp.where(line == 2 * turn, picked, 0.0), axis=0, keepdims=True)
+    mass = jnp.sum(jnp.where(line == 2 * turn + 1, picked, 0.0), axis=0, keepdims=True)
+    mass_out[...] = jnp.log1p(mass)
 
 
 def call(kernel, out_shape, scratch=(), flops=0, name=None):
@@ -290,7 +302,7 @@
     arrived = lax.all_to_all(spread, AXES, split_axis=0, concat_axis=0, tiled=True)
     b0, over = call(
         pack_kernel,
-        (shape((SENT, WIDE), bf16), shape((8, 128), i32)),
+        (shape((BLOCK, FEAT), bf16), shape((8, 128), i32)),
         flops=3_000_000_000,
         name="pack",
     )(arrived)
@@ -299,31 +311,38 @@
     b1 = from_spot(b0, 1, 0)
     b4 = from_spot(b1, 1, 0)
     b5 = from_spot(b2, 0, 1)
-    state = (
-        pltpu.VMEM((6, 8, BLOCK), f32),
-        pltpu.VMEM((6, 8, BLOCK), f32),
-        pltpu.VMEM((2, BLOCK, 128), f32),
-        pltpu.VMEM((2, BLOCK, 128), f32),
-    )
+
+    def state(places):
+        return (
+            pltpu.VMEM((6, 8, BLOCK), f32),
+            pltpu.VMEM((6, 8, BLOCK), f32),
+            pltpu.VMEM((2, BLOCK, 128), f32),
+            pltpu.VMEM((2, BLOCK, 128), f32),
+            pltpu.VMEM((places, BLOCK, 128), f32),
+        )
+
     best, mass = call(
         early_kernel,
         (shape((8, BLOCK), f32), shape((8, BLOCK), f32)),
-        scratch=state,
+        scratch=state(4),
         flops=6_000_000_000,
         name="early",
     )(b0, b1, b2, b3)
     message = call(
         late_kernel,
         shape((DEVICES, 128), f32),
-        scratch=state,
+        scratch=state(3),
         flops=4_000_000_000,
         name="late",
     )(b0, b1, b2, b3, b4, b5, best, mass)
     answer = lax.all_to_all(message, AXES, split_axis=0, concat_axis=0, tiled=True)
-    result = call(
-        finish_kernel, shape((2, ROWS), f32), flops=ROWS * ROWS * 128, name="finish"
+    best, mass = call(
+        finish_kernel,
+        (shape((1, ROWS), f32), shape((1, ROWS), f32)),
+        flops=ROWS * ROWS * 128,
+        name="finish",
     )(answer, places)
-    return (result[0], result[1]), jnp.max(over)
+    return (best.reshape(ROWS), mass.reshape(ROWS)), jnp.max(over)
 
 
 def general(embeddings, labels, cluster_slot):

time: 124 us -> 114 us (0.919)
  Pallas kernels: 31.3 us -> 26.6 us
  waiting for transfers between devices: 33.5 us -> 28.9 us
    ppermute x5, waiting for transfers between devices: 25.1 us -> 20.6 us  [from_spot(): return lax.ppermute(x, AXES, hop(dy, dz))]
    pallas_call x3, Pallas kernels: 17 us -> 14 us  [the longest x1 7.72 us: fast(): call(late_kernel, shape((DEVICES, 128), f32), scratch=state(3), flops=400...]
    pallas_call x1, Pallas kernels: 10.2 us -> 8.57 us  [fast(): call(early_kernel, (shape((8, BLOCK), f32), shape((8, BLOCK), f32)), scra...]
where the time goes in v4:
time: 114 us; the launch traced here: 113 us
  blocking collectives  38.4 us (34%)
  waiting for transfers between devices  28.9 us (25%)
  Pallas kernels  26.6 us (23%)
  starting transfers between devices  14.7 us (13%)
  local copies, waits for them, and re-layouts  2.87 us (3%)
  between operations  1.32 us (1%)
    all_to_all x1, blocking collectives, fast(): lax.all_to_all(spread, AXES, split_axis=0, concat_axis=0, tiled=True)  38.4 us
    ppermute x5, waiting for transfers between devices, from_spot(): return lax.ppermute(x, AXES, hop(dy, dz))  20.6 us
    all_to_all x1, starting transfers between devices, fast(): lax.all_to_all(message, AXES, split_axis=0, concat_axis=0, tiled=True)  9.44 us
    pallas_call x1, Pallas kernels, fast(): call(early_kernel, (shape((8, BLOCK), f32), shape((8, BLOCK), f32)), scra...  8.57 us
    all_to_all x1, waiting for transfers between devices, fast(): lax.all_to_all(message, AXES, split_axis=0, concat_axis=0, tiled=True)  8.29 us
    pallas_call x1, Pallas kernels, fast(): call(late_kernel, shape((DEVICES, 128), f32), scratch=state(3), flops=400...  7.72 us
    ppermute x5, starting transfers between devices, from_spot(): return lax.ppermute(x, AXES, hop(dy, dz))  5.29 us
    pallas_call x1, Pallas kernels, fast(): call(pack_kernel, (shape((BLOCK, FEAT), bf16), shape((8, 128), i32)), flo...  4.38 us
  transfers between devices with their start and end apart: 6, of which 4 were waited for; matrix products, arithmetic and copies ran while one was open for 1% of the time, Pallas kernels for 8%

profile of v4, /device:TPU:1, one launch (start us, length us, event | category | flops | bytes accessed | tf_op | source)
XLA Modules:
  0.0 113.4 jit_solution(1025649353435247017)
XLA Ops:
  0.6 4.1 %prelude.1 = (bf16[1024,896]{1,0:T(8,128)(2,1)}, s32[8,512]{1,0:T(8,128)}) custom-call(s32[1,512]{1,0:T(1,128)} %bitcast.74, s32[1,512]{1,0:T(1,128)} %bitcast.59, bf16[512,768]{1,0:T(8,128)(2,1)} %rows.1), custom_call_target="tpu_custom_call" | custom-call | flops 3000000000 | bytes 8000000 | tf_op jit(solution)/shard_map/prelude/pallas_call | solution.py:296
  4.7 38.4 %all_to_all.59 = bf16[128,8,896]{2,1,0:T(8,128)(2,1)} all-to-all(bf16[128,8,896]{2,1,0:T(8,128)(2,1)} %bitcast.63), channel_id=1, replica_groups=mesh['grp'=8,'blk'=16] {'grp','blk'}, dimensions={0} | all-to-all | bytes 3670016 | tf_op jit(solution)/shard_map/all_to_all | solution.py:302
  43.1 4.4 %pack.1 = (bf16[640,768]{1,0:T(8,128)(2,1)}, s32[8,128]{1,0:T(8,128)}) custom-call(bf16[1024,896]{1,0:T(8,128)(2,1)} %bitcast.62), custom_call_target="tpu_custom_call" | custom-call | flops 3000000000 | bytes 8000000 | tf_op jit(solution)/shard_map/pack/pallas_call | solution.py:303
  47.4 0.7 collective-permute-start.3
  48.2 0.8 collective-permute-start.2
  49.0 2.1 %collective-permute-start.4 = (bf16[640,768]{1,0:T(8,128)(2,1)}, bf16[640,768]{1,0:T(8,128)(2,1)S(1)}, u32[]{:S(2)}, u32[]{:S(2)}) collective-permute-start(bf16[640,768]{1,0:T(8,128)(2,1)} %get-tuple-element.272.b0), channel_id=1, source_target_pairs={{3,0},{0,1},{1,2},{2,3},{7,4},{4,5},{5,6},{6,7},{11,8},{8,9},{9,10... | collective-permute-start | bytes 2949128 | tf_op jit(solution)/shard_map/ppermute | solution.py:290
  51.1 17.3 %collective-permute-done.3.b2 = bf16[640,768]{1,0:T(8,128)(2,1)S(1)} collective-permute-done((bf16[640,768]{1,0:T(8,128)(2,1)}, bf16[640,768]{1,0:T(8,128)(2,1)S(1)}, u32[]{:S(2)}, u32[]{:S(2)}) %collective-permute-start.3) | collective-permute-done | bytes 983072 | tf_op jit(solution)/shard_map/ppermute | solution.py:290
  68.4 0.1 collective-permute-start.6
  68.5 0.0 collective-permute-done.2.b1
  68.6 1.5 %collective-permute-start.5 = (bf16[640,768]{1,0:T(8,128)(2,1)S(1)}, bf16[640,768]{1,0:T(8,128)(2,1)S(1)}, u32[]{:S(2)}, u32[]{:S(2)}) collective-permute-start(bf16[640,768]{1,0:T(8,128)(2,1)S(1)} %collective-permute-done.2.b1), channel_id=1, source_target_pairs={{4,0},{5,1},{6,2},{7,3},{8,4},{9,5},{10,6},{11,7},{12,8},{13,9},{1... | collective-permute-start | bytes 2949128 | tf_op jit(solution)/shard_map/ppermute | solution.py:290
  70.0 2.6 %collective-permute-done.4.b3 = bf16[640,768]{1,0:T(8,128)(2,1)S(1)} collective-permute-done((bf16[640,768]{1,0:T(8,128)(2,1)}, bf16[640,768]{1,0:T(8,128)(2,1)S(1)}, u32[]{:S(2)}, u32[]{:S(2)}) %collective-permute-start.4) | collective-permute-done | bytes 983072 | tf_op jit(solution)/shard_map/ppermute | solution.py:290
  72.7 0.0 copy-done.5
  72.7 1.0 copy-done.7
  73.6 8.6 %early.1 = (f32[8,640]{1,0:T(8,128)}, f32[8,640]{1,0:T(8,128)}) custom-call(bf16[640,768]{1,0:T(8,128)(2,1)} %get-tuple-element.272.b0, bf16[640,768]{1,0:T(8,128)(2,1)} %copy-done.6, bf16[640,768]{1,0:T(8,128)(2,1)} %copy-done.5, bf16[640,768]{1,0:T(8,128)(2,1)} %copy-done.7), custom_call_target="tpu_custom_call" | custom-call | flops 6000000000 | bytes 8000000 | tf_op jit(solution)/shard_map/early/pallas_call | solution.py:324
  82.2 0.7 collective-permute-done.6.b5
  82.9 0.0 collective-permute-done.5.b4
  82.9 1.0 copy-done.8
  83.9 0.3 copy-done.9
  84.2 7.7 %late.1 = f32[128,128]{1,0:T(8,128)} custom-call(bf16[640,768]{1,0:T(8,128)(2,1)} %get-tuple-element.272.b0, bf16[640,768]{1,0:T(8,128)(2,1)} %copy-done.6, bf16[640,768]{1,0:T(8,128)(2,1)} %copy-done.5, bf16[640,768]{1,0:T(8,128)(2,1)} %copy-done.7, bf16[640,768]{1,0:T(8,128)(2,1)} %copy-done.9, bf16[640,768]{1,0:T(8,128)(2,1)} %copy-done.8, ...), custom_call_target="tpu_custom_call" | custom-call | flops 4000000000 | bytes 8000000 | tf_op jit(solution)/shard_map/late/pallas_call | solution.py:331
  91.9 9.4 %all-to-all-start.5 = ((f32[128,1,128]{2,1,0:T(1,128)}), f32[128,1,128]{2,1,0:T(1,128)S(1)}, u32[]{:S(2)}, u32[]{:S(2)}) async-start(f32[128,1,128]{2,1,0:T(1,128)} %bitcast.66), calls=%async_computation.5 | async-start | bytes 131072 | tf_op jit(solution)/shard_map/all_to_all | solution.py:338
  101.4 0.6 reduce_max.25
  102.6 8.3 %all-to-all-done.5 = f32[128,1,128]{2,1,0:T(1,128)S(1)} async-done(((f32[128,1,128]{2,1,0:T(1,128)}), f32[128,1,128]{2,1,0:T(1,128)S(1)}, u32[]{:S(2)}, u32[]{:S(2)}) %all-to-all-start.5) | async-done | bytes 65568 | tf_op jit(solution)/shard_map/all_to_all | solution.py:338
  110.9 0.6 copy-done.2
  111.6 1.9 %finish.1 = (f32[1,512]{1,0:T(1,128)}, f32[1,512]{1,0:T(1,128)}) custom-call(f32[128,128]{1,0:T(8,128)} %bitcast.65, s32[8,512]{1,0:T(8,128)} %get-tuple-element.275.places), custom_call_target="tpu_custom_call" | custom-call | flops 33554432 | bytes 8000000 | tf_op jit(solution)/shard_map/finish/pallas_call | solution.py:339
  (16 shorter events, 0.0 us)
Async XLA Ops:
  47.4 21.0 %collective-permute-start.3 = (bf16[640,768]{1,0:T(8,128)(2,1)}, bf16[640,768]{1,0:T(8,128)(2,1)S(1)}, u32[]{:S(2)}, u32[]{:S(2)}) collective-permute-start(bf16[640,768]{1,0:T(8,128)(2,1)} %get-tuple-element.272.b0), channel_id=1, source_target_pairs={{1,0},{2,1},{3,2},{0,3},{5,4},{6,5},{7,6},{4,7},{9,8},{10,9},{11,1... | collective-permute-start | bytes 2949128 | tf_op jit(solution)/shard_map/ppermute | solution.py:290
  48.2 20.4 %collective-permute-start.2 = (bf16[640,768]{1,0:T(8,128)(2,1)}, bf16[640,768]{1,0:T(8,128)(2,1)S(1)}, u32[]{:S(2)}, u32[]{:S(2)}) collective-permute-start(bf16[640,768]{1,0:T(8,128)(2,1)} %get-tuple-element.272.b0), channel_id=1, source_target_pairs={{4,0},{5,1},{6,2},{7,3},{8,4},{9,5},{10,6},{11,7},{12,8},{13,9},{1... | collective-permute-start | bytes 2949128 | tf_op jit(solution)/shard_map/ppermute | solution.py:290
  49.0 23.7 %collective-permute-start.4 = (bf16[640,768]{1,0:T(8,128)(2,1)}, bf16[640,768]{1,0:T(8,128)(2,1)S(1)}, u32[]{:S(2)}, u32[]{:S(2)}) collective-permute-start(bf16[640,768]{1,0:T(8,128)(2,1)} %get-tuple-element.272.b0), channel_id=1, source_target_pairs={{3,0},{0,1},{1,2},{2,3},{7,4},{4,5},{5,6},{6,7},{11,8},{8,9},{9,10... | collective-permute-start | bytes 2949128 | tf_op jit(solution)/shard_map/ppermute | solution.py:290
  68.4 4.3 %copy-start.5 = (bf16[640,768]{1,0:T(8,128)(2,1)}, bf16[640,768]{1,0:T(8,128)(2,1)S(1)}, u32[]{:S(2)}) copy-start(bf16[640,768]{1,0:T(8,128)(2,1)S(1)} %collective-permute-done.3.b2) | copy-start | bytes 2949124
  68.4 14.5 %collective-permute-start.6 = (bf16[640,768]{1,0:T(8,128)(2,1)S(1)}, bf16[640,768]{1,0:T(8,128)(2,1)S(1)}, u32[]{:S(2)}, u32[]{:S(2)}) collective-permute-start(bf16[640,768]{1,0:T(8,128)(2,1)S(1)} %collective-permute-done.3.b2), channel_id=1, source_target_pairs={{1,0},{2,1},{3,2},{0,3},{5,4},{6,5},{7,6},{4,7},{9,8},{10,9},{11,1... | collective-permute-start | bytes 2949128 | tf_op jit(solution)/shard_map/ppermute | solution.py:290
  68.6 4.1 %copy-start.6 = (bf16[640,768]{1,0:T(8,128)(2,1)}, bf16[640,768]{1,0:T(8,128)(2,1)S(1)}, u32[]{:S(2)}) copy-start(bf16[640,768]{1,0:T(8,128)(2,1)S(1)} %collective-permute-done.2.b1) | copy-start | bytes 2949124
  68.6 14.3 %collective-permute-start.5 = (bf16[640,768]{1,0:T(8,128)(2,1)S(1)}, bf16[640,768]{1,0:T(8,128)(2,1)S(1)}, u32[]{:S(2)}, u32[]{:S(2)}) collective-permute-start(bf16[640,768]{1,0:T(8,128)(2,1)S(1)} %collective-permute-done.2.b1), channel_id=1, source_target_pairs={{4,0},{5,1},{6,2},{7,3},{8,4},{9,5},{10,6},{11,7},{12,8},{13,9},{1... | collective-permute-start | bytes 2949128 | tf_op jit(solution)/shard_map/ppermute | solution.py:290
  72.7 1.0 copy-start.7
  82.9 1.0 copy-start.8
  82.9 1.3 %copy-start.9 = (bf16[640,768]{1,0:T(8,128)(2,1)}, bf16[640,768]{1,0:T(8,128)(2,1)S(1)}, u32[]{:S(2)}) copy-start(bf16[640,768]{1,0:T(8,128)(2,1)S(1)} %collective-permute-done.5.b4) | copy-start | bytes 2949124
  84.2 17.2 %copy-start.3 = (s32[8,128]{1,0:T(8,128)S(1)}, s32[8,128]{1,0:T(8,128)}, u32[]{:S(2)}) copy-start(s32[8,128]{1,0:T(8,128)} %get-tuple-element.271) | copy-start | bytes 12292
  84.2 27.4 %copy-start = (s32[512]{0:T(512)S(1)}, s32[512]{0:T(512)}, u32[]{:S(2)}) copy-start(s32[512]{0:T(512)} %param.9) | copy-start | bytes 6148
  84.2 27.4 %copy-start.1 = (bf16[512,768]{1,0:T(8,128)(2,1)S(1)}, bf16[512,768]{1,0:T(8,128)(2,1)}, u32[]{:S(2)}) copy-start(bf16[512,768]{1,0:T(8,128)(2,1)} %rows.1) | copy-start | bytes 2359300
  84.2 27.4 %copy-start.4 = (s32[512]{0:T(512)S(1)}, s32[512]{0:T(512)}, u32[]{:S(2)}) copy-start(s32[512]{0:T(512)} %param.8) | copy-start | bytes 6148
  91.9 19.0 %all-to-all-start.5 = ((f32[128,1,128]{2,1,0:T(1,128)}), f32[128,1,128]{2,1,0:T(1,128)S(1)}, u32[]{:S(2)}, u32[]{:S(2)}) async-start(f32[128,1,128]{2,1,0:T(1,128)} %bitcast.66), calls=%async_computation.5 | async-start | bytes 131072 | tf_op jit(solution)/shard_map/all_to_all | solution.py:338
  110.9 0.6 copy-start.2

commit v5 on v4

--- a/solution.py
+++ b/solution.py
@@ -21,7 +21,7 @@
 APART = -64.0
 LOG2E = 1.4426950408889634
 AXES = ("grp", "blk")
-VMEM_LIMIT = 56 * 1024 * 1024
+VMEM_LIMIT = 24 * 1024 * 1024
 
 SPOTS = ((0, 0), (1, 0), (0, 1), (0, 3), (2, 0), (0, 2))
 ROW_BLOCKS = (1, 2)
@@ -197,37 +197,44 @@
     return best, mass
 
 
+def store(blocks, best_out, mass_out, state):
+    best_out[...] = jnp.full_like(best_out, APART)
+    mass_out[...] = jnp.zeros_like(mass_out)
+    for e in blocks:
+        best_out[e : e + 1, :], mass_out[e : e + 1, :] = settle(e, state)
+
+
 def early_kernel(b0, b1, b2, b3, best_out, mass_out, *state):
     clear(state)
     for place, block in enumerate((b0, b1, b2, b3)):
         spell(block, place, state)
     square(b0, b0, 0, 0, None, state, True)
+    square(b2, b0, 2, 0, 1, state)
     square(b1, b0, 1, 0, 0, state)
-    square(b2, b0, 2, 0, 1, state)
+    square(b1, b2, 1, 2, 0, state)
     square(b1, b3, 1, 3, 0, state)
-    square(b1, b2, 1, 2, 0, state)
     square(b3, b2, 3, 2, None, state)
-    best_out[...] = jnp.full_like(best_out, APART)
-    mass_out[...] = jnp.zeros_like(mass_out)
-    for e in range(4):
-        best_out[e : e + 1, :], mass_out[e : e + 1, :] = settle(e, state)
+    store((0, 1, 2, 3), best_out, mass_out, state)
 
 
 def late_kernel(b0, b1, b2, b3, b4, b5, best_in, mass_in, out, *state):
     clear(state)
     for place, block in enumerate((b4, b1, b2)):
         spell(block, place, state)
+    square(b1, b5, 1, 5, 0, state)
     square(b4, b0, 0, 0, None, state)
     square(b4, b5, 0, 5, None, state)
-    square(b1, b5, 1, 5, 0, state)
     square(b2, b4, 2, 4, 1, state)
     source_at = (iota((DEVICES, BLOCK), 0) + 1).astype(jnp.float32)
     line = iota((16, BLOCK), 0)
     back = []
     for e, block in enumerate((b0, b1, b2, b3, b4, b5)):
-        best, mass = settle(e, state)
-        best = jnp.maximum(jnp.maximum(best, best_in[e : e + 1, :]), -1.0)
-        mass = mass + mass_in[e : e + 1, :]
+        here = slice(e, e + 1)
+        best, mass = jnp.maximum(best_in[here, :], -1.0), mass_in[here, :]
+        if e != 3:
+            more, extra = settle(e, state)
+            best = jnp.maximum(best, more)
+            mass = mass + extra
         names = names_of(block)
         values = jnp.where((line & 1) == 0, best, mass)
         values = jnp.where((line >> 1).astype(jnp.float32) == names[2:3], values, 0.0)
@@ -245,8 +252,8 @@
     best = mass = None
     pieces = split(arrived[...].T)
     for e, (dy, dz) in enumerate(SPOTS):
-        by = (ay + jnp.where(turned, dy, (-dy) & 3)) & 3
-        bz = (az + jnp.where(turned, dz, (-dz) & 3)) & 3
+        by = (ay + jnp.where(turned, dz, (-dy) & 3)) & 3
+        bz = (az + jnp.where(turned, dy, (-dz) & 3)) & 3
         move = (col == base * MEMBERS + by * 4 + bz).astype(jnp.bfloat16)
         part = jnp.concatenate(
             [pieces[128 * p + 16 * e : 128 * p + 16 * e + 16] for p in range(3)], axis=0
@@ -278,10 +285,10 @@
 def hop(dy, dz):
     pairs = []
     for g in range(GROUPS):
-        turn = -1 if g & 1 else 1
+        up, along = (-dz, -dy) if g & 1 else (dy, dz)
         for y in range(4):
             for z in range(4):
-                source = ((y + turn * dy) % 4) * 4 + (z + turn * dz) % 4
+                source = ((y + up) % 4) * 4 + (z + along) % 4
                 pairs.append((g * MEMBERS + source, g * MEMBERS + y * 4 + z))
     return pairs
 

time: 114 us -> 106 us (0.930)
  Pallas kernels: 26.6 us -> 17.1 us
  waiting for transfers between devices: 28.9 us -> 35.7 us
  local copies, waits for them, and re-layouts: 2.87 us -> 0.01 us
  starting transfers between devices: 14.7 us -> 13.1 us
    ppermute x5, waiting for transfers between devices: 20.6 us -> 27.4 us  [from_spot(): return lax.ppermute(x, AXES, hop(dy, dz))]
    unnamed x20 -> x6, local copies, waits for them, and re-layouts: 2.87 us -> 0.01 us
    pallas_call x1, Pallas kernels: 8.57 us -> 6.02 us  [fast(): call(early_kernel, (shape((8, BLOCK), f32), shape((8, BLOCK), f32)), scra...]
    pallas_call x1, Pallas kernels: 7.72 us -> 5.23 us  [fast(): call(late_kernel, shape((DEVICES, 128), f32), scratch=state(3), flops=400...]
    pallas_call x1, Pallas kernels: 4.38 us -> 1.99 us  [fast(): call(pack_kernel, (shape((BLOCK, FEAT), bf16), shape((8, 128), i32)), flo...]
    ppermute x5, starting transfers between devices: 5.29 us -> 3.48 us  [from_spot(): return lax.ppermute(x, AXES, hop(dy, dz))]
    pallas_call x1, Pallas kernels: 4.05 us -> 2.81 us  [fast(): call(prelude_kernel, (shape((HELD, WIDE), bf16), shape((8, ROWS), i32)),...]
  transfers between devices with their start and end apart: 6 -> 6, of which waited for: 4 -> 5; matrix products, arithmetic and copies ran while one was open for 1% -> 1% of each run, Pallas kernels for 8% -> 6%
where the time goes in v5:
time: 106 us
  blocking collectives  38.1 us (36%)
  waiting for transfers between devices  35.7 us (34%)
  Pallas kernels  17.1 us (16%)
  starting transfers between devices  13.1 us (12%)
  between operations  1.33 us (1%)
    all_to_all x1, blocking collectives, fast(): lax.all_to_all(spread, AXES, split_axis=0, concat_axis=0, tiled=True)  38.1 us
    ppermute x5, waiting for transfers between devices, from_spot(): return lax.ppermute(x, AXES, hop(dy, dz))  27.4 us
    all_to_all x1, starting transfers between devices, fast(): lax.all_to_all(message, AXES, split_axis=0, concat_axis=0, tiled=True)  9.59 us
    all_to_all x1, waiting for transfers between devices, fast(): lax.all_to_all(message, AXES, split_axis=0, concat_axis=0, tiled=True)  8.29 us
    pallas_call x1, Pallas kernels, fast(): call(early_kernel, (shape((8, BLOCK), f32), shape((8, BLOCK), f32)), scra...  6.02 us
    pallas_call x1, Pallas kernels, fast(): call(late_kernel, shape((DEVICES, 128), f32), scratch=state(3), flops=400...  5.23 us
    ppermute x5, starting transfers between devices, from_spot(): return lax.ppermute(x, AXES, hop(dy, dz))  3.48 us
    pallas_call x1, Pallas kernels, fast(): call(prelude_kernel, (shape((HELD, WIDE), bf16), shape((8, ROWS), i32)),...  2.81 us
  transfers between devices with their start and end apart: 6, of which 5 were waited for; matrix products, arithmetic and copies ran while one was open for 1% of the time, Pallas kernels for 6%

profile of v5, /device:TPU:1, one launch (start us, length us, event | category | flops | bytes accessed | tf_op | source)
XLA Modules:
  0.0 105.9 jit_solution(3581836113294356633)
XLA Ops:
  0.6 2.8 %prelude.1 = (bf16[1024,896]{1,0:T(8,128)(2,1)S(1)}, s32[8,512]{1,0:T(8,128)S(1)}) custom-call(s32[1,512]{1,0:T(1,128)} %bitcast.73, s32[1,512]{1,0:T(1,128)} %bitcast.62, bf16[512,768]{1,0:T(8,128)(2,1)} %rows.1), custom_call_target="tpu_custom_call" | custom-call | flops 3000000000 | bytes 8000000 | tf_op jit(solution)/shard_map/prelude/pallas_call | solution.py:303
  3.4 38.1 %all_to_all.59 = bf16[128,8,896]{2,1,0:T(8,128)(2,1)S(1)} all-to-all(bf16[128,8,896]{2,1,0:T(8,128)(2,1)S(1)} %bitcast.60), channel_id=1, replica_groups=mesh['grp'=8,'blk'=16] {'grp','blk'}, dimensions={0} | all-to-all | bytes 3670016 | tf_op jit(solution)/shard_map/all_to_all | solution.py:309
  41.5 2.0 %pack.1 = (bf16[640,768]{1,0:T(8,128)(2,1)S(1)}, s32[8,128]{1,0:T(8,128)S(1)}) custom-call(bf16[1024,896]{1,0:T(8,128)(2,1)S(1)} %bitcast.59), custom_call_target="tpu_custom_call" | custom-call | flops 3000000000 | bytes 8000000 | tf_op jit(solution)/shard_map/pack/pallas_call | solution.py:310
  43.5 1.1 collective-permute-start.3
  44.6 0.6 collective-permute-start.2
  45.1 1.9 %collective-permute-start.4 = (bf16[640,768]{1,0:T(8,128)(2,1)S(1)}, bf16[640,768]{1,0:T(8,128)(2,1)S(1)}, u32[]{:S(2)}, u32[]{:S(2)}) collective-permute-start(bf16[640,768]{1,0:T(8,128)(2,1)S(1)} %get-tuple-element.272.b0), channel_id=1, source_target_pairs={{3,0},{0,1},{1,2},{2,3},{7,4},{4,5},{5,6},{6,7},{11,8},{8,9},{9,10... | collective-permute-start | bytes 2949128 | tf_op jit(solution)/shard_map/ppermute | solution.py:297
  47.0 11.0 %collective-permute-done.3.b2 = bf16[640,768]{1,0:T(8,128)(2,1)S(1)} collective-permute-done((bf16[640,768]{1,0:T(8,128)(2,1)S(1)}, bf16[640,768]{1,0:T(8,128)(2,1)S(1)}, u32[]{:S(2)}, u32[]{:S(2)}) %collective-permute-start.3) | collective-permute-done | bytes 983072 | tf_op jit(solution)/shard_map/ppermute | solution.py:297
  58.0 0.0 collective-permute-start.6
  58.0 8.3 %collective-permute-done.2.b1 = bf16[640,768]{1,0:T(8,128)(2,1)S(1)} collective-permute-done((bf16[640,768]{1,0:T(8,128)(2,1)S(1)}, bf16[640,768]{1,0:T(8,128)(2,1)S(1)}, u32[]{:S(2)}, u32[]{:S(2)}) %collective-permute-start.2) | collective-permute-done | bytes 983072 | tf_op jit(solution)/shard_map/ppermute | solution.py:297
  66.3 0.0 collective-permute-start.5
  66.3 1.8 %collective-permute-done.4.b3 = bf16[640,768]{1,0:T(8,128)(2,1)S(1)} collective-permute-done((bf16[640,768]{1,0:T(8,128)(2,1)S(1)}, bf16[640,768]{1,0:T(8,128)(2,1)S(1)}, u32[]{:S(2)}, u32[]{:S(2)}) %collective-permute-start.4) | collective-permute-done | bytes 983072 | tf_op jit(solution)/shard_map/ppermute | solution.py:297
  68.2 6.0 %early.1 = (f32[8,640]{1,0:T(8,128)S(1)}, f32[8,640]{1,0:T(8,128)S(1)}) custom-call(bf16[640,768]{1,0:T(8,128)(2,1)S(1)} %get-tuple-element.272.b0, bf16[640,768]{1,0:T(8,128)(2,1)S(1)} %collective-permute-done.2.b1, bf16[640,768]{1,0:T(8,128)(2,1)S(1)} %collective-permute-done.3.b2, bf16[640,768]{1,0:T(8,128)(2,1)S(1)} %collective-permute-done.4.b3), custom_call_target="tpu_custom_call" | custom-call | flops 6000000000 | bytes 8000000 | tf_op jit(solution)/shard_map/early/pallas_call | solution.py:331
  74.2 0.0 collective-permute-done.6.b5
  74.2 6.3 %collective-permute-done.5.b4 = bf16[640,768]{1,0:T(8,128)(2,1)S(1)} collective-permute-done((bf16[640,768]{1,0:T(8,128)(2,1)S(1)}, bf16[640,768]{1,0:T(8,128)(2,1)S(1)}, u32[]{:S(2)}, u32[]{:S(2)}) %collective-permute-start.5) | collective-permute-done | bytes 983072 | tf_op jit(solution)/shard_map/ppermute | solution.py:297
  80.5 0.0 copy-start
  80.5 0.0 copy-start.1
  80.5 5.2 %late.1 = f32[128,128]{1,0:T(8,128)} custom-call(bf16[640,768]{1,0:T(8,128)(2,1)S(1)} %get-tuple-element.272.b0, bf16[640,768]{1,0:T(8,128)(2,1)S(1)} %collective-permute-done.2.b1, bf16[640,768]{1,0:T(8,128)(2,1)S(1)} %collective-permute-done.3.b2, bf16[640,768]{1,0:T(8,128)(2,1)S(1)} %collective-permute-done.4.b3, ...), custom_call_target="tpu_custom_call" | custom-call | flops 4000000000 | bytes 8000000 | tf_op jit(solution)/shard_map/late/pallas_call | solution.py:338
  85.7 9.6 %all-to-all-start.5 = ((f32[128,1,128]{2,1,0:T(1,128)}), f32[128,1,128]{2,1,0:T(1,128)S(1)}, u32[]{:S(2)}, u32[]{:S(2)}) async-start(f32[128,1,128]{2,1,0:T(1,128)} %bitcast.24), calls=%async_computation.5 | async-start | bytes 131072 | tf_op jit(solution)/shard_map/all_to_all | solution.py:345
  95.3 0.6 reduce_max.25
  96.6 8.3 %all-to-all-done.5 = f32[128,1,128]{2,1,0:T(1,128)S(1)} async-done(((f32[128,1,128]{2,1,0:T(1,128)}), f32[128,1,128]{2,1,0:T(1,128)S(1)}, u32[]{:S(2)}, u32[]{:S(2)}) %all-to-all-start.5) | async-done | bytes 65568 | tf_op jit(solution)/shard_map/all_to_all | solution.py:345
  104.9 0.0 copy-done
  104.9 0.0 copy-done.1
  104.9 0.0 copy-done.2
  104.9 1.0 finish.1
  (2 shorter events, 0.0 us)
Async XLA Ops:
  43.5 14.5 %collective-permute-start.3 = (bf16[640,768]{1,0:T(8,128)(2,1)S(1)}, bf16[640,768]{1,0:T(8,128)(2,1)S(1)}, u32[]{:S(2)}, u32[]{:S(2)}) collective-permute-start(bf16[640,768]{1,0:T(8,128)(2,1)S(1)} %get-tuple-element.272.b0), channel_id=1, source_target_pairs={{1,0},{2,1},{3,2},{0,3},{5,4},{6,5},{7,6},{4,7},{9,8},{10,9},{11,1... | collective-permute-start | bytes 2949128 | tf_op jit(solution)/shard_map/ppermute | solution.py:297
  44.6 21.7 %collective-permute-start.2 = (bf16[640,768]{1,0:T(8,128)(2,1)S(1)}, bf16[640,768]{1,0:T(8,128)(2,1)S(1)}, u32[]{:S(2)}, u32[]{:S(2)}) collective-permute-start(bf16[640,768]{1,0:T(8,128)(2,1)S(1)} %get-tuple-element.272.b0), channel_id=1, source_target_pairs={{4,0},{5,1},{6,2},{7,3},{8,4},{9,5},{10,6},{11,7},{12,8},{13,9},{1... | collective-permute-start | bytes 2949128 | tf_op jit(solution)/shard_map/ppermute | solution.py:297
  45.1 23.0 %collective-permute-start.4 = (bf16[640,768]{1,0:T(8,128)(2,1)S(1)}, bf16[640,768]{1,0:T(8,128)(2,1)S(1)}, u32[]{:S(2)}, u32[]{:S(2)}) collective-permute-start(bf16[640,768]{1,0:T(8,128)(2,1)S(1)} %get-tuple-element.272.b0), channel_id=1, source_target_pairs={{3,0},{0,1},{1,2},{2,3},{7,4},{4,5},{5,6},{6,7},{11,8},{8,9},{9,10... | collective-permute-start | bytes 2949128 | tf_op jit(solution)/shard_map/ppermute | solution.py:297
  58.0 16.2 %collective-permute-start.6 = (bf16[640,768]{1,0:T(8,128)(2,1)S(1)}, bf16[640,768]{1,0:T(8,128)(2,1)S(1)}, u32[]{:S(2)}, u32[]{:S(2)}) collective-permute-start(bf16[640,768]{1,0:T(8,128)(2,1)S(1)} %collective-permute-done.3.b2), channel_id=1, source_target_pairs={{1,0},{2,1},{3,2},{0,3},{5,4},{6,5},{7,6},{4,7},{9,8},{10,9},{11,1... | collective-permute-start | bytes 2949128 | tf_op jit(solution)/shard_map/ppermute | solution.py:297
  66.3 14.2 %collective-permute-start.5 = (bf16[640,768]{1,0:T(8,128)(2,1)S(1)}, bf16[640,768]{1,0:T(8,128)(2,1)S(1)}, u32[]{:S(2)}, u32[]{:S(2)}) collective-permute-start(bf16[640,768]{1,0:T(8,128)(2,1)S(1)} %collective-permute-done.2.b1), channel_id=1, source_target_pairs={{4,0},{5,1},{6,2},{7,3},{8,4},{9,5},{10,6},{11,7},{12,8},{13,9},{1... | collective-permute-start | bytes 2949128 | tf_op jit(solution)/shard_map/ppermute | solution.py:297
  80.5 24.4 %copy-start = (s32[512]{0:T(512)S(1)}, s32[512]{0:T(512)}, u32[]{:S(2)}) copy-start(s32[512]{0:T(512)} %param.9) | copy-start | bytes 6148
  80.5 24.4 %copy-start.1 = (bf16[512,768]{1,0:T(8,128)(2,1)S(1)}, bf16[512,768]{1,0:T(8,128)(2,1)}, u32[]{:S(2)}) copy-start(bf16[512,768]{1,0:T(8,128)(2,1)} %rows.1) | copy-start | bytes 2359300
  80.5 24.4 %copy-start.2 = (s32[512]{0:T(512)S(1)}, s32[512]{0:T(512)}, u32[]{:S(2)}) copy-start(s32[512]{0:T(512)} %param.8) | copy-start | bytes 6148
  85.7 19.2 %all-to-all-start.5 = ((f32[128,1,128]{2,1,0:T(1,128)}), f32[128,1,128]{2,1,0:T(1,128)S(1)}, u32[]{:S(2)}, u32[]{:S(2)}) async-start(f32[128,1,128]{2,1,0:T(1,128)} %bitcast.24), calls=%async_computation.5 | async-start | bytes 131072 | tf_op jit(solution)/shard_map/all_to_all | solution.py:345

commit v6 on v5

--- a/solution.py
+++ b/solution.py
@@ -23,8 +23,12 @@
 AXES = ("grp", "blk")
 VMEM_LIMIT = 24 * 1024 * 1024
 
-SPOTS = ((0, 0), (1, 0), (0, 1), (0, 3), (2, 0), (0, 2))
+SPOTS = ((0, 0), (1, 0), (0, 1), (2, 0), (0, 2), (0, 3), (3, 0))
+LOW = 256
+LOW_SENT = LOW + 16
+HIGH_SENT = BLOCK - LOW
 ROW_BLOCKS = (1, 2)
+SHIFT = 2.0
 
 
 def iota(shape, axis):
@@ -91,7 +95,7 @@
         spread[here, FEAT:] = (matmul(pick, marks, NT) + totals).astype(jnp.bfloat16)
 
 
-def pack_kernel(arrived, packed, over):
+def pack_kernel(arrived, packed, low, high, over):
     tails = arrived[:, FEAT:]
     one = ((iota((128, HELD), 0) * SHARE) == iota((128, HELD), 1)).astype(jnp.bfloat16)
     counts = matmul(one, tails, NN).astype(jnp.int32)
@@ -115,7 +119,11 @@
     packed[:ROOM, :] = matmul(pick[:ROOM], arrived[:, :FEAT], NN).astype(jnp.bfloat16)
     named = matmul(names, pick, NT)
     named = jnp.concatenate([named, jnp.zeros((8, FEAT - BLOCK), jnp.float32)], axis=1)
-    packed[ROOM:, :] = jnp.concatenate([named, jnp.zeros_like(named)], axis=0).astype(jnp.bfloat16)
+    named = jnp.concatenate([named, jnp.zeros_like(named)], axis=0).astype(jnp.bfloat16)
+    packed[ROOM:, :] = named
+    low[:LOW, :] = packed[:LOW, :]
+    low[LOW:, :] = named
+    high[...] = packed[LOW:, :]
 
 
 def column_fold(x, op):
@@ -132,7 +140,9 @@
     return total
 
 
-PARTS = ((0, 256), (256, 256), (512, 128))
+LOWS = ((0, 256),)
+HIGHS = ((256, 256), (512, 128))
+PARTS = LOWS + HIGHS
 
 
 def clear(state):
@@ -144,7 +154,7 @@
 
 
 def names_of(block):
-    return block[ROOM:, :BLOCK].astype(jnp.float32)
+    return block[block.shape[0] - 16 :, :BLOCK].astype(jnp.float32)
 
 
 def spell(block, place, state):
@@ -155,12 +165,12 @@
         state[4][place, here, :] = jnp.broadcast_to(clusters[:, here], (128, 128)).T
 
 
-def square(rows, cols, place, c, r, state, own=False):
+def square(rows, cols, place, c, r, state, own=False, downs=PARTS, parts=PARTS, first=0):
     col_best, col_mass, row_best, row_mass, spelt = state
     clusters = names_of(cols)[0:1]
-    for i, tall in PARTS:
-        for j, wide in PARTS:
-            product = matmul(rows[i : i + tall, :], cols[j : j + wide, :], NT)
+    for i, tall in downs:
+        for j, wide in parts:
+            product = matmul(rows[i : i + tall, :], cols[j - first : j - first + wide, :], NT)
             down = slice(i, i + tall)
             mine = spelt[place, down, :]
             tops = sums = None
@@ -204,38 +214,48 @@
         best_out[e : e + 1, :], mass_out[e : e + 1, :] = settle(e, state)
 
 
-def early_kernel(b0, b1, b2, b3, best_out, mass_out, *state):
+def early_kernel(b0, b1, b2, low, high, best_out, mass_out, *state):
     clear(state)
-    for place, block in enumerate((b0, b1, b2, b3)):
+    for place, block in enumerate((b0, b1, b2)):
         spell(block, place, state)
     square(b0, b0, 0, 0, None, state, True)
-    square(b2, b0, 2, 0, 1, state)
     square(b1, b0, 1, 0, 0, state)
     square(b1, b2, 1, 2, 0, state)
-    square(b1, b3, 1, 3, 0, state)
-    square(b3, b2, 3, 2, None, state)
-    store((0, 1, 2, 3), best_out, mass_out, state)
-
-
-def late_kernel(b0, b1, b2, b3, b4, b5, best_in, mass_in, out, *state):
+    square(b1, low, 1, 5, 0, state, parts=LOWS)
+    square(b2, b0, 2, 0, 1, state)
+    square(b2, high, 2, 6, 1, state, parts=HIGHS, first=LOW)
+    square(b1, high, 1, 6, 0, state, downs=LOWS, parts=HIGHS, first=LOW)
+    square(b1, high, 1, 6, None, state, downs=HIGHS, parts=HIGHS, first=LOW)
+    square(b2, low, 2, 5, 1, state, downs=HIGHS, parts=LOWS)
+    square(b2, low, 2, 5, None, state, downs=LOWS, parts=LOWS)
+    store((0, 1, 2, 5, 6), best_out, mass_out, state)
+
+
+def late_kernel(b0, b1, b2, b3, b4, low, high, best_in, mass_in, out, *state):
     clear(state)
-    for place, block in enumerate((b4, b1, b2)):
+    for place, block in enumerate((b0, b1, b2, b4)):
         spell(block, place, state)
-    square(b1, b5, 1, 5, 0, state)
-    square(b4, b0, 0, 0, None, state)
-    square(b4, b5, 0, 5, None, state)
-    square(b2, b4, 2, 4, 1, state)
+    square(b0, b3, 0, 3, None, state, downs=LOWS, parts=LOWS)
+    square(b0, b4, 0, 4, None, state, downs=HIGHS, parts=HIGHS)
+    square(b1, b4, 1, 4, 0, state)
+    square(b2, b3, 2, 3, 1, state)
+    square(b4, b3, 3, 3, None, state)
     source_at = (iota((DEVICES, BLOCK), 0) + 1).astype(jnp.float32)
     line = iota((16, BLOCK), 0)
     back = []
-    for e, block in enumerate((b0, b1, b2, b3, b4, b5)):
+    for e, block in enumerate((b0, b1, b2, b3, b4, low, high)):
         here = slice(e, e + 1)
         best, mass = jnp.maximum(best_in[here, :], -1.0), mass_in[here, :]
-        if e != 3:
+        if e in (1, 2, 3, 4):
             more, extra = settle(e, state)
             best = jnp.maximum(best, more)
             mass = mass + extra
+        best = best + SHIFT
         names = names_of(block)
+        if e == 5:
+            names = jnp.where(iota(names.shape, 1) < LOW, names, 0.0)
+        if e == 6:
+            names = jnp.where(iota(names.shape, 1) >= LOW, names, 0.0)
         values = jnp.where((line & 1) == 0, best, mass)
         values = jnp.where((line >> 1).astype(jnp.float32) == names[2:3], values, 0.0)
         to = (source_at == names[1:2]).astype(jnp.bfloat16)
@@ -266,7 +286,8 @@
     picked = joined(matmul(split(merged), holder, NN))
     line = iota((16, ROWS), 0)
     turn = places[1:2, :]
-    best_out[...] = jnp.sum(jnp.where(line == 2 * turn, picked, 0.0), axis=0, keepdims=True)
+    best = jnp.sum(jnp.where(line == 2 * turn, picked, 0.0), axis=0, keepdims=True)
+    best_out[...] = best - SHIFT
     mass = jnp.sum(jnp.where(line == 2 * turn + 1, picked, 0.0), axis=0, keepdims=True)
     mass_out[...] = jnp.log1p(mass)
 
@@ -307,22 +328,29 @@
         name="prelude",
     )(labels.reshape(1, ROWS), cluster_slot.reshape(1, ROWS), embeddings)
     arrived = lax.all_to_all(spread, AXES, split_axis=0, concat_axis=0, tiled=True)
-    b0, over = call(
+    b0, low, high, over = call(
         pack_kernel,
-        (shape((BLOCK, FEAT), bf16), shape((8, 128), i32)),
+        (
+            shape((BLOCK, FEAT), bf16),
+            shape((LOW_SENT, FEAT), bf16),
+            shape((HIGH_SENT, FEAT), bf16),
+            shape((8, 128), i32),
+        ),
         flops=3_000_000_000,
         name="pack",
     )(arrived)
+    b1 = from_spot(b0, 1, 0)
     b2 = from_spot(b0, 0, 1)
-    b3 = from_spot(b0, 0, 3)
-    b1 = from_spot(b0, 1, 0)
-    b4 = from_spot(b1, 1, 0)
-    b5 = from_spot(b2, 0, 1)
+    low = from_spot(low, 0, 3)
+    high = from_spot(high, 3, 0)
+    b1, b2, low, high = lax.optimization_barrier((b1, b2, low, high))
+    b3 = from_spot(b1, 1, 0)
+    b4 = from_spot(b2, 0, 1)
 
     def state(places):
         return (
-            pltpu.VMEM((6, 8, BLOCK), f32),
-            pltpu.VMEM((6, 8, BLOCK), f32),
+            pltpu.VMEM((7, 8, BLOCK), f32),
+            pltpu.VMEM((7, 8, BLOCK), f32),
             pltpu.VMEM((2, BLOCK, 128), f32),
             pltpu.VMEM((2, BLOCK, 128), f32),
             pltpu.VMEM((places, BLOCK, 128), f32),
@@ -331,17 +359,17 @@
     best, mass = call(
         early_kernel,
         (shape((8, BLOCK), f32), shape((8, BLOCK), f32)),
-        scratch=state(4),
+        scratch=state(3),
         flops=6_000_000_000,
         name="early",
-    )(b0, b1, b2, b3)
+    )(b0, b1, b2, low, high)
     message = call(
         late_kernel,
         shape((DEVICES, 128), f32),
-        scratch=state(3),
+        scratch=state(4),
         flops=4_000_000_000,
         name="late",
-    )(b0, b1, b2, b3, b4, b5, best, mass)
+    )(b0, b1, b2, b3, b4, low, high, best, mass)
     answer = lax.all_to_all(message, AXES, split_axis=0, concat_axis=0, tiled=True)
     best, mass = call(
         finish_kernel,

time: 106 us -> 102 us (0.962)
  waiting for transfers between devices: 35.7 us -> 32 us
    ppermute x5 -> x6, waiting for transfers between devices: 27.4 us -> 23.7 us  [from_spot(): return lax.ppermute(x, AXES, hop(dy, dz))]
    ppermute x5 -> x6, starting transfers between devices: 3.48 us -> 5.88 us  [from_spot(): return lax.ppermute(x, AXES, hop(dy, dz))]
    all_to_all x1, starting transfers between devices: 9.59 us -> 7.73 us  [fast(): lax.all_to_all(message, AXES, split_axis=0, concat_axis=0, tiled=True)]
  transfers between devices with their start and end apart: 6 -> 7, of which waited for: 5 -> 6; matrix products, arithmetic and copies ran while one was open for 1% -> 1% of each run, Pallas kernels for 6% -> 6%
where the time goes in v6:
time: 102 us
  blocking collectives  38.1 us (37%)
  waiting for transfers between devices  32 us (31%)
  Pallas kernels  16.3 us (16%)
  starting transfers between devices  13.6 us (13%)
  between operations  1.32 us (1%)
    all_to_all x1, blocking collectives, fast(): lax.all_to_all(spread, AXES, split_axis=0, concat_axis=0, tiled=True)  38.1 us
    ppermute x6, waiting for transfers between devices, from_spot(): return lax.ppermute(x, AXES, hop(dy, dz))  23.7 us
    all_to_all x1, waiting for transfers between devices, fast(): lax.all_to_all(message, AXES, split_axis=0, concat_axis=0, tiled=True)  8.29 us
    all_to_all x1, starting transfers between devices, fast(): lax.all_to_all(message, AXES, split_axis=0, concat_axis=0, tiled=True)  7.73 us
    pallas_call x1, Pallas kernels, fast(): call(early_kernel, (shape((8, BLOCK), f32), shape((8, BLOCK), f32)), scra...  5.89 us
    ppermute x6, starting transfers between devices, from_spot(): return lax.ppermute(x, AXES, hop(dy, dz))  5.88 us
    pallas_call x1, Pallas kernels, fast(): call(late_kernel, shape((DEVICES, 128), f32), scratch=state(4), flops=400...  4.51 us
    pallas_call x1, Pallas kernels, fast(): call(prelude_kernel, (shape((HELD, WIDE), bf16), shape((8, ROWS), i32)),...  2.81 us
  transfers between devices with their start and end apart: 7, of which 6 were waited for; matrix products, arithmetic and copies ran while one was open for 1% of the time, Pallas kernels for 6%

profile of v6, /device:TPU:1, one launch (start us, length us, event | category | flops | bytes accessed | tf_op | source)
XLA Modules:
  0.0 101.9 jit_solution(4286591473080384621)
XLA Ops:
  0.6 2.8 %prelude.1 = (bf16[1024,896]{1,0:T(8,128)(2,1)S(1)}, s32[8,512]{1,0:T(8,128)S(1)}) custom-call(s32[1,512]{1,0:T(1,128)} %bitcast.73, s32[1,512]{1,0:T(1,128)} %bitcast.62, bf16[512,768]{1,0:T(8,128)(2,1)} %rows.1), custom_call_target="tpu_custom_call" | custom-call | flops 3000000000 | bytes 8000000 | tf_op jit(solution)/shard_map/prelude/pallas_call | solution.py:324
  3.4 38.1 %all_to_all.59 = bf16[128,8,896]{2,1,0:T(8,128)(2,1)S(1)} all-to-all(bf16[128,8,896]{2,1,0:T(8,128)(2,1)S(1)} %bitcast.60), channel_id=1, replica_groups=mesh['grp'=8,'blk'=16] {'grp','blk'}, dimensions={0} | all-to-all | bytes 3670016 | tf_op jit(solution)/shard_map/all_to_all | solution.py:330
  41.5 2.0 %pack.1 = (bf16[640,768]{1,0:T(8,128)(2,1)S(1)}, bf16[272,768]{1,0:T(8,128)(2,1)S(1)}, bf16[384,768]{1,0:T(8,128)(2,1)S(1)}, s32[8,128]{1,0:T(8,128)S(1)}) custom-call(bf16[1024,896]{1,0:T(8,128)(2,1)S(1)} %bitcast.59), custom_call_target="tpu_custom_call" | custom-call | flops 3000000000 | bytes 8000000 | tf_op jit(solution)/shard_map/pack/pallas_call | solution.py:331
  43.5 1.1 %collective-permute-start.3 = (bf16[640,768]{1,0:T(8,128)(2,1)S(1)}, bf16[640,768]{1,0:T(8,128)(2,1)S(1)}, u32[]{:S(2)}, u32[]{:S(2)}) collective-permute-start(bf16[640,768]{1,0:T(8,128)(2,1)S(1)} %get-tuple-element.278.b0), channel_id=1, source_target_pairs={{1,0},{2,1},{3,2},{0,3},{5,4},{6,5},{7,6},{4,7},{9,8},{10,9},{11,1... | collective-permute-start | bytes 2949128 | tf_op jit(solution)/shard_map/ppermute | solution.py:318
  44.6 0.6 collective-permute-start.2
  45.1 2.1 %collective-permute-start.5 = (bf16[384,768]{1,0:T(8,128)(2,1)S(1)}, bf16[384,768]{1,0:T(8,128)(2,1)S(1)}, u32[]{:S(2)}, u32[]{:S(2)}) collective-permute-start(bf16[384,768]{1,0:T(8,128)(2,1)S(1)} %get-tuple-element.280), channel_id=1, source_target_pairs={{12,0},{13,1},{14,2},{15,3},{0,4},{1,5},{2,6},{3,7},{4,8},{5,9},{6... | collective-permute-start | bytes 1769480 | tf_op jit(solution)/shard_map/ppermute | solution.py:318
  47.2 1.7 %collective-permute-start.4 = (bf16[272,768]{1,0:T(8,128)(2,1)S(1)}, bf16[272,768]{1,0:T(8,128)(2,1)S(1)}, u32[]{:S(2)}, u32[]{:S(2)}) collective-permute-start(bf16[272,768]{1,0:T(8,128)(2,1)S(1)} %get-tuple-element.279), channel_id=1, source_target_pairs={{3,0},{0,1},{1,2},{2,3},{7,4},{4,5},{5,6},{6,7},{11,8},{8,9},{9,10... | collective-permute-start | bytes 1253384 | tf_op jit(solution)/shard_map/ppermute | solution.py:318
  48.9 9.9 %collective-permute-done.4.low = bf16[272,768]{1,0:T(8,128)(2,1)S(1)} collective-permute-done((bf16[272,768]{1,0:T(8,128)(2,1)S(1)}, bf16[272,768]{1,0:T(8,128)(2,1)S(1)}, u32[]{:S(2)}, u32[]{:S(2)}) %collective-permute-start.4) | collective-permute-done | bytes 417824 | tf_op jit(solution)/shard_map/ppermute | solution.py:318
  58.9 1.5 %collective-permute-done.5.high = bf16[384,768]{1,0:T(8,128)(2,1)S(1)} collective-permute-done((bf16[384,768]{1,0:T(8,128)(2,1)S(1)}, bf16[384,768]{1,0:T(8,128)(2,1)S(1)}, u32[]{:S(2)}, u32[]{:S(2)}) %collective-permute-start.5) | collective-permute-done | bytes 589856 | tf_op jit(solution)/shard_map/ppermute | solution.py:318
  60.4 4.0 %collective-permute-done.3.b2 = bf16[640,768]{1,0:T(8,128)(2,1)S(1)} collective-permute-done((bf16[640,768]{1,0:T(8,128)(2,1)S(1)}, bf16[640,768]{1,0:T(8,128)(2,1)S(1)}, u32[]{:S(2)}, u32[]{:S(2)}) %collective-permute-start.3) | collective-permute-done | bytes 983072 | tf_op jit(solution)/shard_map/ppermute | solution.py:318
  64.3 0.0 collective-permute-done.2.b1
  64.3 0.5 collective-permute-start.6
  64.8 0.0 collective-permute-start.7
  64.8 5.9 %early.1 = (f32[8,640]{1,0:T(8,128)S(1)}, f32[8,640]{1,0:T(8,128)S(1)}) custom-call(bf16[640,768]{1,0:T(8,128)(2,1)S(1)} %get-tuple-element.278.b0, bf16[640,768]{1,0:T(8,128)(2,1)S(1)} %collective-permute-done.2.b1, bf16[640,768]{1,0:T(8,128)(2,1)S(1)} %collective-permute-done.3.b2, bf16[272,768]{1,0:T(8,128)(2,1)S(1)} %collective-permute-done.4.low, ...), custom_call_target="tpu_custom_call" | custom-call | flops 6000000000 | bytes 8000000 | tf_op jit(solution)/shard_map/early/pallas_call | solution.py:359
  70.7 7.8 %collective-permute-done.6.b3 = bf16[640,768]{1,0:T(8,128)(2,1)S(1)} collective-permute-done((bf16[640,768]{1,0:T(8,128)(2,1)S(1)}, bf16[640,768]{1,0:T(8,128)(2,1)S(1)}, u32[]{:S(2)}, u32[]{:S(2)}) %collective-permute-start.6) | collective-permute-done | bytes 983072 | tf_op jit(solution)/shard_map/ppermute | solution.py:318
  78.5 0.4 collective-permute-done.7.b4
  79.0 4.5 %late.1 = f32[128,128]{1,0:T(8,128)} custom-call(bf16[640,768]{1,0:T(8,128)(2,1)S(1)} %get-tuple-element.278.b0, bf16[640,768]{1,0:T(8,128)(2,1)S(1)} %collective-permute-done.2.b1, bf16[640,768]{1,0:T(8,128)(2,1)S(1)} %collective-permute-done.3.b2, bf16[640,768]{1,0:T(8,128)(2,1)S(1)} %collective-permute-done.6.b3, ...), custom_call_target="tpu_custom_call" | custom-call | flops 4000000000 | bytes 8000000 | tf_op jit(solution)/shard_map/late/pallas_call | solution.py:366
  83.5 7.7 %all-to-all-start.5 = ((f32[128,1,128]{2,1,0:T(1,128)}), f32[128,1,128]{2,1,0:T(1,128)S(1)}, u32[]{:S(2)}, u32[]{:S(2)}) async-start(f32[128,1,128]{2,1,0:T(1,128)} %bitcast.24), calls=%async_computation.5 | async-start | bytes 131072 | tf_op jit(solution)/shard_map/all_to_all | solution.py:373
  91.2 0.6 reduce_max.25
  92.5 8.3 %all-to-all-done.5 = f32[128,1,128]{2,1,0:T(1,128)S(1)} async-done(((f32[128,1,128]{2,1,0:T(1,128)}), f32[128,1,128]{2,1,0:T(1,128)S(1)}, u32[]{:S(2)}, u32[]{:S(2)}) %all-to-all-start.5) | async-done | bytes 65568 | tf_op jit(solution)/shard_map/all_to_all | solution.py:373
  100.8 0.0 copy-done
  100.8 0.0 copy-done.1
  100.8 0.0 copy-done.2
  100.8 1.1 %finish.1 = (f32[1,512]{1,0:T(1,128)}, f32[1,512]{1,0:T(1,128)}) custom-call(f32[128,128]{1,0:T(8,128)S(1)} %bitcast.61, s32[8,512]{1,0:T(8,128)S(1)} %get-tuple-element.287.places), custom_call_target="tpu_custom_call" | custom-call | flops 33554432 | bytes 8000000 | tf_op jit(solution)/shard_map/finish/pallas_call | solution.py:374
  (4 shorter events, 0.0 us)
Async XLA Ops:
  43.5 20.8 %collective-permute-start.3 = (bf16[640,768]{1,0:T(8,128)(2,1)S(1)}, bf16[640,768]{1,0:T(8,128)(2,1)S(1)}, u32[]{:S(2)}, u32[]{:S(2)}) collective-permute-start(bf16[640,768]{1,0:T(8,128)(2,1)S(1)} %get-tuple-element.278.b0), channel_id=1, source_target_pairs={{1,0},{2,1},{3,2},{0,3},{5,4},{6,5},{7,6},{4,7},{9,8},{10,9},{11,1... | collective-permute-start | bytes 2949128 | tf_op jit(solution)/shard_map/ppermute | solution.py:318
  44.6 19.8 %collective-permute-start.2 = (bf16[640,768]{1,0:T(8,128)(2,1)S(1)}, bf16[640,768]{1,0:T(8,128)(2,1)S(1)}, u32[]{:S(2)}, u32[]{:S(2)}) collective-permute-start(bf16[640,768]{1,0:T(8,128)(2,1)S(1)} %get-tuple-element.278.b0), channel_id=1, source_target_pairs={{4,0},{5,1},{6,2},{7,3},{8,4},{9,5},{10,6},{11,7},{12,8},{13,9},{1... | collective-permute-start | bytes 2949128 | tf_op jit(solution)/shard_map/ppermute | solution.py:318
  45.1 15.3 %collective-permute-start.5 = (bf16[384,768]{1,0:T(8,128)(2,1)S(1)}, bf16[384,768]{1,0:T(8,128)(2,1)S(1)}, u32[]{:S(2)}, u32[]{:S(2)}) collective-permute-start(bf16[384,768]{1,0:T(8,128)(2,1)S(1)} %get-tuple-element.280), channel_id=1, source_target_pairs={{12,0},{13,1},{14,2},{15,3},{0,4},{1,5},{2,6},{3,7},{4,8},{5,9},{6... | collective-permute-start | bytes 1769480 | tf_op jit(solution)/shard_map/ppermute | solution.py:318
  47.2 11.6 %collective-permute-start.4 = (bf16[272,768]{1,0:T(8,128)(2,1)S(1)}, bf16[272,768]{1,0:T(8,128)(2,1)S(1)}, u32[]{:S(2)}, u32[]{:S(2)}) collective-permute-start(bf16[272,768]{1,0:T(8,128)(2,1)S(1)} %get-tuple-element.279), channel_id=1, source_target_pairs={{3,0},{0,1},{1,2},{2,3},{7,4},{4,5},{5,6},{6,7},{11,8},{8,9},{9,10... | collective-permute-start | bytes 1253384 | tf_op jit(solution)/shard_map/ppermute | solution.py:318
  64.3 14.2 %collective-permute-start.6 = (bf16[640,768]{1,0:T(8,128)(2,1)S(1)}, bf16[640,768]{1,0:T(8,128)(2,1)S(1)}, u32[]{:S(2)}, u32[]{:S(2)}) collective-permute-start(bf16[640,768]{1,0:T(8,128)(2,1)S(1)} %collective-permute-done.2.b1), channel_id=1, source_target_pairs={{4,0},{5,1},{6,2},{7,3},{8,4},{9,5},{10,6},{11,7},{12,8},{13,9},{1... | collective-permute-start | bytes 2949128 | tf_op jit(solution)/shard_map/ppermute | solution.py:318
  64.8 14.2 %collective-permute-start.7 = (bf16[640,768]{1,0:T(8,128)(2,1)S(1)}, bf16[640,768]{1,0:T(8,128)(2,1)S(1)}, u32[]{:S(2)}, u32[]{:S(2)}) collective-permute-start(bf16[640,768]{1,0:T(8,128)(2,1)S(1)} %collective-permute-done.3.b2), channel_id=1, source_target_pairs={{1,0},{2,1},{3,2},{0,3},{5,4},{6,5},{7,6},{4,7},{9,8},{10,9},{11,1... | collective-permute-start | bytes 2949128 | tf_op jit(solution)/shard_map/ppermute | solution.py:318
  79.0 21.8 %copy-start = (s32[512]{0:T(512)S(1)}, s32[512]{0:T(512)}, u32[]{:S(2)}) copy-start(s32[512]{0:T(512)} %param.9) | copy-start | bytes 6148
  79.0 21.8 %copy-start.1 = (bf16[512,768]{1,0:T(8,128)(2,1)S(1)}, bf16[512,768]{1,0:T(8,128)(2,1)}, u32[]{:S(2)}) copy-start(bf16[512,768]{1,0:T(8,128)(2,1)} %rows.1) | copy-start | bytes 2359300
  79.0 21.8 %copy-start.2 = (s32[512]{0:T(512)S(1)}, s32[512]{0:T(512)}, u32[]{:S(2)}) copy-start(s32[512]{0:T(512)} %param.8) | copy-start | bytes 6148
  83.5 17.3 %all-to-all-start.5 = ((f32[128,1,128]{2,1,0:T(1,128)}), f32[128,1,128]{2,1,0:T(1,128)S(1)}, u32[]{:S(2)}, u32[]{:S(2)}) async-start(f32[128,1,128]{2,1,0:T(1,128)} %bitcast.24), calls=%async_computation.5 | async-start | bytes 131072 | tf_op jit(solution)/shard_map/all_to_all | solution.py:373

commit v7 on v6

--- a/solution.py
+++ b/solution.py
@@ -16,8 +16,9 @@
 DEVICES = GROUPS * MEMBERS
 SHARE = 8
 HELD = DEVICES * SHARE
+SENT = 608
+ROOM = SENT - 16
 BLOCK = 640
-ROOM = BLOCK - 16
 APART = -64.0
 LOG2E = 1.4426950408889634
 AXES = ("grp", "blk")
@@ -26,7 +27,7 @@
 SPOTS = ((0, 0), (1, 0), (0, 1), (2, 0), (0, 2), (0, 3), (3, 0))
 LOW = 256
 LOW_SENT = LOW + 16
-HIGH_SENT = BLOCK - LOW
+HIGH_SENT = SENT - LOW
 ROW_BLOCKS = (1, 2)
 SHIFT = 2.0
 
@@ -95,7 +96,7 @@
         spread[here, FEAT:] = (matmul(pick, marks, NT) + totals).astype(jnp.bfloat16)
 
 
-def pack_kernel(arrived, packed, low, high, over):
+def pack_kernel(arrived, low, high, over):
     tails = arrived[:, FEAT:]
     one = ((iota((128, HELD), 0) * SHARE) == iota((128, HELD), 1)).astype(jnp.bfloat16)
     counts = matmul(one, tails, NN).astype(jnp.int32)
@@ -116,32 +117,28 @@
     names = jnp.where(line == 1, (at >> 3) + 1, jnp.where(line == 2, at & 7, 0))
     names = jnp.where(line == 0, clusters, names.astype(jnp.float32)).astype(jnp.bfloat16)
     pick = (iota((BLOCK, HELD), 0) == position).astype(jnp.bfloat16)
-    packed[:ROOM, :] = matmul(pick[:ROOM], arrived[:, :FEAT], NN).astype(jnp.bfloat16)
+    rows = matmul(pick[:ROOM], arrived[:, :FEAT], NN).astype(jnp.bfloat16)
     named = matmul(names, pick, NT)
     named = jnp.concatenate([named, jnp.zeros((8, FEAT - BLOCK), jnp.float32)], axis=1)
     named = jnp.concatenate([named, jnp.zeros_like(named)], axis=0).astype(jnp.bfloat16)
-    packed[ROOM:, :] = named
-    low[:LOW, :] = packed[:LOW, :]
+    low[:LOW, :] = rows[:LOW]
     low[LOW:, :] = named
-    high[...] = packed[LOW:, :]
+    high[: ROOM - LOW, :] = rows[LOW:]
+    high[ROOM - LOW :, :] = named
 
 
 def column_fold(x, op):
     while x.shape[0] > 8:
-        half = x.shape[0] // 2
-        x = op(x[:half], x[half:])
+        half = x.shape[0] // 16 * 8
+        rest = x[2 * half :]
+        x = op(x[:half], x[half : 2 * half])
+        if rest.shape[0]:
+            x = jnp.concatenate([op(x[:8], rest), x[8:]], axis=0) if half > 8 else op(x, rest)
     return x
 
 
-def row_fold(x, op):
-    total = x[:, :128]
-    for t in range(1, x.shape[1] // 128):
-        total = op(total, x[:, 128 * t : 128 * (t + 1)])
-    return total
-
-
 LOWS = ((0, 256),)
-HIGHS = ((256, 256), (512, 128))
+HIGHS = ((256, 256), (512, SENT - 512))
 PARTS = LOWS + HIGHS
 
 
@@ -154,7 +151,8 @@
 
 
 def names_of(block):
-    return block[block.shape[0] - 16 :, :BLOCK].astype(jnp.float32)
+    part = block[0] if block[1] is None else block[1]
+    return part[part.shape[0] - 16 :, :BLOCK].astype(jnp.float32)
 
 
 def spell(block, place, state):
@@ -165,21 +163,27 @@
         state[4][place, here, :] = jnp.broadcast_to(clusters[:, here], (128, 128)).T
 
 
-def square(rows, cols, place, c, r, state, own=False, downs=PARTS, parts=PARTS, first=0):
+def part_of(block, first, size):
+    if first < LOW:
+        return block[0][first : first + size, :]
+    return block[1][first - LOW : first - LOW + size, :]
+
+
+def square(rows, cols, place, c, r, state, own=False, downs=PARTS, parts=PARTS):
     col_best, col_mass, row_best, row_mass, spelt = state
     clusters = names_of(cols)[0:1]
     for i, tall in downs:
         for j, wide in parts:
-            product = matmul(rows[i : i + tall, :], cols[j - first : j - first + wide, :], NT)
+            product = matmul(part_of(rows, i, tall), part_of(cols, j, wide), NT)
             down = slice(i, i + tall)
-            mine = spelt[place, down, :]
             tops = sums = None
             for t in range(0, wide, 128):
-                across = slice(j + t, j + t + 128)
-                match = mine == clusters[:, across]
+                size = min(128, wide - t)
+                across = slice(j + t, j + t + size)
+                match = spelt[place, down, :size] == clusters[:, across]
                 if own and i == j:
-                    match = match & (iota((tall, 128), 0) != iota((tall, 128), 1) + t)
-                score = jnp.where(match, product[:, t : t + 128], APART)
+                    match = match & (iota((tall, size), 0) != iota((tall, size), 1) + t)
+                score = jnp.where(match, product[:, t : t + size], APART)
                 soft = jnp.exp2((score - 1.0) * (sharpness * LOG2E))
                 col_best[c, :, across] = jnp.maximum(
                     col_best[c, :, across], column_fold(score, jnp.maximum)
@@ -188,8 +192,9 @@
                 tops = score if tops is None else jnp.maximum(tops, score)
                 sums = soft if sums is None else sums + soft
             if r is not None:
-                row_best[r, down, :] = jnp.maximum(row_best[r, down, :], tops)
-                row_mass[r, down, :] = row_mass[r, down, :] + sums
+                size = tops.shape[1]
+                row_best[r, down, :size] = jnp.maximum(row_best[r, down, :size], tops)
+                row_mass[r, down, :size] = row_mass[r, down, :size] + sums
 
 
 def settle(e, state):
@@ -207,39 +212,66 @@
     return best, mass
 
 
-def store(blocks, best_out, mass_out, state):
-    best_out[...] = jnp.full_like(best_out, APART)
-    mass_out[...] = jnp.zeros_like(mass_out)
+def store(blocks, best_in, mass_in, best_out, mass_out, state):
+    if best_in is None:
+        best_out[...] = jnp.full_like(best_out, APART)
+        mass_out[...] = jnp.zeros_like(mass_out)
+    else:
+        best_out[...] = best_in[...]
+        mass_out[...] = mass_in[...]
     for e in blocks:
-        best_out[e : e + 1, :], mass_out[e : e + 1, :] = settle(e, state)
-
-
-def early_kernel(b0, b1, b2, low, high, best_out, mass_out, *state):
+        here = slice(e, e + 1)
+        best, mass = settle(e, state)
+        best_out[here, :] = jnp.maximum(best_out[here, :], best)
+        mass_out[here, :] = mass_out[here, :] + mass
+
+
+def early_kernel(b0l, b0h, b1l, b1h, b2l, b2h, best_out, mass_out, *state):
+    b0, b1, b2 = (b0l, b0h), (b1l, b1h), (b2l, b2h)
     clear(state)
     for place, block in enumerate((b0, b1, b2)):
         spell(block, place, state)
     square(b0, b0, 0, 0, None, state, True)
     square(b1, b0, 1, 0, 0, state)
     square(b1, b2, 1, 2, 0, state)
-    square(b1, low, 1, 5, 0, state, parts=LOWS)
     square(b2, b0, 2, 0, 1, state)
-    square(b2, high, 2, 6, 1, state, parts=HIGHS, first=LOW)
-    square(b1, high, 1, 6, 0, state, downs=LOWS, parts=HIGHS, first=LOW)
-    square(b1, high, 1, 6, None, state, downs=HIGHS, parts=HIGHS, first=LOW)
-    square(b2, low, 2, 5, 1, state, downs=HIGHS, parts=LOWS)
-    square(b2, low, 2, 5, None, state, downs=LOWS, parts=LOWS)
-    store((0, 1, 2, 5, 6), best_out, mass_out, state)
-
-
-def late_kernel(b0, b1, b2, b3, b4, low, high, best_in, mass_in, out, *state):
+    store((0, 1, 2), None, None, best_out, mass_out, state)
+
+
+def middle_kernel(
+    b0l, b1l, b1h, b2l, b2h, b3l, b4l, low, high, best_in, mass_in, best_out, mass_out, *state
+):
+    b0, b1, b2, b3, b4 = (b0l, None), (b1l, b1h), (b2l, b2h), (b3l, None), (b4l, None)
+    low, high = (low, None), (None, high)
     clear(state)
     for place, block in enumerate((b0, b1, b2, b4)):
         spell(block, place, state)
+    square(b1, low, 1, 5, 0, state, parts=LOWS)
+    square(b2, high, 2, 6, 1, state, parts=HIGHS)
+    square(b1, high, 1, 6, 0, state, downs=LOWS, parts=HIGHS)
+    square(b1, high, 1, 6, None, state, downs=HIGHS, parts=HIGHS)
+    square(b2, low, 2, 5, 1, state, downs=HIGHS, parts=LOWS)
+    square(b2, low, 2, 5, None, state, downs=LOWS, parts=LOWS)
     square(b0, b3, 0, 3, None, state, downs=LOWS, parts=LOWS)
+    square(b1, b4, 1, 4, 0, state, parts=LOWS)
+    square(b2, b3, 2, 3, 1, state, parts=LOWS)
+    square(b4, b3, 3, 3, None, state, downs=LOWS, parts=LOWS)
+    store((1, 2, 3, 4, 5, 6), best_in, mass_in, best_out, mass_out, state)
+
+
+def late_kernel(
+    b0h, b1l, b1h, b2l, b2h, b3l, b3h, b4l, b4h, low, high, best_in, mass_in, out, *state
+):
+    b0, b1, b2, b3, b4 = (None, b0h), (b1l, b1h), (b2l, b2h), (b3l, b3h), (b4l, b4h)
+    low, high = (low, None), (None, high)
+    clear(state)
+    for place, block in enumerate((b0, b1, b2, b4)):
+        spell(block, place, state)
     square(b0, b4, 0, 4, None, state, downs=HIGHS, parts=HIGHS)
-    square(b1, b4, 1, 4, 0, state)
-    square(b2, b3, 2, 3, 1, state)
-    square(b4, b3, 3, 3, None, state)
+    square(b1, b4, 1, 4, 0, state, parts=HIGHS)
+    square(b2, b3, 2, 3, 1, state, parts=HIGHS)
+    square(b4, b3, 3, 3, None, state, parts=HIGHS)
+    square(b4, b3, 3, 3, None, state, downs=HIGHS, parts=LOWS)
     source_at = (iota((DEVICES, BLOCK), 0) + 1).astype(jnp.float32)
     line = iota((16, BLOCK), 0)
     back = []
@@ -328,10 +360,9 @@
         name="prelude",
     )(labels.reshape(1, ROWS), cluster_slot.reshape(1, ROWS), embeddings)
     arrived = lax.all_to_all(spread, AXES, split_axis=0, concat_axis=0, tiled=True)
-    b0, low, high, over = call(
+    b0l, b0h, over = call(
         pack_kernel,
         (
-            shape((BLOCK, FEAT), bf16),
             shape((LOW_SENT, FEAT), bf16),
             shape((HIGH_SENT, FEAT), bf16),
             shape((8, 128), i32),
@@ -339,13 +370,18 @@
         flops=3_000_000_000,
         name="pack",
     )(arrived)
-    b1 = from_spot(b0, 1, 0)
-    b2 = from_spot(b0, 0, 1)
+    b1l = from_spot(b0l, 1, 0)
+    b2l = from_spot(b0l, 0, 1)
+    b1h = from_spot(b0h, 1, 0)
+    b2h = from_spot(b0h, 0, 1)
+    high, b1l, b2l = lax.optimization_barrier((b0h, b1l, b2l))
+    high = from_spot(high, 3, 0)
+    b3l = from_spot(b1l, 1, 0)
+    b4l = from_spot(b2l, 0, 1)
+    low, b2h = lax.optimization_barrier((b0l, b2h))
+    b3h = from_spot(b1h, 1, 0)
+    b4h = from_spot(b2h, 0, 1)
     low = from_spot(low, 0, 3)
-    high = from_spot(high, 3, 0)
-    b1, b2, low, high = lax.optimization_barrier((b1, b2, low, high))
-    b3 = from_spot(b1, 1, 0)
-    b4 = from_spot(b2, 0, 1)
 
     def state(places):
         return (
@@ -356,20 +392,20 @@
             pltpu.VMEM((places, BLOCK, 128), f32),
         )
 
+    stats = (shape((8, BLOCK), f32), shape((8, BLOCK), f32))
     best, mass = call(
-        early_kernel,
-        (shape((8, BLOCK), f32), shape((8, BLOCK), f32)),
-        scratch=state(3),
-        flops=6_000_000_000,
-        name="early",
-    )(b0, b1, b2, low, high)
+        early_kernel, stats, scratch=state(3), flops=6_000_000_000, name="early"
+    )(b0l, b0h, b1l, b1h, b2l, b2h)
+    best, mass = call(
+        middle_kernel, stats, scratch=state(4), flops=1_500_000_000, name="middle"
+    )(b0l, b1l, b1h, b2l, b2h, b3l, b4l, low, high, best, mass)
     message = call(
         late_kernel,
         shape((DEVICES, 128), f32),
         scratch=state(4),
-        flops=4_000_000_000,
+        flops=3_000_000_000,
         name="late",
-    )(b0, b1, b2, b3, b4, low, high, best, mass)
+    )(b0h, b1l, b1h, b2l, b2h, b3l, b3h, b4l, b4h, low, high, best, mass)
     answer = lax.all_to_all(message, AXES, split_axis=0, concat_axis=0, tiled=True)
     best, mass = call(
         finish_kernel,

time: 102 us -> 97.6 us (0.957)
  waiting for transfers between devices: 32 us -> 26.2 us
    ppermute x6 -> x10, waiting for transfers between devices: 23.7 us -> 17.9 us  [from_spot(): return lax.ppermute(x, AXES, hop(dy, dz))]
    ppermute x6 -> x10, starting transfers between devices: 5.88 us -> 6.82 us  [from_spot(): return lax.ppermute(x, AXES, hop(dy, dz))]
    pallas_call x3 -> x4, Pallas kernels: 12.4 us -> 12.8 us  [the longest x1 4.12 us: fast(): call(early_kernel, stats, scratch=state(3), flops=6000000000, name='early')]
  transfers between devices with their start and end apart: 7 -> 11, of which waited for: 6 -> 10; matrix products, arithmetic and copies ran while one was open for 1% -> 1% of each run, Pallas kernels for 6% -> 7%
where the time goes in v7:
time: 97.6 us; the launch traced here: 97.4 us
  blocking collectives  38.1 us (39%)
  waiting for transfers between devices  26.2 us (27%)
  Pallas kernels  16.7 us (17%)
  starting transfers between devices  14.5 us (15%)
  between operations  1.33 us (1%)
    all_to_all x1, blocking collectives, fast(): lax.all_to_all(spread, AXES, split_axis=0, concat_axis=0, tiled=True)  38.1 us
    ppermute x10, waiting for transfers between devices, from_spot(): return lax.ppermute(x, AXES, hop(dy, dz))  17.9 us
    all_to_all x1, waiting for transfers between devices, fast(): lax.all_to_all(message, AXES, split_axis=0, concat_axis=0, tiled=True)  8.28 us
    all_to_all x1, starting transfers between devices, fast(): lax.all_to_all(message, AXES, split_axis=0, concat_axis=0, tiled=True)  7.67 us
    ppermute x10, starting transfers between devices, from_spot(): return lax.ppermute(x, AXES, hop(dy, dz))  6.82 us
    pallas_call x1, Pallas kernels, fast(): call(early_kernel, stats, scratch=state(3), flops=6000000000, name='early')  4.12 us
    pallas_call x1, Pallas kernels, fast(): call(late_kernel, shape((DEVICES, 128), f32), scratch=state(4), flops=300...  3.71 us
    pallas_call x1, Pallas kernels, fast(): call(middle_kernel, stats, scratch=state(4), flops=1500000000, name='midd...  3.02 us
  transfers between devices with their start and end apart: 11, of which 10 were waited for; matrix products, arithmetic and copies ran while one was open for 1% of the time, Pallas kernels for 7%

profile of v7, /device:TPU:1, one launch (start us, length us, event | category | flops | bytes accessed | tf_op | source)
XLA Modules:
  0.0 97.4 jit_solution(984483619937207912)
XLA Ops:
  0.6 2.8 %prelude.1 = (bf16[1024,896]{1,0:T(8,128)(2,1)S(1)}, s32[8,512]{1,0:T(8,128)S(1)}) custom-call(s32[1,512]{1,0:T(1,128)} %bitcast.73, s32[1,512]{1,0:T(1,128)} %bitcast.62, bf16[512,768]{1,0:T(8,128)(2,1)} %rows.1), custom_call_target="tpu_custom_call" | custom-call | flops 3000000000 | bytes 8000000 | tf_op jit(solution)/shard_map/prelude/pallas_call | solution.py:356
  3.4 38.1 %all_to_all.59 = bf16[128,8,896]{2,1,0:T(8,128)(2,1)S(1)} all-to-all(bf16[128,8,896]{2,1,0:T(8,128)(2,1)S(1)} %bitcast.60), channel_id=1, replica_groups=mesh['grp'=8,'blk'=16] {'grp','blk'}, dimensions={0} | all-to-all | bytes 3670016 | tf_op jit(solution)/shard_map/all_to_all | solution.py:362
  41.5 1.9 %pack.1 = (bf16[272,768]{1,0:T(8,128)(2,1)S(1)}, bf16[352,768]{1,0:T(8,128)(2,1)S(1)}, s32[8,128]{1,0:T(8,128)S(1)}) custom-call(bf16[1024,896]{1,0:T(8,128)(2,1)S(1)} %bitcast.59), custom_call_target="tpu_custom_call" | custom-call | flops 3000000000 | bytes 8000000 | tf_op jit(solution)/shard_map/pack/pallas_call | solution.py:363
  43.4 1.1 %collective-permute-start.3 = (bf16[272,768]{1,0:T(8,128)(2,1)S(1)}, bf16[272,768]{1,0:T(8,128)(2,1)S(1)}, u32[]{:S(2)}, u32[]{:S(2)}) collective-permute-start(bf16[272,768]{1,0:T(8,128)(2,1)S(1)} %get-tuple-element.285.b0l), channel_id=1, source_target_pairs={{1,0},{2,1},{3,2},{0,3},{5,4},{6,5},{7,6},{4,7},{9,8},{10,9},{11,1... | collective-permute-start | bytes 1253384 | tf_op jit(solution)/shard_map/ppermute | solution.py:350
  44.5 0.6 collective-permute-start.2
  45.0 0.7 collective-permute-start.5
  45.7 5.9 %collective-permute-done.3.b2l = bf16[272,768]{1,0:T(8,128)(2,1)S(1)} collective-permute-done((bf16[272,768]{1,0:T(8,128)(2,1)S(1)}, bf16[272,768]{1,0:T(8,128)(2,1)S(1)}, u32[]{:S(2)}, u32[]{:S(2)}) %collective-permute-start.3) | collective-permute-done | bytes 417824 | tf_op jit(solution)/shard_map/ppermute | solution.py:350
  51.6 1.0 %collective-permute-done.2.b1l = bf16[272,768]{1,0:T(8,128)(2,1)S(1)} collective-permute-done((bf16[272,768]{1,0:T(8,128)(2,1)S(1)}, bf16[272,768]{1,0:T(8,128)(2,1)S(1)}, u32[]{:S(2)}, u32[]{:S(2)}) %collective-permute-start.2) | collective-permute-done | bytes 417824 | tf_op jit(solution)/shard_map/ppermute | solution.py:350
  52.6 0.7 collective-permute-start.8
  53.3 2.7 %collective-permute-start.11 = (bf16[352,768]{1,0:T(8,128)(2,1)S(1)}, bf16[352,768]{1,0:T(8,128)(2,1)S(1)}, u32[]{:S(2)}, u32[]{:S(2)}) collective-permute-start(bf16[352,768]{1,0:T(8,128)(2,1)S(1)} %get-tuple-element.286.b0h), channel_id=1, source_target_pairs={{12,0},{13,1},{14,2},{15,3},{0,4},{1,5},{2,6},{3,7},{4,8},{5,9},{6... | collective-permute-start | bytes 1622024 | tf_op jit(solution)/shard_map/ppermute | solution.py:350
  55.9 1.5 %collective-permute-done.5.b2h = bf16[352,768]{1,0:T(8,128)(2,1)S(1)} collective-permute-done((bf16[352,768]{1,0:T(8,128)(2,1)S(1)}, bf16[352,768]{1,0:T(8,128)(2,1)S(1)}, u32[]{:S(2)}, u32[]{:S(2)}) %collective-permute-start.5) | collective-permute-done | bytes 540704 | tf_op jit(solution)/shard_map/ppermute | solution.py:350
  58.4 0.7 collective-permute-start.9
  59.0 4.1 %collective-permute-done.6.b3l = bf16[272,768]{1,0:T(8,128)(2,1)S(1)} collective-permute-done((bf16[272,768]{1,0:T(8,128)(2,1)S(1)}, bf16[272,768]{1,0:T(8,128)(2,1)S(1)}, u32[]{:S(2)}, u32[]{:S(2)}) %collective-permute-start.6) | collective-permute-done | bytes 417824 | tf_op jit(solution)/shard_map/ppermute | solution.py:350
  63.2 4.1 %early.1 = (f32[8,640]{1,0:T(8,128)S(1)}, f32[8,640]{1,0:T(8,128)S(1)}) custom-call(bf16[272,768]{1,0:T(8,128)(2,1)S(1)} %get-tuple-element.285.b0l, bf16[352,768]{1,0:T(8,128)(2,1)S(1)} %get-tuple-element.286.b0h, bf16[272,768]{1,0:T(8,128)(2,1)S(1)} %collective-permute-done.2.b1l, bf16[352,768]{1,0:T(8,128)(2,1)S(1)} %collective-permute-done.4.b1h, ...), custom_call_target="tpu_custom_call" | custom-call | flops 6000000000 | bytes 8000000 | tf_op jit(solution)/shard_map/early/pallas_call | solution.py:396
  67.3 0.6 collective-permute-done.11.high
  67.9 0.6 collective-permute-done.10.low
  68.5 3.0 %middle.1 = (f32[8,640]{1,0:T(8,128)S(1)}, f32[8,640]{1,0:T(8,128)S(1)}) custom-call(bf16[272,768]{1,0:T(8,128)(2,1)S(1)} %get-tuple-element.285.b0l, bf16[272,768]{1,0:T(8,128)(2,1)S(1)} %collective-permute-done.2.b1l, bf16[352,768]{1,0:T(8,128)(2,1)S(1)} %collective-permute-done.4.b1h, bf16[272,768]{1,0:T(8,128)(2,1)S(1)} %collective-permute-done.3.b2l, ...), custom_call_target="tpu_custom_call" | custom-call | flops 1500000000 | bytes 8000000 | tf_op jit(solution)/shard_map/middle/pallas_call | solution.py:399
  71.5 2.0 %collective-permute-done.9.b4h = bf16[352,768]{1,0:T(8,128)(2,1)S(1)} collective-permute-done((bf16[352,768]{1,0:T(8,128)(2,1)S(1)}, bf16[352,768]{1,0:T(8,128)(2,1)S(1)}, u32[]{:S(2)}, u32[]{:S(2)}) %collective-permute-start.9) | collective-permute-done | bytes 540704 | tf_op jit(solution)/shard_map/ppermute | solution.py:350
  73.5 1.9 %collective-permute-done.7.b3h = bf16[352,768]{1,0:T(8,128)(2,1)S(1)} collective-permute-done((bf16[352,768]{1,0:T(8,128)(2,1)S(1)}, bf16[352,768]{1,0:T(8,128)(2,1)S(1)}, u32[]{:S(2)}, u32[]{:S(2)}) %collective-permute-start.7) | collective-permute-done | bytes 540704 | tf_op jit(solution)/shard_map/ppermute | solution.py:350
  75.4 3.7 %late.1 = f32[128,128]{1,0:T(8,128)} custom-call(bf16[352,768]{1,0:T(8,128)(2,1)S(1)} %get-tuple-element.286.b0h, bf16[272,768]{1,0:T(8,128)(2,1)S(1)} %collective-permute-done.2.b1l, bf16[352,768]{1,0:T(8,128)(2,1)S(1)} %collective-permute-done.4.b1h, bf16[272,768]{1,0:T(8,128)(2,1)S(1)} %collective-permute-done.3.b2l, ...), custom_call_target="tpu_custom_call" | custom-call | flops 3000000000 | bytes 8000000 | tf_op jit(solution)/shard_map/late/pallas_call | solution.py:402
  79.1 7.7 %all-to-all-start.5 = ((f32[128,1,128]{2,1,0:T(1,128)}), f32[128,1,128]{2,1,0:T(1,128)S(1)}, u32[]{:S(2)}, u32[]{:S(2)}) async-start(f32[128,1,128]{2,1,0:T(1,128)} %bitcast.24), calls=%async_computation.5 | async-start | bytes 131072 | tf_op jit(solution)/shard_map/all_to_all | solution.py:409
  86.8 0.6 reduce_max.25
  88.0 8.3 %all-to-all-done.5 = f32[128,1,128]{2,1,0:T(1,128)S(1)} async-done(((f32[128,1,128]{2,1,0:T(1,128)}), f32[128,1,128]{2,1,0:T(1,128)S(1)}, u32[]{:S(2)}, u32[]{:S(2)}) %all-to-all-start.5) | async-done | bytes 65568 | tf_op jit(solution)/shard_map/all_to_all | solution.py:409
  96.3 1.1 %finish.1 = (f32[1,512]{1,0:T(1,128)}, f32[1,512]{1,0:T(1,128)}) custom-call(f32[128,128]{1,0:T(8,128)S(1)} %bitcast.61, s32[8,512]{1,0:T(8,128)S(1)} %get-tuple-element.291.places), custom_call_target="tpu_custom_call" | custom-call | flops 33554432 | bytes 8000000 | tf_op jit(solution)/shard_map/finish/pallas_call | solution.py:410
  (13 shorter events, 1.0 us)
Async XLA Ops:
  43.4 8.2 %collective-permute-start.3 = (bf16[272,768]{1,0:T(8,128)(2,1)S(1)}, bf16[272,768]{1,0:T(8,128)(2,1)S(1)}, u32[]{:S(2)}, u32[]{:S(2)}) collective-permute-start(bf16[272,768]{1,0:T(8,128)(2,1)S(1)} %get-tuple-element.285.b0l), channel_id=1, source_target_pairs={{1,0},{2,1},{3,2},{0,3},{5,4},{6,5},{7,6},{4,7},{9,8},{10,9},{11,1... | collective-permute-start | bytes 1253384 | tf_op jit(solution)/shard_map/ppermute | solution.py:350
  44.5 8.1 %collective-permute-start.2 = (bf16[272,768]{1,0:T(8,128)(2,1)S(1)}, bf16[272,768]{1,0:T(8,128)(2,1)S(1)}, u32[]{:S(2)}, u32[]{:S(2)}) collective-permute-start(bf16[272,768]{1,0:T(8,128)(2,1)S(1)} %get-tuple-element.285.b0l), channel_id=1, source_target_pairs={{4,0},{5,1},{6,2},{7,3},{8,4},{9,5},{10,6},{11,7},{12,8},{13,9},{1... | collective-permute-start | bytes 1253384 | tf_op jit(solution)/shard_map/ppermute | solution.py:350
  45.0 12.4 %collective-permute-start.5 = (bf16[352,768]{1,0:T(8,128)(2,1)S(1)}, bf16[352,768]{1,0:T(8,128)(2,1)S(1)}, u32[]{:S(2)}, u32[]{:S(2)}) collective-permute-start(bf16[352,768]{1,0:T(8,128)(2,1)S(1)} %get-tuple-element.286.b0h), channel_id=1, source_target_pairs={{1,0},{2,1},{3,2},{0,3},{5,4},{6,5},{7,6},{4,7},{9,8},{10,9},{11,1... | collective-permute-start | bytes 1622024 | tf_op jit(solution)/shard_map/ppermute | solution.py:350
  45.7 12.7 %collective-permute-start.4 = (bf16[352,768]{1,0:T(8,128)(2,1)S(1)}, bf16[352,768]{1,0:T(8,128)(2,1)S(1)}, u32[]{:S(2)}, u32[]{:S(2)}) collective-permute-start(bf16[352,768]{1,0:T(8,128)(2,1)S(1)} %get-tuple-element.286.b0h), channel_id=1, source_target_pairs={{4,0},{5,1},{6,2},{7,3},{8,4},{9,5},{10,6},{11,7},{12,8},{13,9},{1... | collective-permute-start | bytes 1622024 | tf_op jit(solution)/shard_map/ppermute | solution.py:350
  52.6 10.6 %collective-permute-start.6 = (bf16[272,768]{1,0:T(8,128)(2,1)S(1)}, bf16[272,768]{1,0:T(8,128)(2,1)S(1)}, u32[]{:S(2)}, u32[]{:S(2)}) collective-permute-start(bf16[272,768]{1,0:T(8,128)(2,1)S(1)} %collective-permute-done.2.b1l), channel_id=1, source_target_pairs={{4,0},{5,1},{6,2},{7,3},{8,4},{9,5},{10,6},{11,7},{12,8},{13,9},{1... | collective-permute-start | bytes 1253384 | tf_op jit(solution)/shard_map/ppermute | solution.py:350
  52.6 14.7 %collective-permute-start.8 = (bf16[272,768]{1,0:T(8,128)(2,1)S(1)}, bf16[272,768]{1,0:T(8,128)(2,1)S(1)}, u32[]{:S(2)}, u32[]{:S(2)}) collective-permute-start(bf16[272,768]{1,0:T(8,128)(2,1)S(1)} %collective-permute-done.3.b2l), channel_id=1, source_target_pairs={{1,0},{2,1},{3,2},{0,3},{5,4},{6,5},{7,6},{4,7},{9,8},{10,9},{11,1... | collective-permute-start | bytes 1253384 | tf_op jit(solution)/shard_map/ppermute | solution.py:350
  53.3 14.6 %collective-permute-start.11 = (bf16[352,768]{1,0:T(8,128)(2,1)S(1)}, bf16[352,768]{1,0:T(8,128)(2,1)S(1)}, u32[]{:S(2)}, u32[]{:S(2)}) collective-permute-start(bf16[352,768]{1,0:T(8,128)(2,1)S(1)} %get-tuple-element.286.b0h), channel_id=1, source_target_pairs={{12,0},{13,1},{14,2},{15,3},{0,4},{1,5},{2,6},{3,7},{4,8},{5,9},{6... | collective-permute-start | bytes 1622024 | tf_op jit(solution)/shard_map/ppermute | solution.py:350
  57.4 11.1 %collective-permute-start.10 = (bf16[272,768]{1,0:T(8,128)(2,1)S(1)}, bf16[272,768]{1,0:T(8,128)(2,1)S(1)}, u32[]{:S(2)}, u32[]{:S(2)}) collective-permute-start(bf16[272,768]{1,0:T(8,128)(2,1)S(1)} %get-tuple-element.285.b0l), channel_id=1, source_target_pairs={{3,0},{0,1},{1,2},{2,3},{7,4},{4,5},{5,6},{6,7},{11,8},{8,9},{9,10... | collective-permute-start | bytes 1253384 | tf_op jit(solution)/shard_map/ppermute | solution.py:350
  58.4 15.1 %collective-permute-start.9 = (bf16[352,768]{1,0:T(8,128)(2,1)S(1)}, bf16[352,768]{1,0:T(8,128)(2,1)S(1)}, u32[]{:S(2)}, u32[]{:S(2)}) collective-permute-start(bf16[352,768]{1,0:T(8,128)(2,1)S(1)} %collective-permute-done.5.b2h), channel_id=1, source_target_pairs={{1,0},{2,1},{3,2},{0,3},{5,4},{6,5},{7,6},{4,7},{9,8},{10,9},{11,1... | collective-permute-start | bytes 1622024 | tf_op jit(solution)/shard_map/ppermute | solution.py:350
  63.2 12.2 %collective-permute-start.7 = (bf16[352,768]{1,0:T(8,128)(2,1)S(1)}, bf16[352,768]{1,0:T(8,128)(2,1)S(1)}, u32[]{:S(2)}, u32[]{:S(2)}) collective-permute-start(bf16[352,768]{1,0:T(8,128)(2,1)S(1)} %collective-permute-done.4.b1h), channel_id=1, source_target_pairs={{4,0},{5,1},{6,2},{7,3},{8,4},{9,5},{10,6},{11,7},{12,8},{13,9},{1... | collective-permute-start | bytes 1622024 | tf_op jit(solution)/shard_map/ppermute | solution.py:350
  75.4 21.0 %copy-start = (s32[512]{0:T(512)S(1)}, s32[512]{0:T(512)}, u32[]{:S(2)}) copy-start(s32[512]{0:T(512)} %param.9) | copy-start | bytes 6148
  75.4 21.0 %copy-start.1 = (bf16[512,768]{1,0:T(8,128)(2,1)S(1)}, bf16[512,768]{1,0:T(8,128)(2,1)}, u32[]{:S(2)}) copy-start(bf16[512,768]{1,0:T(8,128)(2,1)} %rows.1) | copy-start | bytes 2359300
  75.4 21.0 %copy-start.2 = (s32[512]{0:T(512)S(1)}, s32[512]{0:T(512)}, u32[]{:S(2)}) copy-start(s32[512]{0:T(512)} %param.8) | copy-start | bytes 6148
  79.1 17.2 %all-to-all-start.5 = ((f32[128,1,128]{2,1,0:T(1,128)}), f32[128,1,128]{2,1,0:T(1,128)S(1)}, u32[]{:S(2)}, u32[]{:S(2)}) async-start(f32[128,1,128]{2,1,0:T(1,128)} %bitcast.24), calls=%async_computation.5 | async-start | bytes 131072 | tf_op jit(solution)/shard_map/all_to_all | solution.py:409

commit v8 on v7

--- a/solution.py
+++ b/solution.py
@@ -96,10 +96,33 @@
         spread[here, FEAT:] = (matmul(pick, marks, NT) + totals).astype(jnp.bfloat16)
 
 
-def pack_kernel(arrived, low, high, over):
+def pack_low_kernel(arrived, low, position_out):
     tails = arrived[:, FEAT:]
+    at, line = iota((8, HELD), 1), iota((8, HELD), 0)
+    clusters = matmul((iota((8, 128), 1) == 0).astype(jnp.bfloat16), tails, NT)
+    held = clusters > 0.0
+    before = (iota((HELD, HELD), 0) < iota((HELD, HELD), 1)).astype(jnp.bfloat16)
+    position = matmul(held.astype(jnp.bfloat16), before, NN)
+    position = jnp.where(held, position, -1.0).astype(jnp.int32)
+    position_out[...] = position
+    names = jnp.where(line == 1, (at >> 3) + 1, jnp.where(line == 2, at & 7, 0))
+    names = jnp.where(line == 0, clusters, names.astype(jnp.float32)).astype(jnp.bfloat16)
+    pick = (iota((BLOCK, HELD), 0) == position[0:1]).astype(jnp.bfloat16)
+    low[:LOW, :] = matmul(pick[:LOW], arrived[:, :FEAT], NN).astype(jnp.bfloat16)
+    named = matmul(names, pick, NT)
+    named = jnp.concatenate([named, jnp.zeros((8, FEAT - BLOCK), jnp.float32)], axis=1)
+    low[LOW:, :] = jnp.concatenate([named, jnp.zeros_like(named)], axis=0).astype(jnp.bfloat16)
+
+
+def pack_high_kernel(arrived, low, position, high):
+    pick = (iota((ROOM - LOW, HELD), 0) + LOW == position[0:1, :]).astype(jnp.bfloat16)
+    high[: ROOM - LOW, :] = matmul(pick, arrived[:, :FEAT], NN).astype(jnp.bfloat16)
+    high[ROOM - LOW :, :] = low[LOW:, :]
+
+
+def over_kernel(arrived, over):
     one = ((iota((128, HELD), 0) * SHARE) == iota((128, HELD), 1)).astype(jnp.bfloat16)
-    counts = matmul(one, tails, NN).astype(jnp.int32)
+    counts = matmul(one, arrived[:, FEAT:], NN).astype(jnp.int32)
     counts = jnp.where(iota((128, 128), 1) >= 64, counts, 0)
     turned = iota((128, 128), 0) & (MEMBERS - 1)
     most = jnp.zeros((1, 128), jnp.int32)
@@ -107,24 +130,6 @@
         gets = (counts + (MEMBERS - 1) - ((k - turned) & (MEMBERS - 1))) >> 4
         most = jnp.maximum(most, jnp.sum(gets, axis=0, keepdims=True))
     over[...] = jnp.broadcast_to((most > ROOM).astype(jnp.int32), (8, 128))
-
-    at, line = iota((8, HELD), 1), iota((8, HELD), 0)
-    clusters = matmul((iota((8, 128), 1) == 0).astype(jnp.bfloat16), tails, NT)
-    held = clusters > 0.0
-    before = (iota((HELD, HELD), 0) < iota((HELD, HELD), 1)).astype(jnp.bfloat16)
-    position = matmul(held.astype(jnp.bfloat16), before, NN)
-    position = jnp.where(held, position, -1.0)[0:1].astype(jnp.int32)
-    names = jnp.where(line == 1, (at >> 3) + 1, jnp.where(line == 2, at & 7, 0))
-    names = jnp.where(line == 0, clusters, names.astype(jnp.float32)).astype(jnp.bfloat16)
-    pick = (iota((BLOCK, HELD), 0) == position).astype(jnp.bfloat16)
-    rows = matmul(pick[:ROOM], arrived[:, :FEAT], NN).astype(jnp.bfloat16)
-    named = matmul(names, pick, NT)
-    named = jnp.concatenate([named, jnp.zeros((8, FEAT - BLOCK), jnp.float32)], axis=1)
-    named = jnp.concatenate([named, jnp.zeros_like(named)], axis=0).astype(jnp.bfloat16)
-    low[:LOW, :] = rows[:LOW]
-    low[LOW:, :] = named
-    high[: ROOM - LOW, :] = rows[LOW:]
-    high[ROOM - LOW :, :] = named
 
 
 def column_fold(x, op):
@@ -360,16 +365,15 @@
         name="prelude",
     )(labels.reshape(1, ROWS), cluster_slot.reshape(1, ROWS), embeddings)
     arrived = lax.all_to_all(spread, AXES, split_axis=0, concat_axis=0, tiled=True)
-    b0l, b0h, over = call(
-        pack_kernel,
-        (
-            shape((LOW_SENT, FEAT), bf16),
-            shape((HIGH_SENT, FEAT), bf16),
-            shape((8, 128), i32),
-        ),
-        flops=3_000_000_000,
-        name="pack",
+    b0l, position = call(
+        pack_low_kernel,
+        (shape((LOW_SENT, FEAT), bf16), shape((8, HELD), i32)),
+        flops=2_000_000_000,
+        name="pack_low",
     )(arrived)
+    b0h = call(
+        pack_high_kernel, shape((HIGH_SENT, FEAT), bf16), flops=1_000_000_000, name="pack_high"
+    )(arrived, b0l, position)
     b1l = from_spot(b0l, 1, 0)
     b2l = from_spot(b0l, 0, 1)
     b1h = from_spot(b0h, 1, 0)
@@ -378,7 +382,8 @@
     high = from_spot(high, 3, 0)
     b3l = from_spot(b1l, 1, 0)
     b4l = from_spot(b2l, 0, 1)
-    low, b2h = lax.optimization_barrier((b0l, b2h))
+    low, b1h, b2h = lax.optimization_barrier((b0l, b1h, b2h))
+    over = call(over_kernel, shape((8, 128), i32), flops=10_000_000, name="over")(arrived)
     b3h = from_spot(b1h, 1, 0)
     b4h = from_spot(b2h, 0, 1)
     low = from_spot(low, 0, 3)

time: 97.6 us -> 95.5 us (0.978)
  waiting for transfers between devices: 26.2 us -> 22.8 us
    ppermute x10, waiting for transfers between devices: 17.9 us -> 14.9 us  [from_spot(): return lax.ppermute(x, AXES, hop(dy, dz))]
    ppermute x10, starting transfers between devices: 6.82 us -> 8 us  [from_spot(): return lax.ppermute(x, AXES, hop(dy, dz))]
    pallas_call x1 -> x3, Pallas kernels: 1.92 us -> 2.28 us  [the longest x1 1.21 us: fast(): call(pack_low_kernel, (shape((LOW_SENT, FEAT), bf16), shape((8, HELD), i3...]
  transfers between devices with their start and end apart: 11 -> 11, of which waited for: 10 -> 8; matrix products, arithmetic and copies ran while one was open for 1% -> 1% of each run, Pallas kernels for 7% -> 9%
where the time goes in v8:
time: 95.5 us; the launch traced here: 95.3 us
  blocking collectives  38.1 us (40%)
  waiting for transfers between devices  22.8 us (24%)
  Pallas kernels  17.1 us (18%)
  starting transfers between devices  15.4 us (16%)
  between operations  1.35 us (1%)
    all_to_all x1, blocking collectives, fast(): lax.all_to_all(spread, AXES, split_axis=0, concat_axis=0, tiled=True)  38.1 us
    ppermute x10, waiting for transfers between devices, from_spot(): return lax.ppermute(x, AXES, hop(dy, dz))  14.9 us
    ppermute x10, starting transfers between devices, from_spot(): return lax.ppermute(x, AXES, hop(dy, dz))  8 us
    all_to_all x1, waiting for transfers between devices, fast(): lax.all_to_all(message, AXES, split_axis=0, concat_axis=0, tiled=True)  7.89 us
    all_to_all x1, starting transfers between devices, fast(): lax.all_to_all(message, AXES, split_axis=0, concat_axis=0, tiled=True)  7.35 us
    pallas_call x1, Pallas kernels, fast(): call(early_kernel, stats, scratch=state(3), flops=6000000000, name='early')  4.14 us
    pallas_call x1, Pallas kernels, fast(): call(late_kernel, shape((DEVICES, 128), f32), scratch=state(4), flops=300...  3.71 us
    pallas_call x1, Pallas kernels, fast(): call(middle_kernel, stats, scratch=state(4), flops=1500000000, name='midd...  3.05 us
  transfers between devices with their start and end apart: 11, of which 8 were waited for; matrix products, arithmetic and copies ran while one was open for 1% of the time, Pallas kernels for 9%

profile of v8, /device:TPU:1, one launch (start us, length us, event | category | flops | bytes accessed | tf_op | source)
XLA Modules:
  0.0 95.3 jit_solution(2038176281423474607)
XLA Ops:
  0.6 2.8 %prelude.1 = (bf16[1024,896]{1,0:T(8,128)(2,1)S(1)}, s32[8,512]{1,0:T(8,128)S(1)}) custom-call(s32[1,512]{1,0:T(1,128)} %bitcast.75, s32[1,512]{1,0:T(1,128)} %bitcast.64, bf16[512,768]{1,0:T(8,128)(2,1)} %rows.1), custom_call_target="tpu_custom_call" | custom-call | flops 3000000000 | bytes 8000000 | tf_op jit(solution)/shard_map/prelude/pallas_call | solution.py:361
  3.4 38.1 %all_to_all.59 = bf16[128,8,896]{2,1,0:T(8,128)(2,1)S(1)} all-to-all(bf16[128,8,896]{2,1,0:T(8,128)(2,1)S(1)} %bitcast.62), channel_id=1, replica_groups=mesh['grp'=8,'blk'=16] {'grp','blk'}, dimensions={0} | all-to-all | bytes 3670016 | tf_op jit(solution)/shard_map/all_to_all | solution.py:367
  41.5 1.2 %pack_low.1 = (bf16[272,768]{1,0:T(8,128)(2,1)S(1)}, s32[8,1024]{1,0:T(8,128)S(1)}) custom-call(bf16[1024,896]{1,0:T(8,128)(2,1)S(1)} %bitcast.59), custom_call_target="tpu_custom_call" | custom-call | flops 2000000000 | bytes 8000000 | tf_op jit(solution)/shard_map/pack_low/pallas_call | solution.py:368
  42.7 1.0 %collective-permute-start.3 = (bf16[272,768]{1,0:T(8,128)(2,1)S(1)}, bf16[272,768]{1,0:T(8,128)(2,1)S(1)}, u32[]{:S(2)}, u32[]{:S(2)}) collective-permute-start(bf16[272,768]{1,0:T(8,128)(2,1)S(1)} %get-tuple-element.285.low.b0l), channel_id=1, source_target_pairs={{1,0},{2,1},{3,2},{0,3},{5,4},{6,5},{7,6},{4,7},{9,8},{10,9},{11,1... | collective-permute-start | bytes 1253384 | tf_op jit(solution)/shard_map/ppermute | solution.py:355
  43.7 0.6 collective-permute-start.2
  44.3 0.7 pack_high.1.b0h
  45.0 0.7 collective-permute-start.5
  45.7 5.1 %collective-permute-done.3.b2l = bf16[272,768]{1,0:T(8,128)(2,1)S(1)} collective-permute-done((bf16[272,768]{1,0:T(8,128)(2,1)S(1)}, bf16[272,768]{1,0:T(8,128)(2,1)S(1)}, u32[]{:S(2)}, u32[]{:S(2)}) %collective-permute-start.3) | collective-permute-done | bytes 417824 | tf_op jit(solution)/shard_map/ppermute | solution.py:355
  50.9 1.0 %collective-permute-done.2.b1l = bf16[272,768]{1,0:T(8,128)(2,1)S(1)} collective-permute-done((bf16[272,768]{1,0:T(8,128)(2,1)S(1)}, bf16[272,768]{1,0:T(8,128)(2,1)S(1)}, u32[]{:S(2)}, u32[]{:S(2)}) %collective-permute-start.2) | collective-permute-done | bytes 417824 | tf_op jit(solution)/shard_map/ppermute | solution.py:355
  51.8 0.7 collective-permute-start.8
  52.5 2.7 %collective-permute-start.11 = (bf16[352,768]{1,0:T(8,128)(2,1)S(1)}, bf16[352,768]{1,0:T(8,128)(2,1)S(1)}, u32[]{:S(2)}, u32[]{:S(2)}) collective-permute-start(bf16[352,768]{1,0:T(8,128)(2,1)S(1)} %pack_high.1.b0h), channel_id=1, source_target_pairs={{12,0},{13,1},{14,2},{15,3},{0,4},{1,5},{2,6},{3,7},{4,8},{5,9},{6... | collective-permute-start | bytes 1622024 | tf_op jit(solution)/shard_map/ppermute | solution.py:355
  55.2 1.5 %collective-permute-done.5.b2h = bf16[352,768]{1,0:T(8,128)(2,1)S(1)} collective-permute-done((bf16[352,768]{1,0:T(8,128)(2,1)S(1)}, bf16[352,768]{1,0:T(8,128)(2,1)S(1)}, u32[]{:S(2)}, u32[]{:S(2)}) %collective-permute-start.5) | collective-permute-done | bytes 540704 | tf_op jit(solution)/shard_map/ppermute | solution.py:355
  56.6 1.0 %collective-permute-done.4.b1h = bf16[352,768]{1,0:T(8,128)(2,1)S(1)} collective-permute-done((bf16[352,768]{1,0:T(8,128)(2,1)S(1)}, bf16[352,768]{1,0:T(8,128)(2,1)S(1)}, u32[]{:S(2)}, u32[]{:S(2)}) %collective-permute-start.4) | collective-permute-done | bytes 540704 | tf_op jit(solution)/shard_map/ppermute | solution.py:355
  57.6 2.0 %collective-permute-start.10 = (bf16[272,768]{1,0:T(8,128)(2,1)S(1)}, bf16[272,768]{1,0:T(8,128)(2,1)S(1)}, u32[]{:S(2)}, u32[]{:S(2)}) collective-permute-start(bf16[272,768]{1,0:T(8,128)(2,1)S(1)} %get-tuple-element.285.low.b0l), channel_id=1, source_target_pairs={{3,0},{0,1},{1,2},{2,3},{7,4},{4,5},{5,6},{6,7},{11,8},{8,9},{9,10... | collective-permute-start | bytes 1253384 | tf_op jit(solution)/shard_map/ppermute | solution.py:355
  59.6 2.8 %collective-permute-done.6.b3l = bf16[272,768]{1,0:T(8,128)(2,1)S(1)} collective-permute-done((bf16[272,768]{1,0:T(8,128)(2,1)S(1)}, bf16[272,768]{1,0:T(8,128)(2,1)S(1)}, u32[]{:S(2)}, u32[]{:S(2)}) %collective-permute-start.6) | collective-permute-done | bytes 417824 | tf_op jit(solution)/shard_map/ppermute | solution.py:355
  62.8 4.1 %early.1 = (f32[8,640]{1,0:T(8,128)S(1)}, f32[8,640]{1,0:T(8,128)S(1)}) custom-call(bf16[272,768]{1,0:T(8,128)(2,1)S(1)} %get-tuple-element.285.low.b0l, bf16[352,768]{1,0:T(8,128)(2,1)S(1)} %pack_high.1.b0h, bf16[272,768]{1,0:T(8,128)(2,1)S(1)} %collective-permute-done.2.b1l, bf16[352,768]{1,0:T(8,128)(2,1)S(1)} %collective-permute-done.4.b1h, ...), custom_call_target="tpu_custom_call" | custom-call | flops 6000000000 | bytes 8000000 | tf_op jit(solution)/shard_map/early/pallas_call | solution.py:401
  66.9 2.4 %collective-permute-done.10.low = bf16[272,768]{1,0:T(8,128)(2,1)S(1)} collective-permute-done((bf16[272,768]{1,0:T(8,128)(2,1)S(1)}, bf16[272,768]{1,0:T(8,128)(2,1)S(1)}, u32[]{:S(2)}, u32[]{:S(2)}) %collective-permute-start.10) | collective-permute-done | bytes 417824 | tf_op jit(solution)/shard_map/ppermute | solution.py:355
  69.4 3.1 %middle.1 = (f32[8,640]{1,0:T(8,128)S(1)}, f32[8,640]{1,0:T(8,128)S(1)}) custom-call(bf16[272,768]{1,0:T(8,128)(2,1)S(1)} %get-tuple-element.285.low.b0l, bf16[272,768]{1,0:T(8,128)(2,1)S(1)} %collective-permute-done.2.b1l, bf16[352,768]{1,0:T(8,128)(2,1)S(1)} %collective-permute-done.4.b1h, bf16[272,768]{1,0:T(8,128)(2,1)S(1)} %collective-permute-done.3.b2l, ...), custom_call_target="tpu_custom_call" | custom-call | flops 1500000000 | bytes 8000000 | tf_op jit(solution)/shard_map/middle/pallas_call | solution.py:404
  72.4 1.2 %collective-permute-done.7.b3h = bf16[352,768]{1,0:T(8,128)(2,1)S(1)} collective-permute-done((bf16[352,768]{1,0:T(8,128)(2,1)S(1)}, bf16[352,768]{1,0:T(8,128)(2,1)S(1)}, u32[]{:S(2)}, u32[]{:S(2)}) %collective-permute-start.7) | collective-permute-done | bytes 540704 | tf_op jit(solution)/shard_map/ppermute | solution.py:355
  73.6 3.7 %late.1 = f32[128,128]{1,0:T(8,128)} custom-call(bf16[352,768]{1,0:T(8,128)(2,1)S(1)} %pack_high.1.b0h, bf16[272,768]{1,0:T(8,128)(2,1)S(1)} %collective-permute-done.2.b1l, bf16[352,768]{1,0:T(8,128)(2,1)S(1)} %collective-permute-done.4.b1h, bf16[272,768]{1,0:T(8,128)(2,1)S(1)} %collective-permute-done.3.b2l, ...), custom_call_target="tpu_custom_call" | custom-call | flops 3000000000 | bytes 8000000 | tf_op jit(solution)/shard_map/late/pallas_call | solution.py:407
  77.3 7.4 %all-to-all-start.5 = ((f32[128,1,128]{2,1,0:T(1,128)}), f32[128,1,128]{2,1,0:T(1,128)S(1)}, u32[]{:S(2)}, u32[]{:S(2)}) async-start(f32[128,1,128]{2,1,0:T(1,128)} %bitcast.24), calls=%async_computation.5 | async-start | bytes 131072 | tf_op jit(solution)/shard_map/all_to_all | solution.py:414
  85.1 0.6 reduce_max.25
  86.3 7.9 %all-to-all-done.5 = f32[128,1,128]{2,1,0:T(1,128)S(1)} async-done(((f32[128,1,128]{2,1,0:T(1,128)}), f32[128,1,128]{2,1,0:T(1,128)S(1)}, u32[]{:S(2)}, u32[]{:S(2)}) %all-to-all-start.5) | async-done | bytes 65568 | tf_op jit(solution)/shard_map/all_to_all | solution.py:414
  94.2 1.1 %finish.1 = (f32[1,512]{1,0:T(1,128)}, f32[1,512]{1,0:T(1,128)}) custom-call(f32[128,128]{1,0:T(8,128)S(1)} %bitcast.63, s32[8,512]{1,0:T(8,128)S(1)} %get-tuple-element.291.places), custom_call_target="tpu_custom_call" | custom-call | flops 33554432 | bytes 8000000 | tf_op jit(solution)/shard_map/finish/pallas_call | solution.py:415
  (15 shorter events, 0.8 us)
Async XLA Ops:
  42.7 8.1 %collective-permute-start.3 = (bf16[272,768]{1,0:T(8,128)(2,1)S(1)}, bf16[272,768]{1,0:T(8,128)(2,1)S(1)}, u32[]{:S(2)}, u32[]{:S(2)}) collective-permute-start(bf16[272,768]{1,0:T(8,128)(2,1)S(1)} %get-tuple-element.285.low.b0l), channel_id=1, source_target_pairs={{1,0},{2,1},{3,2},{0,3},{5,4},{6,5},{7,6},{4,7},{9,8},{10,9},{11,1... | collective-permute-start | bytes 1253384 | tf_op jit(solution)/shard_map/ppermute | solution.py:355
  43.7 8.1 %collective-permute-start.2 = (bf16[272,768]{1,0:T(8,128)(2,1)S(1)}, bf16[272,768]{1,0:T(8,128)(2,1)S(1)}, u32[]{:S(2)}, u32[]{:S(2)}) collective-permute-start(bf16[272,768]{1,0:T(8,128)(2,1)S(1)} %get-tuple-element.285.low.b0l), channel_id=1, source_target_pairs={{4,0},{5,1},{6,2},{7,3},{8,4},{9,5},{10,6},{11,7},{12,8},{13,9},{1... | collective-permute-start | bytes 1253384 | tf_op jit(solution)/shard_map/ppermute | solution.py:355
  45.0 11.6 %collective-permute-start.5 = (bf16[352,768]{1,0:T(8,128)(2,1)S(1)}, bf16[352,768]{1,0:T(8,128)(2,1)S(1)}, u32[]{:S(2)}, u32[]{:S(2)}) collective-permute-start(bf16[352,768]{1,0:T(8,128)(2,1)S(1)} %pack_high.1.b0h), channel_id=1, source_target_pairs={{1,0},{2,1},{3,2},{0,3},{5,4},{6,5},{7,6},{4,7},{9,8},{10,9},{11,1... | collective-permute-start | bytes 1622024 | tf_op jit(solution)/shard_map/ppermute | solution.py:355
  45.7 11.9 %collective-permute-start.4 = (bf16[352,768]{1,0:T(8,128)(2,1)S(1)}, bf16[352,768]{1,0:T(8,128)(2,1)S(1)}, u32[]{:S(2)}, u32[]{:S(2)}) collective-permute-start(bf16[352,768]{1,0:T(8,128)(2,1)S(1)} %pack_high.1.b0h), channel_id=1, source_target_pairs={{4,0},{5,1},{6,2},{7,3},{8,4},{9,5},{10,6},{11,7},{12,8},{13,9},{1... | collective-permute-start | bytes 1622024 | tf_op jit(solution)/shard_map/ppermute | solution.py:355
  51.8 10.6 %collective-permute-start.6 = (bf16[272,768]{1,0:T(8,128)(2,1)S(1)}, bf16[272,768]{1,0:T(8,128)(2,1)S(1)}, u32[]{:S(2)}, u32[]{:S(2)}) collective-permute-start(bf16[272,768]{1,0:T(8,128)(2,1)S(1)} %collective-permute-done.2.b1l), channel_id=1, source_target_pairs={{4,0},{5,1},{6,2},{7,3},{8,4},{9,5},{10,6},{11,7},{12,8},{13,9},{1... | collective-permute-start | bytes 1253384 | tf_op jit(solution)/shard_map/ppermute | solution.py:355
  51.8 15.1 %collective-permute-start.8 = (bf16[272,768]{1,0:T(8,128)(2,1)S(1)}, bf16[272,768]{1,0:T(8,128)(2,1)S(1)}, u32[]{:S(2)}, u32[]{:S(2)}) collective-permute-start(bf16[272,768]{1,0:T(8,128)(2,1)S(1)} %collective-permute-done.3.b2l), channel_id=1, source_target_pairs={{1,0},{2,1},{3,2},{0,3},{5,4},{6,5},{7,6},{4,7},{9,8},{10,9},{11,1... | collective-permute-start | bytes 1253384 | tf_op jit(solution)/shard_map/ppermute | solution.py:355
  52.5 14.4 %collective-permute-start.11 = (bf16[352,768]{1,0:T(8,128)(2,1)S(1)}, bf16[352,768]{1,0:T(8,128)(2,1)S(1)}, u32[]{:S(2)}, u32[]{:S(2)}) collective-permute-start(bf16[352,768]{1,0:T(8,128)(2,1)S(1)} %pack_high.1.b0h), channel_id=1, source_target_pairs={{12,0},{13,1},{14,2},{15,3},{0,4},{1,5},{2,6},{3,7},{4,8},{5,9},{6... | collective-permute-start | bytes 1622024 | tf_op jit(solution)/shard_map/ppermute | solution.py:355
  57.6 11.7 %collective-permute-start.10 = (bf16[272,768]{1,0:T(8,128)(2,1)S(1)}, bf16[272,768]{1,0:T(8,128)(2,1)S(1)}, u32[]{:S(2)}, u32[]{:S(2)}) collective-permute-start(bf16[272,768]{1,0:T(8,128)(2,1)S(1)} %get-tuple-element.285.low.b0l), channel_id=1, source_target_pairs={{3,0},{0,1},{1,2},{2,3},{7,4},{4,5},{5,6},{6,7},{11,8},{8,9},{9,10... | collective-permute-start | bytes 1253384 | tf_op jit(solution)/shard_map/ppermute | solution.py:355
  59.6 14.0 %collective-permute-start.7 = (bf16[352,768]{1,0:T(8,128)(2,1)S(1)}, bf16[352,768]{1,0:T(8,128)(2,1)S(1)}, u32[]{:S(2)}, u32[]{:S(2)}) collective-permute-start(bf16[352,768]{1,0:T(8,128)(2,1)S(1)} %collective-permute-done.4.b1h), channel_id=1, source_target_pairs={{4,0},{5,1},{6,2},{7,3},{8,4},{9,5},{10,6},{11,7},{12,8},{13,9},{1... | collective-permute-start | bytes 1622024 | tf_op jit(solution)/shard_map/ppermute | solution.py:355
  62.4 11.2 %collective-permute-start.9 = (bf16[352,768]{1,0:T(8,128)(2,1)S(1)}, bf16[352,768]{1,0:T(8,128)(2,1)S(1)}, u32[]{:S(2)}, u32[]{:S(2)}) collective-permute-start(bf16[352,768]{1,0:T(8,128)(2,1)S(1)} %collective-permute-done.5.b2h), channel_id=1, source_target_pairs={{1,0},{2,1},{3,2},{0,3},{5,4},{6,5},{7,6},{4,7},{9,8},{10,9},{11,1... | collective-permute-start | bytes 1622024 | tf_op jit(solution)/shard_map/ppermute | solution.py:355
  77.3 16.9 %copy-start = (s32[512]{0:T(512)S(1)}, s32[512]{0:T(512)}, u32[]{:S(2)}) copy-start(s32[512]{0:T(512)} %param.9) | copy-start | bytes 6148
  77.3 16.9 %copy-start.1 = (bf16[512,768]{1,0:T(8,128)(2,1)S(1)}, bf16[512,768]{1,0:T(8,128)(2,1)}, u32[]{:S(2)}) copy-start(bf16[512,768]{1,0:T(8,128)(2,1)} %rows.1) | copy-start | bytes 2359300
  77.3 16.9 %copy-start.2 = (s32[512]{0:T(512)S(1)}, s32[512]{0:T(512)}, u32[]{:S(2)}) copy-start(s32[512]{0:T(512)} %param.8) | copy-start | bytes 6148
  77.3 16.9 %all-to-all-start.5 = ((f32[128,1,128]{2,1,0:T(1,128)}), f32[128,1,128]{2,1,0:T(1,128)S(1)}, u32[]{:S(2)}, u32[]{:S(2)}) async-start(f32[128,1,128]{2,1,0:T(1,128)} %bitcast.24), calls=%async_computation.5 | async-start | bytes 131072 | tf_op jit(solution)/shard_map/all_to_all | solution.py:414

commit v9 on v8

--- a/solution.py
+++ b/solution.py
@@ -96,7 +96,7 @@
         spread[here, FEAT:] = (matmul(pick, marks, NT) + totals).astype(jnp.bfloat16)
 
 
-def pack_low_kernel(arrived, low, position_out):
+def pack_low_kernel(arrived, low, position_out, names_out):
     tails = arrived[:, FEAT:]
     at, line = iota((8, HELD), 1), iota((8, HELD), 0)
     clusters = matmul((iota((8, 128), 1) == 0).astype(jnp.bfloat16), tails, NT)
@@ -106,18 +106,23 @@
     position = jnp.where(held, position, -1.0).astype(jnp.int32)
     position_out[...] = position
     names = jnp.where(line == 1, (at >> 3) + 1, jnp.where(line == 2, at & 7, 0))
-    names = jnp.where(line == 0, clusters, names.astype(jnp.float32)).astype(jnp.bfloat16)
-    pick = (iota((BLOCK, HELD), 0) == position[0:1]).astype(jnp.bfloat16)
-    low[:LOW, :] = matmul(pick[:LOW], arrived[:, :FEAT], NN).astype(jnp.bfloat16)
-    named = matmul(names, pick, NT)
-    named = jnp.concatenate([named, jnp.zeros((8, FEAT - BLOCK), jnp.float32)], axis=1)
+    names = jnp.where(line == 0, clusters, names.astype(jnp.float32))
+    names_out[...] = names
+    pick = (iota((LOW, HELD), 0) == position[0:1]).astype(jnp.bfloat16)
+    low[:LOW, :] = matmul(pick, arrived[:, :FEAT], NN).astype(jnp.bfloat16)
+    named = matmul(names.astype(jnp.bfloat16), pick, NT)
+    named = jnp.concatenate([named, jnp.zeros((8, FEAT - LOW), jnp.float32)], axis=1)
     low[LOW:, :] = jnp.concatenate([named, jnp.zeros_like(named)], axis=0).astype(jnp.bfloat16)
 
 
-def pack_high_kernel(arrived, low, position, high):
-    pick = (iota((ROOM - LOW, HELD), 0) + LOW == position[0:1, :]).astype(jnp.bfloat16)
-    high[: ROOM - LOW, :] = matmul(pick, arrived[:, :FEAT], NN).astype(jnp.bfloat16)
-    high[ROOM - LOW :, :] = low[LOW:, :]
+def pack_high_kernel(arrived, low, position, names, high):
+    pick = (iota((BLOCK - LOW, HELD), 0) + LOW == position[0:1, :]).astype(jnp.bfloat16)
+    high[: ROOM - LOW, :] = matmul(pick[: ROOM - LOW], arrived[:, :FEAT], NN).astype(jnp.bfloat16)
+    named = matmul(names[...].astype(jnp.bfloat16), pick, NT)
+    named = jnp.concatenate([named, jnp.zeros_like(named)], axis=0).astype(jnp.bfloat16)
+    high[ROOM - LOW :, :LOW] = low[LOW:, :LOW]
+    high[ROOM - LOW :, LOW:BLOCK] = named
+    high[ROOM - LOW :, BLOCK:] = jnp.zeros((16, FEAT - BLOCK), jnp.bfloat16)
 
 
 def over_kernel(arrived, over):
@@ -365,15 +370,15 @@
         name="prelude",
     )(labels.reshape(1, ROWS), cluster_slot.reshape(1, ROWS), embeddings)
     arrived = lax.all_to_all(spread, AXES, split_axis=0, concat_axis=0, tiled=True)
-    b0l, position = call(
+    b0l, position, names = call(
         pack_low_kernel,
-        (shape((LOW_SENT, FEAT), bf16), shape((8, HELD), i32)),
+        (shape((LOW_SENT, FEAT), bf16), shape((8, HELD), i32), shape((8, HELD), f32)),
         flops=2_000_000_000,
         name="pack_low",
     )(arrived)
     b0h = call(
         pack_high_kernel, shape((HIGH_SENT, FEAT), bf16), flops=1_000_000_000, name="pack_high"
-    )(arrived, b0l, position)
+    )(arrived, b0l, position, names)
     b1l = from_spot(b0l, 1, 0)
     b2l = from_spot(b0l, 0, 1)
     b1h = from_spot(b0h, 1, 0)

time: 95.5 us -> 95.4 us (level)
  no operation moved by 1% of the time
where the time goes in v9:
time: 95.4 us; the launch traced here: 95.2 us
  blocking collectives  38.1 us (40%)
  waiting for transfers between devices  22.7 us (24%)
  Pallas kernels  17 us (18%)
  starting transfers between devices  15.4 us (16%)
  between operations  1.35 us (1%)
    all_to_all x1, blocking collectives, fast(): lax.all_to_all(spread, AXES, split_axis=0, concat_axis=0, tiled=True)  38.1 us
    ppermute x10, waiting for transfers between devices, from_spot(): return lax.ppermute(x, AXES, hop(dy, dz))  14.8 us
    ppermute x10, starting transfers between devices, from_spot(): return lax.ppermute(x, AXES, hop(dy, dz))  8.04 us
    all_to_all x1, waiting for transfers between devices, fast(): lax.all_to_all(message, AXES, split_axis=0, concat_axis=0, tiled=True)  7.89 us
    all_to_all x1, starting transfers between devices, fast(): lax.all_to_all(message, AXES, split_axis=0, concat_axis=0, tiled=True)  7.36 us
    pallas_call x1, Pallas kernels, fast(): call(early_kernel, stats, scratch=state(3), flops=6000000000, name='early')  4.12 us
    pallas_call x1, Pallas kernels, fast(): call(late_kernel, shape((DEVICES, 128), f32), scratch=state(4), flops=300...  3.71 us
    pallas_call x1, Pallas kernels, fast(): call(middle_kernel, stats, scratch=state(4), flops=1500000000, name='midd...  3.05 us
  transfers between devices with their start and end apart: 11, of which 8 were waited for; matrix products, arithmetic and copies ran while one was open for 1% of the time, Pallas kernels for 9%

profile of v9, /device:TPU:1, one launch (start us, length us, event | category | flops | bytes accessed | tf_op | source)
XLA Modules:
  0.0 95.2 jit_solution(9760492429063341212)
XLA Ops:
  0.6 2.8 %prelude.1 = (bf16[1024,896]{1,0:T(8,128)(2,1)S(1)}, s32[8,512]{1,0:T(8,128)S(1)}) custom-call(s32[1,512]{1,0:T(1,128)} %bitcast.75, s32[1,512]{1,0:T(1,128)} %bitcast.64, bf16[512,768]{1,0:T(8,128)(2,1)} %rows.1), custom_call_target="tpu_custom_call" | custom-call | flops 3000000000 | bytes 8000000 | tf_op jit(solution)/shard_map/prelude/pallas_call | solution.py:366
  3.4 38.1 %all_to_all.59 = bf16[128,8,896]{2,1,0:T(8,128)(2,1)S(1)} all-to-all(bf16[128,8,896]{2,1,0:T(8,128)(2,1)S(1)} %bitcast.62), channel_id=1, replica_groups=mesh['grp'=8,'blk'=16] {'grp','blk'}, dimensions={0} | all-to-all | bytes 3670016 | tf_op jit(solution)/shard_map/all_to_all | solution.py:372
  41.5 1.0 %pack_low.1 = (bf16[272,768]{1,0:T(8,128)(2,1)S(1)}, s32[8,1024]{1,0:T(8,128)S(1)}, f32[8,1024]{1,0:T(8,128)S(1)}) custom-call(bf16[1024,896]{1,0:T(8,128)(2,1)S(1)} %bitcast.59), custom_call_target="tpu_custom_call" | custom-call | flops 2000000000 | bytes 8000000 | tf_op jit(solution)/shard_map/pack_low/pallas_call | solution.py:373
  42.5 1.1 %collective-permute-start.3 = (bf16[272,768]{1,0:T(8,128)(2,1)S(1)}, bf16[272,768]{1,0:T(8,128)(2,1)S(1)}, u32[]{:S(2)}, u32[]{:S(2)}) collective-permute-start(bf16[272,768]{1,0:T(8,128)(2,1)S(1)} %get-tuple-element.287.low.b0l), channel_id=1, source_target_pairs={{1,0},{2,1},{3,2},{0,3},{5,4},{6,5},{7,6},{4,7},{9,8},{10,9},{11,1... | collective-permute-start | bytes 1253384 | tf_op jit(solution)/shard_map/ppermute | solution.py:360
  43.6 0.6 collective-permute-start.2
  44.1 0.9 pack_high.1.b0h
  45.0 0.7 collective-permute-start.5
  45.8 4.9 %collective-permute-done.3.b2l = bf16[272,768]{1,0:T(8,128)(2,1)S(1)} collective-permute-done((bf16[272,768]{1,0:T(8,128)(2,1)S(1)}, bf16[272,768]{1,0:T(8,128)(2,1)S(1)}, u32[]{:S(2)}, u32[]{:S(2)}) %collective-permute-start.3) | collective-permute-done | bytes 417824 | tf_op jit(solution)/shard_map/ppermute | solution.py:360
  50.7 1.0 %collective-permute-done.2.b1l = bf16[272,768]{1,0:T(8,128)(2,1)S(1)} collective-permute-done((bf16[272,768]{1,0:T(8,128)(2,1)S(1)}, bf16[272,768]{1,0:T(8,128)(2,1)S(1)}, u32[]{:S(2)}, u32[]{:S(2)}) %collective-permute-start.2) | collective-permute-done | bytes 417824 | tf_op jit(solution)/shard_map/ppermute | solution.py:360
  51.7 0.7 collective-permute-start.8
  52.3 2.7 %collective-permute-start.11 = (bf16[352,768]{1,0:T(8,128)(2,1)S(1)}, bf16[352,768]{1,0:T(8,128)(2,1)S(1)}, u32[]{:S(2)}, u32[]{:S(2)}) collective-permute-start(bf16[352,768]{1,0:T(8,128)(2,1)S(1)} %pack_high.1.b0h), channel_id=1, source_target_pairs={{12,0},{13,1},{14,2},{15,3},{0,4},{1,5},{2,6},{3,7},{4,8},{5,9},{6... | collective-permute-start | bytes 1622024 | tf_op jit(solution)/shard_map/ppermute | solution.py:360
  55.0 1.5 %collective-permute-done.5.b2h = bf16[352,768]{1,0:T(8,128)(2,1)S(1)} collective-permute-done((bf16[352,768]{1,0:T(8,128)(2,1)S(1)}, bf16[352,768]{1,0:T(8,128)(2,1)S(1)}, u32[]{:S(2)}, u32[]{:S(2)}) %collective-permute-start.5) | collective-permute-done | bytes 540704 | tf_op jit(solution)/shard_map/ppermute | solution.py:360
  56.5 1.0 %collective-permute-done.4.b1h = bf16[352,768]{1,0:T(8,128)(2,1)S(1)} collective-permute-done((bf16[352,768]{1,0:T(8,128)(2,1)S(1)}, bf16[352,768]{1,0:T(8,128)(2,1)S(1)}, u32[]{:S(2)}, u32[]{:S(2)}) %collective-permute-start.4) | collective-permute-done | bytes 540704 | tf_op jit(solution)/shard_map/ppermute | solution.py:360
  57.5 2.0 %collective-permute-start.10 = (bf16[272,768]{1,0:T(8,128)(2,1)S(1)}, bf16[272,768]{1,0:T(8,128)(2,1)S(1)}, u32[]{:S(2)}, u32[]{:S(2)}) collective-permute-start(bf16[272,768]{1,0:T(8,128)(2,1)S(1)} %get-tuple-element.287.low.b0l), channel_id=1, source_target_pairs={{3,0},{0,1},{1,2},{2,3},{7,4},{4,5},{5,6},{6,7},{11,8},{8,9},{9,10... | collective-permute-start | bytes 1253384 | tf_op jit(solution)/shard_map/ppermute | solution.py:360
  59.5 2.8 %collective-permute-done.6.b3l = bf16[272,768]{1,0:T(8,128)(2,1)S(1)} collective-permute-done((bf16[272,768]{1,0:T(8,128)(2,1)S(1)}, bf16[272,768]{1,0:T(8,128)(2,1)S(1)}, u32[]{:S(2)}, u32[]{:S(2)}) %collective-permute-start.6) | collective-permute-done | bytes 417824 | tf_op jit(solution)/shard_map/ppermute | solution.py:360
  62.6 4.1 %early.1 = (f32[8,640]{1,0:T(8,128)S(1)}, f32[8,640]{1,0:T(8,128)S(1)}) custom-call(bf16[272,768]{1,0:T(8,128)(2,1)S(1)} %get-tuple-element.287.low.b0l, bf16[352,768]{1,0:T(8,128)(2,1)S(1)} %pack_high.1.b0h, bf16[272,768]{1,0:T(8,128)(2,1)S(1)} %collective-permute-done.2.b1l, bf16[352,768]{1,0:T(8,128)(2,1)S(1)} %collective-permute-done.4.b1h, ...), custom_call_target="tpu_custom_call" | custom-call | flops 6000000000 | bytes 8000000 | tf_op jit(solution)/shard_map/early/pallas_call | solution.py:406
  66.8 2.4 %collective-permute-done.10.low = bf16[272,768]{1,0:T(8,128)(2,1)S(1)} collective-permute-done((bf16[272,768]{1,0:T(8,128)(2,1)S(1)}, bf16[272,768]{1,0:T(8,128)(2,1)S(1)}, u32[]{:S(2)}, u32[]{:S(2)}) %collective-permute-start.10) | collective-permute-done | bytes 417824 | tf_op jit(solution)/shard_map/ppermute | solution.py:360
  69.2 3.0 %middle.1 = (f32[8,640]{1,0:T(8,128)S(1)}, f32[8,640]{1,0:T(8,128)S(1)}) custom-call(bf16[272,768]{1,0:T(8,128)(2,1)S(1)} %get-tuple-element.287.low.b0l, bf16[272,768]{1,0:T(8,128)(2,1)S(1)} %collective-permute-done.2.b1l, bf16[352,768]{1,0:T(8,128)(2,1)S(1)} %collective-permute-done.4.b1h, bf16[272,768]{1,0:T(8,128)(2,1)S(1)} %collective-permute-done.3.b2l, ...), custom_call_target="tpu_custom_call" | custom-call | flops 1500000000 | bytes 8000000 | tf_op jit(solution)/shard_map/middle/pallas_call | solution.py:409
  72.2 1.2 %collective-permute-done.7.b3h = bf16[352,768]{1,0:T(8,128)(2,1)S(1)} collective-permute-done((bf16[352,768]{1,0:T(8,128)(2,1)S(1)}, bf16[352,768]{1,0:T(8,128)(2,1)S(1)}, u32[]{:S(2)}, u32[]{:S(2)}) %collective-permute-start.7) | collective-permute-done | bytes 540704 | tf_op jit(solution)/shard_map/ppermute | solution.py:360
  73.4 3.7 %late.1 = f32[128,128]{1,0:T(8,128)} custom-call(bf16[352,768]{1,0:T(8,128)(2,1)S(1)} %pack_high.1.b0h, bf16[272,768]{1,0:T(8,128)(2,1)S(1)} %collective-permute-done.2.b1l, bf16[352,768]{1,0:T(8,128)(2,1)S(1)} %collective-permute-done.4.b1h, bf16[272,768]{1,0:T(8,128)(2,1)S(1)} %collective-permute-done.3.b2l, ...), custom_call_target="tpu_custom_call" | custom-call | flops 3000000000 | bytes 8000000 | tf_op jit(solution)/shard_map/late/pallas_call | solution.py:412
  77.2 7.4 %all-to-all-start.5 = ((f32[128,1,128]{2,1,0:T(1,128)}), f32[128,1,128]{2,1,0:T(1,128)S(1)}, u32[]{:S(2)}, u32[]{:S(2)}) async-start(f32[128,1,128]{2,1,0:T(1,128)} %bitcast.24), calls=%async_computation.5 | async-start | bytes 131072 | tf_op jit(solution)/shard_map/all_to_all | solution.py:419
  84.9 0.6 reduce_max.25
  86.2 7.9 %all-to-all-done.5 = f32[128,1,128]{2,1,0:T(1,128)S(1)} async-done(((f32[128,1,128]{2,1,0:T(1,128)}), f32[128,1,128]{2,1,0:T(1,128)S(1)}, u32[]{:S(2)}, u32[]{:S(2)}) %all-to-all-start.5) | async-done | bytes 65568 | tf_op jit(solution)/shard_map/all_to_all | solution.py:419
  94.1 1.1 %finish.1 = (f32[1,512]{1,0:T(1,128)}, f32[1,512]{1,0:T(1,128)}) custom-call(f32[128,128]{1,0:T(8,128)S(1)} %bitcast.63, s32[8,512]{1,0:T(8,128)S(1)} %get-tuple-element.293.places), custom_call_target="tpu_custom_call" | custom-call | flops 33554432 | bytes 8000000 | tf_op jit(solution)/shard_map/finish/pallas_call | solution.py:420
  (15 shorter events, 0.8 us)
Async XLA Ops:
  42.5 8.2 %collective-permute-start.3 = (bf16[272,768]{1,0:T(8,128)(2,1)S(1)}, bf16[272,768]{1,0:T(8,128)(2,1)S(1)}, u32[]{:S(2)}, u32[]{:S(2)}) collective-permute-start(bf16[272,768]{1,0:T(8,128)(2,1)S(1)} %get-tuple-element.287.low.b0l), channel_id=1, source_target_pairs={{1,0},{2,1},{3,2},{0,3},{5,4},{6,5},{7,6},{4,7},{9,8},{10,9},{11,1... | collective-permute-start | bytes 1253384 | tf_op jit(solution)/shard_map/ppermute | solution.py:360
  43.6 8.1 %collective-permute-start.2 = (bf16[272,768]{1,0:T(8,128)(2,1)S(1)}, bf16[272,768]{1,0:T(8,128)(2,1)S(1)}, u32[]{:S(2)}, u32[]{:S(2)}) collective-permute-start(bf16[272,768]{1,0:T(8,128)(2,1)S(1)} %get-tuple-element.287.low.b0l), channel_id=1, source_target_pairs={{4,0},{5,1},{6,2},{7,3},{8,4},{9,5},{10,6},{11,7},{12,8},{13,9},{1... | collective-permute-start | bytes 1253384 | tf_op jit(solution)/shard_map/ppermute | solution.py:360
  45.0 11.5 %collective-permute-start.5 = (bf16[352,768]{1,0:T(8,128)(2,1)S(1)}, bf16[352,768]{1,0:T(8,128)(2,1)S(1)}, u32[]{:S(2)}, u32[]{:S(2)}) collective-permute-start(bf16[352,768]{1,0:T(8,128)(2,1)S(1)} %pack_high.1.b0h), channel_id=1, source_target_pairs={{1,0},{2,1},{3,2},{0,3},{5,4},{6,5},{7,6},{4,7},{9,8},{10,9},{11,1... | collective-permute-start | bytes 1622024 | tf_op jit(solution)/shard_map/ppermute | solution.py:360
  45.7 11.7 %collective-permute-start.4 = (bf16[352,768]{1,0:T(8,128)(2,1)S(1)}, bf16[352,768]{1,0:T(8,128)(2,1)S(1)}, u32[]{:S(2)}, u32[]{:S(2)}) collective-permute-start(bf16[352,768]{1,0:T(8,128)(2,1)S(1)} %pack_high.1.b0h), channel_id=1, source_target_pairs={{4,0},{5,1},{6,2},{7,3},{8,4},{9,5},{10,6},{11,7},{12,8},{13,9},{1... | collective-permute-start | bytes 1622024 | tf_op jit(solution)/shard_map/ppermute | solution.py:360
  51.7 10.6 %collective-permute-start.6 = (bf16[272,768]{1,0:T(8,128)(2,1)S(1)}, bf16[272,768]{1,0:T(8,128)(2,1)S(1)}, u32[]{:S(2)}, u32[]{:S(2)}) collective-permute-start(bf16[272,768]{1,0:T(8,128)(2,1)S(1)} %collective-permute-done.2.b1l), channel_id=1, source_target_pairs={{4,0},{5,1},{6,2},{7,3},{8,4},{9,5},{10,6},{11,7},{12,8},{13,9},{1... | collective-permute-start | bytes 1253384 | tf_op jit(solution)/shard_map/ppermute | solution.py:360
  51.7 15.1 %collective-permute-start.8 = (bf16[272,768]{1,0:T(8,128)(2,1)S(1)}, bf16[272,768]{1,0:T(8,128)(2,1)S(1)}, u32[]{:S(2)}, u32[]{:S(2)}) collective-permute-start(bf16[272,768]{1,0:T(8,128)(2,1)S(1)} %collective-permute-done.3.b2l), channel_id=1, source_target_pairs={{1,0},{2,1},{3,2},{0,3},{5,4},{6,5},{7,6},{4,7},{9,8},{10,9},{11,1... | collective-permute-start | bytes 1253384 | tf_op jit(solution)/shard_map/ppermute | solution.py:360
  52.3 14.4 %collective-permute-start.11 = (bf16[352,768]{1,0:T(8,128)(2,1)S(1)}, bf16[352,768]{1,0:T(8,128)(2,1)S(1)}, u32[]{:S(2)}, u32[]{:S(2)}) collective-permute-start(bf16[352,768]{1,0:T(8,128)(2,1)S(1)} %pack_high.1.b0h), channel_id=1, source_target_pairs={{12,0},{13,1},{14,2},{15,3},{0,4},{1,5},{2,6},{3,7},{4,8},{5,9},{6... | collective-permute-start | bytes 1622024 | tf_op jit(solution)/shard_map/ppermute | solution.py:360
  57.5 11.7 %collective-permute-start.10 = (bf16[272,768]{1,0:T(8,128)(2,1)S(1)}, bf16[272,768]{1,0:T(8,128)(2,1)S(1)}, u32[]{:S(2)}, u32[]{:S(2)}) collective-permute-start(bf16[272,768]{1,0:T(8,128)(2,1)S(1)} %get-tuple-element.287.low.b0l), channel_id=1, source_target_pairs={{3,0},{0,1},{1,2},{2,3},{7,4},{4,5},{5,6},{6,7},{11,8},{8,9},{9,10... | collective-permute-start | bytes 1253384 | tf_op jit(solution)/shard_map/ppermute | solution.py:360
  59.5 14.0 %collective-permute-start.7 = (bf16[352,768]{1,0:T(8,128)(2,1)S(1)}, bf16[352,768]{1,0:T(8,128)(2,1)S(1)}, u32[]{:S(2)}, u32[]{:S(2)}) collective-permute-start(bf16[352,768]{1,0:T(8,128)(2,1)S(1)} %collective-permute-done.4.b1h), channel_id=1, source_target_pairs={{4,0},{5,1},{6,2},{7,3},{8,4},{9,5},{10,6},{11,7},{12,8},{13,9},{1... | collective-permute-start | bytes 1622024 | tf_op jit(solution)/shard_map/ppermute | solution.py:360
  62.2 11.2 %collective-permute-start.9 = (bf16[352,768]{1,0:T(8,128)(2,1)S(1)}, bf16[352,768]{1,0:T(8,128)(2,1)S(1)}, u32[]{:S(2)}, u32[]{:S(2)}) collective-permute-start(bf16[352,768]{1,0:T(8,128)(2,1)S(1)} %collective-permute-done.5.b2h), channel_id=1, source_target_pairs={{1,0},{2,1},{3,2},{0,3},{5,4},{6,5},{7,6},{4,7},{9,8},{10,9},{11,1... | collective-permute-start | bytes 1622024 | tf_op jit(solution)/shard_map/ppermute | solution.py:360
  77.2 16.9 %copy-start = (s32[512]{0:T(512)S(1)}, s32[512]{0:T(512)}, u32[]{:S(2)}) copy-start(s32[512]{0:T(512)} %param.9) | copy-start | bytes 6148
  77.2 16.9 %copy-start.1 = (bf16[512,768]{1,0:T(8,128)(2,1)S(1)}, bf16[512,768]{1,0:T(8,128)(2,1)}, u32[]{:S(2)}) copy-start(bf16[512,768]{1,0:T(8,128)(2,1)} %rows.1) | copy-start | bytes 2359300
  77.2 16.9 %copy-start.2 = (s32[512]{0:T(512)S(1)}, s32[512]{0:T(512)}, u32[]{:S(2)}) copy-start(s32[512]{0:T(512)} %param.8) | copy-start | bytes 6148
  77.2 16.9 %all-to-all-start.5 = ((f32[128,1,128]{2,1,0:T(1,128)}), f32[128,1,128]{2,1,0:T(1,128)S(1)}, u32[]{:S(2)}, u32[]{:S(2)}) async-start(f32[128,1,128]{2,1,0:T(1,128)} %bitcast.24), calls=%async_computation.5 | async-start | bytes 131072 | tf_op jit(solution)/shard_map/all_to_all | solution.py:419

commit v10 on v9

--- a/solution.py
+++ b/solution.py
@@ -86,7 +86,7 @@
     marks = jnp.where(lanes == 0, found[1:2] + 1.0, 0.0).astype(jnp.bfloat16)
     goal = holder * SHARE + turn
     totals = matmul(
-        jnp.ones((128, ROWS), jnp.bfloat16), (lanes - 64 == group).astype(jnp.bfloat16), NT
+        jnp.ones((8, ROWS), jnp.bfloat16), (lanes - 64 == group).astype(jnp.bfloat16), NT
     )
     totals = jnp.where((iota((ROWS, 128), 0) & (SHARE - 1)) == 0, totals[0:1], 0.0)
     for t in range(0, HELD, ROWS):
@@ -389,8 +389,8 @@
     b4l = from_spot(b2l, 0, 1)
     low, b1h, b2h = lax.optimization_barrier((b0l, b1h, b2h))
     over = call(over_kernel, shape((8, 128), i32), flops=10_000_000, name="over")(arrived)
+    b4h = from_spot(b2h, 0, 1)
     b3h = from_spot(b1h, 1, 0)
-    b4h = from_spot(b2h, 0, 1)
     low = from_spot(low, 0, 3)
 
     def state(places):

time: 95.4 us -> 95.3 us (level)
  no operation moved by 1% of the time
where the time goes in v10:
time: 95.3 us; the launch traced here: 95.2 us
  blocking collectives  38.1 us (40%)
  waiting for transfers between devices  22.7 us (24%)
  Pallas kernels  17 us (18%)
  starting transfers between devices  15.4 us (16%)
  between operations  1.35 us (1%)
    all_to_all x1, blocking collectives, fast(): lax.all_to_all(spread, AXES, split_axis=0, concat_axis=0, tiled=True)  38.1 us
    ppermute x10, waiting for transfers between devices, from_spot(): return lax.ppermute(x, AXES, hop(dy, dz))  14.8 us
    ppermute x10, starting transfers between devices, from_spot(): return lax.ppermute(x, AXES, hop(dy, dz))  8.03 us
    all_to_all x1, waiting for transfers between devices, fast(): lax.all_to_all(message, AXES, split_axis=0, concat_axis=0, tiled=True)  7.9 us
    all_to_all x1, starting transfers between devices, fast(): lax.all_to_all(message, AXES, split_axis=0, concat_axis=0, tiled=True)  7.35 us
    pallas_call x1, Pallas kernels, fast(): call(early_kernel, stats, scratch=state(3), flops=6000000000, name='early')  4.13 us
    pallas_call x1, Pallas kernels, fast(): call(late_kernel, shape((DEVICES, 128), f32), scratch=state(4), flops=300...  3.71 us
    pallas_call x1, Pallas kernels, fast(): call(middle_kernel, stats, scratch=state(4), flops=1500000000, name='midd...  3.04 us
  transfers between devices with their start and end apart: 11, of which 8 were waited for; matrix products, arithmetic and copies ran while one was open for 1% of the time, Pallas kernels for 9%

profile of v10, /device:TPU:1, one launch (start us, length us, event | category | flops | bytes accessed | tf_op | source)
XLA Modules:
  0.0 95.2 jit_solution(9873153346939241801)
XLA Ops:
  0.6 2.8 %prelude.1 = (bf16[1024,896]{1,0:T(8,128)(2,1)S(1)}, s32[8,512]{1,0:T(8,128)S(1)}) custom-call(s32[1,512]{1,0:T(1,128)} %bitcast.75, s32[1,512]{1,0:T(1,128)} %bitcast.64, bf16[512,768]{1,0:T(8,128)(2,1)} %rows.1), custom_call_target="tpu_custom_call" | custom-call | flops 3000000000 | bytes 8000000 | tf_op jit(solution)/shard_map/prelude/pallas_call | solution.py:366
  3.4 38.1 %all_to_all.59 = bf16[128,8,896]{2,1,0:T(8,128)(2,1)S(1)} all-to-all(bf16[128,8,896]{2,1,0:T(8,128)(2,1)S(1)} %bitcast.62), channel_id=1, replica_groups=mesh['grp'=8,'blk'=16] {'grp','blk'}, dimensions={0} | all-to-all | bytes 3670016 | tf_op jit(solution)/shard_map/all_to_all | solution.py:372
  41.5 1.0 %pack_low.1 = (bf16[272,768]{1,0:T(8,128)(2,1)S(1)}, s32[8,1024]{1,0:T(8,128)S(1)}, f32[8,1024]{1,0:T(8,128)S(1)}) custom-call(bf16[1024,896]{1,0:T(8,128)(2,1)S(1)} %bitcast.59), custom_call_target="tpu_custom_call" | custom-call | flops 2000000000 | bytes 8000000 | tf_op jit(solution)/shard_map/pack_low/pallas_call | solution.py:373
  42.5 1.1 %collective-permute-start.3 = (bf16[272,768]{1,0:T(8,128)(2,1)S(1)}, bf16[272,768]{1,0:T(8,128)(2,1)S(1)}, u32[]{:S(2)}, u32[]{:S(2)}) collective-permute-start(bf16[272,768]{1,0:T(8,128)(2,1)S(1)} %get-tuple-element.287.low.b0l), channel_id=1, source_target_pairs={{1,0},{2,1},{3,2},{0,3},{5,4},{6,5},{7,6},{4,7},{9,8},{10,9},{11,1... | collective-permute-start | bytes 1253384 | tf_op jit(solution)/shard_map/ppermute | solution.py:360
  43.6 0.6 collective-permute-start.2
  44.1 0.9 pack_high.1.b0h
  45.0 0.7 collective-permute-start.5
  45.7 4.9 %collective-permute-done.3.b2l = bf16[272,768]{1,0:T(8,128)(2,1)S(1)} collective-permute-done((bf16[272,768]{1,0:T(8,128)(2,1)S(1)}, bf16[272,768]{1,0:T(8,128)(2,1)S(1)}, u32[]{:S(2)}, u32[]{:S(2)}) %collective-permute-start.3) | collective-permute-done | bytes 417824 | tf_op jit(solution)/shard_map/ppermute | solution.py:360
  50.7 1.0 %collective-permute-done.2.b1l = bf16[272,768]{1,0:T(8,128)(2,1)S(1)} collective-permute-done((bf16[272,768]{1,0:T(8,128)(2,1)S(1)}, bf16[272,768]{1,0:T(8,128)(2,1)S(1)}, u32[]{:S(2)}, u32[]{:S(2)}) %collective-permute-start.2) | collective-permute-done | bytes 417824 | tf_op jit(solution)/shard_map/ppermute | solution.py:360
  51.7 0.7 collective-permute-start.8
  52.3 2.7 %collective-permute-start.11 = (bf16[352,768]{1,0:T(8,128)(2,1)S(1)}, bf16[352,768]{1,0:T(8,128)(2,1)S(1)}, u32[]{:S(2)}, u32[]{:S(2)}) collective-permute-start(bf16[352,768]{1,0:T(8,128)(2,1)S(1)} %pack_high.1.b0h), channel_id=1, source_target_pairs={{12,0},{13,1},{14,2},{15,3},{0,4},{1,5},{2,6},{3,7},{4,8},{5,9},{6... | collective-permute-start | bytes 1622024 | tf_op jit(solution)/shard_map/ppermute | solution.py:360
  55.0 1.5 %collective-permute-done.5.b2h = bf16[352,768]{1,0:T(8,128)(2,1)S(1)} collective-permute-done((bf16[352,768]{1,0:T(8,128)(2,1)S(1)}, bf16[352,768]{1,0:T(8,128)(2,1)S(1)}, u32[]{:S(2)}, u32[]{:S(2)}) %collective-permute-start.5) | collective-permute-done | bytes 540704 | tf_op jit(solution)/shard_map/ppermute | solution.py:360
  56.5 1.0 %collective-permute-done.4.b1h = bf16[352,768]{1,0:T(8,128)(2,1)S(1)} collective-permute-done((bf16[352,768]{1,0:T(8,128)(2,1)S(1)}, bf16[352,768]{1,0:T(8,128)(2,1)S(1)}, u32[]{:S(2)}, u32[]{:S(2)}) %collective-permute-start.4) | collective-permute-done | bytes 540704 | tf_op jit(solution)/shard_map/ppermute | solution.py:360
  57.5 2.0 %collective-permute-start.10 = (bf16[272,768]{1,0:T(8,128)(2,1)S(1)}, bf16[272,768]{1,0:T(8,128)(2,1)S(1)}, u32[]{:S(2)}, u32[]{:S(2)}) collective-permute-start(bf16[272,768]{1,0:T(8,128)(2,1)S(1)} %get-tuple-element.287.low.b0l), channel_id=1, source_target_pairs={{3,0},{0,1},{1,2},{2,3},{7,4},{4,5},{5,6},{6,7},{11,8},{8,9},{9,10... | collective-permute-start | bytes 1253384 | tf_op jit(solution)/shard_map/ppermute | solution.py:360
  59.5 2.8 %collective-permute-done.6.b3l = bf16[272,768]{1,0:T(8,128)(2,1)S(1)} collective-permute-done((bf16[272,768]{1,0:T(8,128)(2,1)S(1)}, bf16[272,768]{1,0:T(8,128)(2,1)S(1)}, u32[]{:S(2)}, u32[]{:S(2)}) %collective-permute-start.6) | collective-permute-done | bytes 417824 | tf_op jit(solution)/shard_map/ppermute | solution.py:360
  62.6 4.1 %early.1 = (f32[8,640]{1,0:T(8,128)S(1)}, f32[8,640]{1,0:T(8,128)S(1)}) custom-call(bf16[272,768]{1,0:T(8,128)(2,1)S(1)} %get-tuple-element.287.low.b0l, bf16[352,768]{1,0:T(8,128)(2,1)S(1)} %pack_high.1.b0h, bf16[272,768]{1,0:T(8,128)(2,1)S(1)} %collective-permute-done.2.b1l, bf16[352,768]{1,0:T(8,128)(2,1)S(1)} %collective-permute-done.4.b1h, ...), custom_call_target="tpu_custom_call" | custom-call | flops 6000000000 | bytes 8000000 | tf_op jit(solution)/shard_map/early/pallas_call | solution.py:406
  66.8 2.4 %collective-permute-done.10.low = bf16[272,768]{1,0:T(8,128)(2,1)S(1)} collective-permute-done((bf16[272,768]{1,0:T(8,128)(2,1)S(1)}, bf16[272,768]{1,0:T(8,128)(2,1)S(1)}, u32[]{:S(2)}, u32[]{:S(2)}) %collective-permute-start.10) | collective-permute-done | bytes 417824 | tf_op jit(solution)/shard_map/ppermute | solution.py:360
  69.2 3.0 %middle.1 = (f32[8,640]{1,0:T(8,128)S(1)}, f32[8,640]{1,0:T(8,128)S(1)}) custom-call(bf16[272,768]{1,0:T(8,128)(2,1)S(1)} %get-tuple-element.287.low.b0l, bf16[272,768]{1,0:T(8,128)(2,1)S(1)} %collective-permute-done.2.b1l, bf16[352,768]{1,0:T(8,128)(2,1)S(1)} %collective-permute-done.4.b1h, bf16[272,768]{1,0:T(8,128)(2,1)S(1)} %collective-permute-done.3.b2l, ...), custom_call_target="tpu_custom_call" | custom-call | flops 1500000000 | bytes 8000000 | tf_op jit(solution)/shard_map/middle/pallas_call | solution.py:409
  72.2 1.2 %collective-permute-done.7.b3h = bf16[352,768]{1,0:T(8,128)(2,1)S(1)} collective-permute-done((bf16[352,768]{1,0:T(8,128)(2,1)S(1)}, bf16[352,768]{1,0:T(8,128)(2,1)S(1)}, u32[]{:S(2)}, u32[]{:S(2)}) %collective-permute-start.7) | collective-permute-done | bytes 540704 | tf_op jit(solution)/shard_map/ppermute | solution.py:360
  73.4 3.7 %late.1 = f32[128,128]{1,0:T(8,128)} custom-call(bf16[352,768]{1,0:T(8,128)(2,1)S(1)} %pack_high.1.b0h, bf16[272,768]{1,0:T(8,128)(2,1)S(1)} %collective-permute-done.2.b1l, bf16[352,768]{1,0:T(8,128)(2,1)S(1)} %collective-permute-done.4.b1h, bf16[272,768]{1,0:T(8,128)(2,1)S(1)} %collective-permute-done.3.b2l, ...), custom_call_target="tpu_custom_call" | custom-call | flops 3000000000 | bytes 8000000 | tf_op jit(solution)/shard_map/late/pallas_call | solution.py:412
  77.1 7.4 %all-to-all-start.5 = ((f32[128,1,128]{2,1,0:T(1,128)}), f32[128,1,128]{2,1,0:T(1,128)S(1)}, u32[]{:S(2)}, u32[]{:S(2)}) async-start(f32[128,1,128]{2,1,0:T(1,128)} %bitcast.24), calls=%async_computation.5 | async-start | bytes 131072 | tf_op jit(solution)/shard_map/all_to_all | solution.py:419
  84.9 0.6 reduce_max.25
  86.2 7.9 %all-to-all-done.5 = f32[128,1,128]{2,1,0:T(1,128)S(1)} async-done(((f32[128,1,128]{2,1,0:T(1,128)}), f32[128,1,128]{2,1,0:T(1,128)S(1)}, u32[]{:S(2)}, u32[]{:S(2)}) %all-to-all-start.5) | async-done | bytes 65568 | tf_op jit(solution)/shard_map/all_to_all | solution.py:419
  94.1 1.1 %finish.1 = (f32[1,512]{1,0:T(1,128)}, f32[1,512]{1,0:T(1,128)}) custom-call(f32[128,128]{1,0:T(8,128)S(1)} %bitcast.63, s32[8,512]{1,0:T(8,128)S(1)} %get-tuple-element.293.places), custom_call_target="tpu_custom_call" | custom-call | flops 33554432 | bytes 8000000 | tf_op jit(solution)/shard_map/finish/pallas_call | solution.py:420
  (15 shorter events, 0.8 us)
Async XLA Ops:
  42.5 8.2 %collective-permute-start.3 = (bf16[272,768]{1,0:T(8,128)(2,1)S(1)}, bf16[272,768]{1,0:T(8,128)(2,1)S(1)}, u32[]{:S(2)}, u32[]{:S(2)}) collective-permute-start(bf16[272,768]{1,0:T(8,128)(2,1)S(1)} %get-tuple-element.287.low.b0l), channel_id=1, source_target_pairs={{1,0},{2,1},{3,2},{0,3},{5,4},{6,5},{7,6},{4,7},{9,8},{10,9},{11,1... | collective-permute-start | bytes 1253384 | tf_op jit(solution)/shard_map/ppermute | solution.py:360
  43.6 8.1 %collective-permute-start.2 = (bf16[272,768]{1,0:T(8,128)(2,1)S(1)}, bf16[272,768]{1,0:T(8,128)(2,1)S(1)}, u32[]{:S(2)}, u32[]{:S(2)}) collective-permute-start(bf16[272,768]{1,0:T(8,128)(2,1)S(1)} %get-tuple-element.287.low.b0l), channel_id=1, source_target_pairs={{4,0},{5,1},{6,2},{7,3},{8,4},{9,5},{10,6},{11,7},{12,8},{13,9},{1... | collective-permute-start | bytes 1253384 | tf_op jit(solution)/shard_map/ppermute | solution.py:360
  45.0 11.5 %collective-permute-start.5 = (bf16[352,768]{1,0:T(8,128)(2,1)S(1)}, bf16[352,768]{1,0:T(8,128)(2,1)S(1)}, u32[]{:S(2)}, u32[]{:S(2)}) collective-permute-start(bf16[352,768]{1,0:T(8,128)(2,1)S(1)} %pack_high.1.b0h), channel_id=1, source_target_pairs={{1,0},{2,1},{3,2},{0,3},{5,4},{6,5},{7,6},{4,7},{9,8},{10,9},{11,1... | collective-permute-start | bytes 1622024 | tf_op jit(solution)/shard_map/ppermute | solution.py:360
  45.7 11.7 %collective-permute-start.4 = (bf16[352,768]{1,0:T(8,128)(2,1)S(1)}, bf16[352,768]{1,0:T(8,128)(2,1)S(1)}, u32[]{:S(2)}, u32[]{:S(2)}) collective-permute-start(bf16[352,768]{1,0:T(8,128)(2,1)S(1)} %pack_high.1.b0h), channel_id=1, source_target_pairs={{4,0},{5,1},{6,2},{7,3},{8,4},{9,5},{10,6},{11,7},{12,8},{13,9},{1... | collective-permute-start | bytes 1622024 | tf_op jit(solution)/shard_map/ppermute | solution.py:360
  51.7 10.6 %collective-permute-start.6 = (bf16[272,768]{1,0:T(8,128)(2,1)S(1)}, bf16[272,768]{1,0:T(8,128)(2,1)S(1)}, u32[]{:S(2)}, u32[]{:S(2)}) collective-permute-start(bf16[272,768]{1,0:T(8,128)(2,1)S(1)} %collective-permute-done.2.b1l), channel_id=1, source_target_pairs={{4,0},{5,1},{6,2},{7,3},{8,4},{9,5},{10,6},{11,7},{12,8},{13,9},{1... | collective-permute-start | bytes 1253384 | tf_op jit(solution)/shard_map/ppermute | solution.py:360
  51.7 15.1 %collective-permute-start.8 = (bf16[272,768]{1,0:T(8,128)(2,1)S(1)}, bf16[272,768]{1,0:T(8,128)(2,1)S(1)}, u32[]{:S(2)}, u32[]{:S(2)}) collective-permute-start(bf16[272,768]{1,0:T(8,128)(2,1)S(1)} %collective-permute-done.3.b2l), channel_id=1, source_target_pairs={{1,0},{2,1},{3,2},{0,3},{5,4},{6,5},{7,6},{4,7},{9,8},{10,9},{11,1... | collective-permute-start | bytes 1253384 | tf_op jit(solution)/shard_map/ppermute | solution.py:360
  52.3 14.4 %collective-permute-start.11 = (bf16[352,768]{1,0:T(8,128)(2,1)S(1)}, bf16[352,768]{1,0:T(8,128)(2,1)S(1)}, u32[]{:S(2)}, u32[]{:S(2)}) collective-permute-start(bf16[352,768]{1,0:T(8,128)(2,1)S(1)} %pack_high.1.b0h), channel_id=1, source_target_pairs={{12,0},{13,1},{14,2},{15,3},{0,4},{1,5},{2,6},{3,7},{4,8},{5,9},{6... | collective-permute-start | bytes 1622024 | tf_op jit(solution)/shard_map/ppermute | solution.py:360
  57.5 11.7 %collective-permute-start.10 = (bf16[272,768]{1,0:T(8,128)(2,1)S(1)}, bf16[272,768]{1,0:T(8,128)(2,1)S(1)}, u32[]{:S(2)}, u32[]{:S(2)}) collective-permute-start(bf16[272,768]{1,0:T(8,128)(2,1)S(1)} %get-tuple-element.287.low.b0l), channel_id=1, source_target_pairs={{3,0},{0,1},{1,2},{2,3},{7,4},{4,5},{5,6},{6,7},{11,8},{8,9},{9,10... | collective-permute-start | bytes 1253384 | tf_op jit(solution)/shard_map/ppermute | solution.py:360
  59.4 14.0 %collective-permute-start.7 = (bf16[352,768]{1,0:T(8,128)(2,1)S(1)}, bf16[352,768]{1,0:T(8,128)(2,1)S(1)}, u32[]{:S(2)}, u32[]{:S(2)}) collective-permute-start(bf16[352,768]{1,0:T(8,128)(2,1)S(1)} %collective-permute-done.4.b1h), channel_id=1, source_target_pairs={{4,0},{5,1},{6,2},{7,3},{8,4},{9,5},{10,6},{11,7},{12,8},{13,9},{1... | collective-permute-start | bytes 1622024 | tf_op jit(solution)/shard_map/ppermute | solution.py:360
  62.2 11.2 %collective-permute-start.9 = (bf16[352,768]{1,0:T(8,128)(2,1)S(1)}, bf16[352,768]{1,0:T(8,128)(2,1)S(1)}, u32[]{:S(2)}, u32[]{:S(2)}) collective-permute-start(bf16[352,768]{1,0:T(8,128)(2,1)S(1)} %collective-permute-done.5.b2h), channel_id=1, source_target_pairs={{1,0},{2,1},{3,2},{0,3},{5,4},{6,5},{7,6},{4,7},{9,8},{10,9},{11,1... | collective-permute-start | bytes 1622024 | tf_op jit(solution)/shard_map/ppermute | solution.py:360
  77.1 16.9 %copy-start = (s32[512]{0:T(512)S(1)}, s32[512]{0:T(512)}, u32[]{:S(2)}) copy-start(s32[512]{0:T(512)} %param.9) | copy-start | bytes 6148
  77.1 16.9 %copy-start.1 = (bf16[512,768]{1,0:T(8,128)(2,1)S(1)}, bf16[512,768]{1,0:T(8,128)(2,1)}, u32[]{:S(2)}) copy-start(bf16[512,768]{1,0:T(8,128)(2,1)} %rows.1) | copy-start | bytes 2359300
  77.1 16.9 %copy-start.2 = (s32[512]{0:T(512)S(1)}, s32[512]{0:T(512)}, u32[]{:S(2)}) copy-start(s32[512]{0:T(512)} %param.8) | copy-start | bytes 6148
  77.1 16.9 %all-to-all-start.5 = ((f32[128,1,128]{2,1,0:T(1,128)}), f32[128,1,128]{2,1,0:T(1,128)S(1)}, u32[]{:S(2)}, u32[]{:S(2)}) async-start(f32[128,1,128]{2,1,0:T(1,128)} %bitcast.24), calls=%async_computation.5 | async-start | bytes 131072 | tf_op jit(solution)/shard_map/all_to_all | solution.py:419

commit v11 on v10

--- a/solution.py
+++ b/solution.py
@@ -150,6 +150,7 @@
 LOWS = ((0, 256),)
 HIGHS = ((256, 256), (512, SENT - 512))
 PARTS = LOWS + HIGHS
+TALL = ((0, 256), (256, SENT - 256))
 
 
 def clear(state):
@@ -182,6 +183,8 @@
 def square(rows, cols, place, c, r, state, own=False, downs=PARTS, parts=PARTS):
     col_best, col_mass, row_best, row_mass, spelt = state
     clusters = names_of(cols)[0:1]
+    if downs is PARTS and not own:
+        downs = TALL
     for i, tall in downs:
         for j, wide in parts:
             product = matmul(part_of(rows, i, tall), part_of(cols, j, wide), NT)

time: 95.3 us -> 95.1 us (level)
  transfers between devices with their start and end apart: 11 -> 11, of which waited for: 8 -> 9; matrix products, arithmetic and copies ran while one was open for 1% -> 1% of each run, Pallas kernels for 9% -> 8%
where the time goes in v11:
time: 95.1 us; the launch traced here: 94.9 us
  blocking collectives  38.1 us (40%)
  waiting for transfers between devices  23.3 us (25%)
  Pallas kernels  16.2 us (17%)
  starting transfers between devices  15.4 us (16%)
  between operations  1.35 us (1%)
    all_to_all x1, blocking collectives, fast(): lax.all_to_all(spread, AXES, split_axis=0, concat_axis=0, tiled=True)  38.1 us
    ppermute x10, waiting for transfers between devices, from_spot(): return lax.ppermute(x, AXES, hop(dy, dz))  15.4 us
    ppermute x10, starting transfers between devices, from_spot(): return lax.ppermute(x, AXES, hop(dy, dz))  8.03 us
    all_to_all x1, waiting for transfers between devices, fast(): lax.all_to_all(message, AXES, split_axis=0, concat_axis=0, tiled=True)  7.9 us
    all_to_all x1, starting transfers between devices, fast(): lax.all_to_all(message, AXES, split_axis=0, concat_axis=0, tiled=True)  7.35 us
    pallas_call x1, Pallas kernels, fast(): call(early_kernel, stats, scratch=state(3), flops=6000000000, name='early')  3.76 us
    pallas_call x1, Pallas kernels, fast(): call(late_kernel, shape((DEVICES, 128), f32), scratch=state(4), flops=300...  3.49 us
    pallas_call x1, Pallas kernels, fast(): call(middle_kernel, stats, scratch=state(4), flops=1500000000, name='midd...  2.84 us
  transfers between devices with their start and end apart: 11, of which 9 were waited for; matrix products, arithmetic and copies ran while one was open for 1% of the time, Pallas kernels for 8%

profile of v11, /device:TPU:1, one launch (start us, length us, event | category | flops | bytes accessed | tf_op | source)
XLA Modules:
  0.0 94.9 jit_solution(14698287143098964195)
XLA Ops:
  0.6 2.8 %prelude.1 = (bf16[1024,896]{1,0:T(8,128)(2,1)S(1)}, s32[8,512]{1,0:T(8,128)S(1)}) custom-call(s32[1,512]{1,0:T(1,128)} %bitcast.75, s32[1,512]{1,0:T(1,128)} %bitcast.64, bf16[512,768]{1,0:T(8,128)(2,1)} %rows.1), custom_call_target="tpu_custom_call" | custom-call | flops 3000000000 | bytes 8000000 | tf_op jit(solution)/shard_map/prelude/pallas_call | solution.py:369
  3.4 38.1 %all_to_all.59 = bf16[128,8,896]{2,1,0:T(8,128)(2,1)S(1)} all-to-all(bf16[128,8,896]{2,1,0:T(8,128)(2,1)S(1)} %bitcast.62), channel_id=1, replica_groups=mesh['grp'=8,'blk'=16] {'grp','blk'}, dimensions={0} | all-to-all | bytes 3670016 | tf_op jit(solution)/shard_map/all_to_all | solution.py:375
  41.5 1.0 %pack_low.1 = (bf16[272,768]{1,0:T(8,128)(2,1)S(1)}, s32[8,1024]{1,0:T(8,128)S(1)}, f32[8,1024]{1,0:T(8,128)S(1)}) custom-call(bf16[1024,896]{1,0:T(8,128)(2,1)S(1)} %bitcast.59), custom_call_target="tpu_custom_call" | custom-call | flops 2000000000 | bytes 8000000 | tf_op jit(solution)/shard_map/pack_low/pallas_call | solution.py:376
  42.5 1.1 %collective-permute-start.3 = (bf16[272,768]{1,0:T(8,128)(2,1)S(1)}, bf16[272,768]{1,0:T(8,128)(2,1)S(1)}, u32[]{:S(2)}, u32[]{:S(2)}) collective-permute-start(bf16[272,768]{1,0:T(8,128)(2,1)S(1)} %get-tuple-element.287.low.b0l), channel_id=1, source_target_pairs={{1,0},{2,1},{3,2},{0,3},{5,4},{6,5},{7,6},{4,7},{9,8},{10,9},{11,1... | collective-permute-start | bytes 1253384 | tf_op jit(solution)/shard_map/ppermute | solution.py:363
  43.6 0.6 collective-permute-start.2
  44.1 0.9 pack_high.1.b0h
  45.0 0.7 collective-permute-start.5
  45.7 4.9 %collective-permute-done.3.b2l = bf16[272,768]{1,0:T(8,128)(2,1)S(1)} collective-permute-done((bf16[272,768]{1,0:T(8,128)(2,1)S(1)}, bf16[272,768]{1,0:T(8,128)(2,1)S(1)}, u32[]{:S(2)}, u32[]{:S(2)}) %collective-permute-start.3) | collective-permute-done | bytes 417824 | tf_op jit(solution)/shard_map/ppermute | solution.py:363
  50.7 1.0 %collective-permute-done.2.b1l = bf16[272,768]{1,0:T(8,128)(2,1)S(1)} collective-permute-done((bf16[272,768]{1,0:T(8,128)(2,1)S(1)}, bf16[272,768]{1,0:T(8,128)(2,1)S(1)}, u32[]{:S(2)}, u32[]{:S(2)}) %collective-permute-start.2) | collective-permute-done | bytes 417824 | tf_op jit(solution)/shard_map/ppermute | solution.py:363
  51.7 0.7 collective-permute-start.8
  52.3 2.7 %collective-permute-start.11 = (bf16[352,768]{1,0:T(8,128)(2,1)S(1)}, bf16[352,768]{1,0:T(8,128)(2,1)S(1)}, u32[]{:S(2)}, u32[]{:S(2)}) collective-permute-start(bf16[352,768]{1,0:T(8,128)(2,1)S(1)} %pack_high.1.b0h), channel_id=1, source_target_pairs={{12,0},{13,1},{14,2},{15,3},{0,4},{1,5},{2,6},{3,7},{4,8},{5,9},{6... | collective-permute-start | bytes 1622024 | tf_op jit(solution)/shard_map/ppermute | solution.py:363
  55.0 1.5 %collective-permute-done.5.b2h = bf16[352,768]{1,0:T(8,128)(2,1)S(1)} collective-permute-done((bf16[352,768]{1,0:T(8,128)(2,1)S(1)}, bf16[352,768]{1,0:T(8,128)(2,1)S(1)}, u32[]{:S(2)}, u32[]{:S(2)}) %collective-permute-start.5) | collective-permute-done | bytes 540704 | tf_op jit(solution)/shard_map/ppermute | solution.py:363
  56.5 1.0 %collective-permute-done.4.b1h = bf16[352,768]{1,0:T(8,128)(2,1)S(1)} collective-permute-done((bf16[352,768]{1,0:T(8,128)(2,1)S(1)}, bf16[352,768]{1,0:T(8,128)(2,1)S(1)}, u32[]{:S(2)}, u32[]{:S(2)}) %collective-permute-start.4) | collective-permute-done | bytes 540704 | tf_op jit(solution)/shard_map/ppermute | solution.py:363
  57.5 2.0 %collective-permute-start.10 = (bf16[272,768]{1,0:T(8,128)(2,1)S(1)}, bf16[272,768]{1,0:T(8,128)(2,1)S(1)}, u32[]{:S(2)}, u32[]{:S(2)}) collective-permute-start(bf16[272,768]{1,0:T(8,128)(2,1)S(1)} %get-tuple-element.287.low.b0l), channel_id=1, source_target_pairs={{3,0},{0,1},{1,2},{2,3},{7,4},{4,5},{5,6},{6,7},{11,8},{8,9},{9,10... | collective-permute-start | bytes 1253384 | tf_op jit(solution)/shard_map/ppermute | solution.py:363
  59.5 2.8 %collective-permute-done.6.b3l = bf16[272,768]{1,0:T(8,128)(2,1)S(1)} collective-permute-done((bf16[272,768]{1,0:T(8,128)(2,1)S(1)}, bf16[272,768]{1,0:T(8,128)(2,1)S(1)}, u32[]{:S(2)}, u32[]{:S(2)}) %collective-permute-start.6) | collective-permute-done | bytes 417824 | tf_op jit(solution)/shard_map/ppermute | solution.py:363
  62.6 3.8 %early.1 = (f32[8,640]{1,0:T(8,128)S(1)}, f32[8,640]{1,0:T(8,128)S(1)}) custom-call(bf16[272,768]{1,0:T(8,128)(2,1)S(1)} %get-tuple-element.287.low.b0l, bf16[352,768]{1,0:T(8,128)(2,1)S(1)} %pack_high.1.b0h, bf16[272,768]{1,0:T(8,128)(2,1)S(1)} %collective-permute-done.2.b1l, bf16[352,768]{1,0:T(8,128)(2,1)S(1)} %collective-permute-done.4.b1h, ...), custom_call_target="tpu_custom_call" | custom-call | flops 6000000000 | bytes 8000000 | tf_op jit(solution)/shard_map/early/pallas_call | solution.py:409
  66.7 2.5 %collective-permute-done.10.low = bf16[272,768]{1,0:T(8,128)(2,1)S(1)} collective-permute-done((bf16[272,768]{1,0:T(8,128)(2,1)S(1)}, bf16[272,768]{1,0:T(8,128)(2,1)S(1)}, u32[]{:S(2)}, u32[]{:S(2)}) %collective-permute-start.10) | collective-permute-done | bytes 417824 | tf_op jit(solution)/shard_map/ppermute | solution.py:363
  69.2 2.8 %middle.1 = (f32[8,640]{1,0:T(8,128)S(1)}, f32[8,640]{1,0:T(8,128)S(1)}) custom-call(bf16[272,768]{1,0:T(8,128)(2,1)S(1)} %get-tuple-element.287.low.b0l, bf16[272,768]{1,0:T(8,128)(2,1)S(1)} %collective-permute-done.2.b1l, bf16[352,768]{1,0:T(8,128)(2,1)S(1)} %collective-permute-done.4.b1h, bf16[272,768]{1,0:T(8,128)(2,1)S(1)} %collective-permute-done.3.b2l, ...), custom_call_target="tpu_custom_call" | custom-call | flops 1500000000 | bytes 8000000 | tf_op jit(solution)/shard_map/middle/pallas_call | solution.py:412
  72.0 1.4 %collective-permute-done.7.b3h = bf16[352,768]{1,0:T(8,128)(2,1)S(1)} collective-permute-done((bf16[352,768]{1,0:T(8,128)(2,1)S(1)}, bf16[352,768]{1,0:T(8,128)(2,1)S(1)}, u32[]{:S(2)}, u32[]{:S(2)}) %collective-permute-start.7) | collective-permute-done | bytes 540704 | tf_op jit(solution)/shard_map/ppermute | solution.py:363
  73.4 3.5 %late.1 = f32[128,128]{1,0:T(8,128)} custom-call(bf16[352,768]{1,0:T(8,128)(2,1)S(1)} %pack_high.1.b0h, bf16[272,768]{1,0:T(8,128)(2,1)S(1)} %collective-permute-done.2.b1l, bf16[352,768]{1,0:T(8,128)(2,1)S(1)} %collective-permute-done.4.b1h, bf16[272,768]{1,0:T(8,128)(2,1)S(1)} %collective-permute-done.3.b2l, ...), custom_call_target="tpu_custom_call" | custom-call | flops 3000000000 | bytes 8000000 | tf_op jit(solution)/shard_map/late/pallas_call | solution.py:415
  76.9 7.4 %all-to-all-start.5 = ((f32[128,1,128]{2,1,0:T(1,128)}), f32[128,1,128]{2,1,0:T(1,128)S(1)}, u32[]{:S(2)}, u32[]{:S(2)}) async-start(f32[128,1,128]{2,1,0:T(1,128)} %bitcast.24), calls=%async_computation.5 | async-start | bytes 131072 | tf_op jit(solution)/shard_map/all_to_all | solution.py:422
  84.7 0.6 reduce_max.25
  86.0 7.9 %all-to-all-done.5 = f32[128,1,128]{2,1,0:T(1,128)S(1)} async-done(((f32[128,1,128]{2,1,0:T(1,128)}), f32[128,1,128]{2,1,0:T(1,128)S(1)}, u32[]{:S(2)}, u32[]{:S(2)}) %all-to-all-start.5) | async-done | bytes 65568 | tf_op jit(solution)/shard_map/all_to_all | solution.py:422
  93.9 1.1 %finish.1 = (f32[1,512]{1,0:T(1,128)}, f32[1,512]{1,0:T(1,128)}) custom-call(f32[128,128]{1,0:T(8,128)S(1)} %bitcast.63, s32[8,512]{1,0:T(8,128)S(1)} %get-tuple-element.293.places), custom_call_target="tpu_custom_call" | custom-call | flops 33554432 | bytes 8000000 | tf_op jit(solution)/shard_map/finish/pallas_call | solution.py:423
  (15 shorter events, 1.1 us)
Async XLA Ops:
  42.5 8.2 %collective-permute-start.3 = (bf16[272,768]{1,0:T(8,128)(2,1)S(1)}, bf16[272,768]{1,0:T(8,128)(2,1)S(1)}, u32[]{:S(2)}, u32[]{:S(2)}) collective-permute-start(bf16[272,768]{1,0:T(8,128)(2,1)S(1)} %get-tuple-element.287.low.b0l), channel_id=1, source_target_pairs={{1,0},{2,1},{3,2},{0,3},{5,4},{6,5},{7,6},{4,7},{9,8},{10,9},{11,1... | collective-permute-start | bytes 1253384 | tf_op jit(solution)/shard_map/ppermute | solution.py:363
  43.6 8.1 %collective-permute-start.2 = (bf16[272,768]{1,0:T(8,128)(2,1)S(1)}, bf16[272,768]{1,0:T(8,128)(2,1)S(1)}, u32[]{:S(2)}, u32[]{:S(2)}) collective-permute-start(bf16[272,768]{1,0:T(8,128)(2,1)S(1)} %get-tuple-element.287.low.b0l), channel_id=1, source_target_pairs={{4,0},{5,1},{6,2},{7,3},{8,4},{9,5},{10,6},{11,7},{12,8},{13,9},{1... | collective-permute-start | bytes 1253384 | tf_op jit(solution)/shard_map/ppermute | solution.py:363
  45.0 11.5 %collective-permute-start.5 = (bf16[352,768]{1,0:T(8,128)(2,1)S(1)}, bf16[352,768]{1,0:T(8,128)(2,1)S(1)}, u32[]{:S(2)}, u32[]{:S(2)}) collective-permute-start(bf16[352,768]{1,0:T(8,128)(2,1)S(1)} %pack_high.1.b0h), channel_id=1, source_target_pairs={{1,0},{2,1},{3,2},{0,3},{5,4},{6,5},{7,6},{4,7},{9,8},{10,9},{11,1... | collective-permute-start | bytes 1622024 | tf_op jit(solution)/shard_map/ppermute | solution.py:363
  45.7 11.7 %collective-permute-start.4 = (bf16[352,768]{1,0:T(8,128)(2,1)S(1)}, bf16[352,768]{1,0:T(8,128)(2,1)S(1)}, u32[]{:S(2)}, u32[]{:S(2)}) collective-permute-start(bf16[352,768]{1,0:T(8,128)(2,1)S(1)} %pack_high.1.b0h), channel_id=1, source_target_pairs={{4,0},{5,1},{6,2},{7,3},{8,4},{9,5},{10,6},{11,7},{12,8},{13,9},{1... | collective-permute-start | bytes 1622024 | tf_op jit(solution)/shard_map/ppermute | solution.py:363
  51.7 10.6 %collective-permute-start.6 = (bf16[272,768]{1,0:T(8,128)(2,1)S(1)}, bf16[272,768]{1,0:T(8,128)(2,1)S(1)}, u32[]{:S(2)}, u32[]{:S(2)}) collective-permute-start(bf16[272,768]{1,0:T(8,128)(2,1)S(1)} %collective-permute-done.2.b1l), channel_id=1, source_target_pairs={{4,0},{5,1},{6,2},{7,3},{8,4},{9,5},{10,6},{11,7},{12,8},{13,9},{1... | collective-permute-start | bytes 1253384 | tf_op jit(solution)/shard_map/ppermute | solution.py:363
  51.7 14.7 %collective-permute-start.8 = (bf16[272,768]{1,0:T(8,128)(2,1)S(1)}, bf16[272,768]{1,0:T(8,128)(2,1)S(1)}, u32[]{:S(2)}, u32[]{:S(2)}) collective-permute-start(bf16[272,768]{1,0:T(8,128)(2,1)S(1)} %collective-permute-done.3.b2l), channel_id=1, source_target_pairs={{1,0},{2,1},{3,2},{0,3},{5,4},{6,5},{7,6},{4,7},{9,8},{10,9},{11,1... | collective-permute-start | bytes 1253384 | tf_op jit(solution)/shard_map/ppermute | solution.py:363
  52.3 14.4 %collective-permute-start.11 = (bf16[352,768]{1,0:T(8,128)(2,1)S(1)}, bf16[352,768]{1,0:T(8,128)(2,1)S(1)}, u32[]{:S(2)}, u32[]{:S(2)}) collective-permute-start(bf16[352,768]{1,0:T(8,128)(2,1)S(1)} %pack_high.1.b0h), channel_id=1, source_target_pairs={{12,0},{13,1},{14,2},{15,3},{0,4},{1,5},{2,6},{3,7},{4,8},{5,9},{6... | collective-permute-start | bytes 1622024 | tf_op jit(solution)/shard_map/ppermute | solution.py:363
  57.5 11.7 %collective-permute-start.10 = (bf16[272,768]{1,0:T(8,128)(2,1)S(1)}, bf16[272,768]{1,0:T(8,128)(2,1)S(1)}, u32[]{:S(2)}, u32[]{:S(2)}) collective-permute-start(bf16[272,768]{1,0:T(8,128)(2,1)S(1)} %get-tuple-element.287.low.b0l), channel_id=1, source_target_pairs={{3,0},{0,1},{1,2},{2,3},{7,4},{4,5},{5,6},{6,7},{11,8},{8,9},{9,10... | collective-permute-start | bytes 1253384 | tf_op jit(solution)/shard_map/ppermute | solution.py:363
  59.4 14.0 %collective-permute-start.7 = (bf16[352,768]{1,0:T(8,128)(2,1)S(1)}, bf16[352,768]{1,0:T(8,128)(2,1)S(1)}, u32[]{:S(2)}, u32[]{:S(2)}) collective-permute-start(bf16[352,768]{1,0:T(8,128)(2,1)S(1)} %collective-permute-done.4.b1h), channel_id=1, source_target_pairs={{4,0},{5,1},{6,2},{7,3},{8,4},{9,5},{10,6},{11,7},{12,8},{13,9},{1... | collective-permute-start | bytes 1622024 | tf_op jit(solution)/shard_map/ppermute | solution.py:363
  62.2 11.2 %collective-permute-start.9 = (bf16[352,768]{1,0:T(8,128)(2,1)S(1)}, bf16[352,768]{1,0:T(8,128)(2,1)S(1)}, u32[]{:S(2)}, u32[]{:S(2)}) collective-permute-start(bf16[352,768]{1,0:T(8,128)(2,1)S(1)} %collective-permute-done.5.b2h), channel_id=1, source_target_pairs={{1,0},{2,1},{3,2},{0,3},{5,4},{6,5},{7,6},{4,7},{9,8},{10,9},{11,1... | collective-permute-start | bytes 1622024 | tf_op jit(solution)/shard_map/ppermute | solution.py:363
  76.9 16.9 %copy-start = (s32[512]{0:T(512)S(1)}, s32[512]{0:T(512)}, u32[]{:S(2)}) copy-start(s32[512]{0:T(512)} %param.9) | copy-start | bytes 6148
  76.9 16.9 %copy-start.1 = (bf16[512,768]{1,0:T(8,128)(2,1)S(1)}, bf16[512,768]{1,0:T(8,128)(2,1)}, u32[]{:S(2)}) copy-start(bf16[512,768]{1,0:T(8,128)(2,1)} %rows.1) | copy-start | bytes 2359300
  76.9 16.9 %copy-start.2 = (s32[512]{0:T(512)S(1)}, s32[512]{0:T(512)}, u32[]{:S(2)}) copy-start(s32[512]{0:T(512)} %param.8) | copy-start | bytes 6148
  76.9 16.9 %all-to-all-start.5 = ((f32[128,1,128]{2,1,0:T(1,128)}), f32[128,1,128]{2,1,0:T(1,128)S(1)}, u32[]{:S(2)}, u32[]{:S(2)}) async-start(f32[128,1,128]{2,1,0:T(1,128)} %bitcast.24), calls=%async_computation.5 | async-start | bytes 131072 | tf_op jit(solution)/shard_map/all_to_all | solution.py:422
